TPU v7x, 32 devices: a whole 2x2x4 slice. The times are simulated.
32 devices in a mesh: ctx: 16 (over z, y, x), wa: 2 (over core).
Axes of the slice: x: 2, y: 2, z: 4, core: 2. Of those that a mesh axis runs over, the one named last changes fastest.
Arguments:
- tokens: bfloat16 [16384, 640], P('ctx'), may hold values from -6 to 6
- cotangent: bfloat16 [16384, 640], P('ctx'), may hold values from -6 to 6
- seq_ids: int32 [16384], P('ctx'), may hold values from 0 to 7, as said below
- w_query: bfloat16 [640, 1024], P(None, 'wa'), may hold values from -0.5 to 0.5
- w_keyval: bfloat16 [2, 640, 256], replicated, may hold values from -0.25 to 0.25
- w_out: bfloat16 [1024, 640], P('wa'), may hold values from -0.1875 to 0.1875
- w_gateup: bfloat16 [2, 640, 2048], P(None, None, 'wa'), may hold values from -0.25 to 0.25
- w_down: bfloat16 [2048, 640], P('wa'), may hold values from -0.125 to 0.125
- norm_gains: float32 [4, 640], replicated, may hold values from -0.5 to 0.5
- mom_query: float32 [640, 1024], P('ctx', 'wa'), may hold values from -600 to 600
- mom_keyval: float32 [2, 640, 256], P(None, 'ctx', 'wa'), may hold values from -600 to 600
- mom_out: float32 [1024, 640], P('wa', 'ctx'), may hold values from -600 to 600
- mom_gateup: float32 [2, 640, 2048], P(None, 'ctx', 'wa'), may hold values from -600 to 600
- mom_down: float32 [2048, 640], P('wa', 'ctx'), may hold values from -600 to 600
- gain_first: float32 [4, 640], P(None, 'ctx'), may hold values from -180 to 180
- gain_second: float32 [4, 640], P(None, 'ctx'), may hold values from 1000 to 10000
Outputs:
- block_out: bfloat16 [16384, 640], P('ctx')
- input_grad: float32 [16384, 640], P('ctx')
- grad_query: float32 [640, 1024], P('ctx', 'wa')
- grad_keyval: float32 [2, 640, 256], P(None, 'ctx', 'wa')
- grad_out: float32 [1024, 640], P('wa', 'ctx')
- grad_gateup: float32 [2, 640, 2048], P(None, 'ctx', 'wa')
- grad_down: float32 [2048, 640], P('wa', 'ctx')
- grad_gains: float32 [4, 640], P(None, 'ctx')
- new_mom_query: float32 [640, 1024], P('ctx', 'wa')
- new_mom_keyval: float32 [2, 640, 256], P(None, 'ctx', 'wa')
- new_mom_out: float32 [1024, 640], P('wa', 'ctx')
- new_mom_gateup: float32 [2, 640, 2048], P(None, 'ctx', 'wa')
- new_mom_down: float32 [2048, 640], P('wa', 'ctx')
- upd_query: float32 [640, 1024], P('ctx', 'wa')
- upd_keyval: float32 [2, 640, 256], P(None, 'ctx', 'wa')
- upd_out: float32 [1024, 640], P('wa', 'ctx')
- upd_gateup: float32 [2, 640, 2048], P(None, 'ctx', 'wa')
- upd_down: float32 [2048, 640], P('wa', 'ctx')
- new_gain_first: float32 [4, 640], P(None, 'ctx')
- new_gain_second: float32 [4, 640], P(None, 'ctx')
- gain_update: float32 [4, 640], P(None, 'ctx')
Inputs may be any that keep to these rules, and one draw needn't show every extreme that they name: `seq_ids`: never falling along the tokens; each value marks one sequence of 1024 to 4096 tokens; the first sequence has 4096 tokens.
All inputs are finite; a program needn't handle non-finite values.
Results may differ from a plain program's by a relative error of at most 0.024.
Values may be sent and summed in bfloat16 or wider, within the bound.
A program may use at most 384 MiB of HBM per device.

v0:
```python
from functools import partial
import math

import jax
import jax.numpy as jnp
from jax import lax
from jax.sharding import PartitionSpec as P

D = 640
FF = 2048
HD = 256
WINDOW = 512
SOFT_CAP = 10
NS_STEPS = 5
HQ = 1024


EPS_NORM = 1e-06
ROPE_BASE = 10000.0
MOMENTUM = 0.95
MUON_RATE = 0.2
ADAM_ONE = 0.9
ADAM_TWO = 0.95
ADAM_EPS = 1e-08
GAIN_RATE = 0.1
QUINTIC_A = 3.4445
QUINTIC_B = -4.775
QUINTIC_C = 2.0315
MASK_FILL = -1e30
HIGHEST_PREC = lax.Precision.HIGHEST
MATRIX_COUNT = 7


def shifted(block, axis, distance):
    devices = range(lax.axis_size(axis))
    route = [(i - distance, i) for i in devices if i - distance in devices]
    return lax.ppermute(block, axis, route)


def rms_scale(activation, gain_row):
    return (
        activation
        * lax.rsqrt(jnp.mean(activation * activation, axis=-1, keepdims=True) + EPS_NORM)
        * (1.0 + gain_row)
    )


def geglu(gate_pre, up_proj):
    return jax.nn.gelu(gate_pre, approximate=True) * up_proj


def inverse_freq():
    return jnp.power(ROPE_BASE, -2.0 * jnp.arange(HD // 2, dtype=jnp.float32) / HD)


def angle_tables(vectors, angles):
    cosine_tab = jnp.cos(angles)
    sine_tab = jnp.sin(angles)
    if vectors.ndim == 3:
        cosine_tab = cosine_tab[:, None, :]
        sine_tab = sine_tab[:, None, :]
    return (cosine_tab, sine_tab)


def rotate(vectors, angles):
    half_dim = vectors.shape[-1] // 2
    cosine_tab, sine_tab = angle_tables(vectors, angles)
    left_part = vectors[..., :half_dim]
    right_part = vectors[..., half_dim:]
    return jnp.concatenate(
        [
            left_part * cosine_tab - right_part * sine_tab,
            right_part * cosine_tab + left_part * sine_tab,
        ],
        axis=-1,
    )


def rotate_back(grads_rot, angles):
    half_dim = grads_rot.shape[-1] // 2
    cosine_tab, sine_tab = angle_tables(grads_rot, angles)
    left_part = grads_rot[..., :half_dim]
    right_part = grads_rot[..., half_dim:]
    return jnp.concatenate(
        [
            left_part * cosine_tab + right_part * sine_tab,
            right_part * cosine_tab - left_part * sine_tab,
        ],
        axis=-1,
    )


def local_positions(seq_ids, ctx_index):
    tok_count = seq_ids.shape[0]
    begin_at = ctx_index * tok_count
    return begin_at + jnp.arange(tok_count, dtype=jnp.int32)


def block_scores(query_blk, key_blk, query_pos, query_ids, key_pos, key_ids):
    raw_scores = jnp.einsum("bhd,sd->hbs", query_blk, key_blk, preferred_element_type=jnp.float32)
    tanh_cap = jnp.tanh(raw_scores / SOFT_CAP)
    pos_gap = query_pos[:, None] - key_pos[None, :]
    allowed = (query_ids[:, None] == key_ids[None, :]) & (pos_gap >= 0) & (pos_gap < WINDOW)
    masked = jnp.where(allowed[None], SOFT_CAP * tanh_cap, MASK_FILL)
    return (masked, tanh_cap)


def orthogonalize(matrix):
    flipped = matrix.shape[0] > matrix.shape[1]
    iterate = matrix.T if flipped else matrix
    iterate = iterate / (jnp.sqrt(jnp.sum(iterate * iterate)) + 1e-07)
    for sweep in range(NS_STEPS):
        gram_mat = jnp.dot(iterate, iterate.T, precision=HIGHEST_PREC)
        poly_mat = QUINTIC_B * gram_mat + QUINTIC_C * jnp.dot(
            gram_mat, gram_mat, precision=HIGHEST_PREC
        )
        iterate = QUINTIC_A * iterate + jnp.dot(poly_mat, iterate, precision=HIGHEST_PREC)
    return iterate.T if flipped else iterate


def muon_update(matrix):
    return (
        -MUON_RATE * 0.2 * math.sqrt(max(matrix.shape[0], matrix.shape[1])) * orthogonalize(matrix)
    )


def take_block(array_in, along_dim, block_index, block_size):
    return lax.dynamic_slice_in_dim(array_in, block_index * block_size, block_size, along_dim)


def split_blocks(matrix, ctx_dim, ctx_count, wa_count):
    row_count, col_count = matrix.shape
    if ctx_dim == 0:
        tile_grid = matrix.reshape(
            ctx_count, row_count // ctx_count, wa_count, col_count // wa_count
        ).transpose(0, 2, 1, 3)
    else:
        tile_grid = matrix.reshape(
            wa_count, row_count // wa_count, ctx_count, col_count // ctx_count
        ).transpose(2, 0, 1, 3)
    return tile_grid.reshape(ctx_count * wa_count, -1)


def join_blocks(tile_rows, ctx_dim, row_count, col_count, ctx_count, wa_count):
    if ctx_dim == 0:
        tile_grid = tile_rows.reshape(
            ctx_count, wa_count, row_count // ctx_count, col_count // wa_count
        ).transpose(0, 2, 1, 3)
    else:
        tile_grid = tile_rows.reshape(
            ctx_count, wa_count, row_count // wa_count, col_count // ctx_count
        ).transpose(1, 2, 0, 3)
    return tile_grid.reshape(row_count, col_count)


def owner_tiles(
    operand,
    mat_idx,
    ctx_dim,
    row_count,
    col_count,
    ctx_count,
    wa_count,
    offset,
    total_cols,
    from_slots,
):
    elem_count = row_count * col_count // (ctx_count * wa_count)
    tile_src = operand[:, :elem_count] if from_slots else operand[mat_idx]
    matrix = join_blocks(tile_src, ctx_dim, row_count, col_count, ctx_count, wa_count)
    tile_rows = split_blocks(muon_update(matrix), ctx_dim, ctx_count, wa_count)
    placed = jnp.zeros((ctx_count * wa_count, total_cols), jnp.float32)
    return placed.at[:, offset : offset + elem_count].set(tile_rows)


def empty_tiles(operand, dev_count, total_cols):
    return jnp.zeros((dev_count, total_cols), jnp.float32)


def per_device(
    tokens,
    cotangent,
    seq_ids,
    w_query,
    w_keyval,
    w_out,
    w_gateup,
    w_down,
    norm_gains,
    mom_query,
    mom_keyval,
    mom_out,
    mom_gateup,
    mom_down,
    gain_first,
    gain_second,
):
    ctx_index = lax.axis_index("ctx")
    wa_index = lax.axis_index("wa")
    ctx_count = lax.axis_size("ctx")
    wa_count = lax.axis_size("wa")
    tok_count = tokens.shape[0]
    head_local = w_query.shape[1] // HD
    block_rows = min(512, tok_count)
    key_span = block_rows + WINDOW
    block_total = tok_count // block_rows
    positions = local_positions(seq_ids, ctx_index)
    angles = positions.astype(jnp.float32)[:, None] * inverse_freq()[None, :]
    resid_in = tokens.astype(jnp.float32)
    normed = rms_scale(resid_in, norm_gains[0]).astype(jnp.bfloat16)
    query_proj = jnp.dot(normed, w_query, preferred_element_type=jnp.float32)
    key_proj = jnp.dot(normed, w_keyval[0], preferred_element_type=jnp.float32)
    value_proj = jnp.dot(normed, w_keyval[1], preferred_element_type=jnp.float32)
    query_rot = (
        rotate(query_proj.reshape(tok_count, head_local, HD), angles) * HD ** (-0.5)
    ).astype(jnp.bfloat16)
    key_rot = rotate(key_proj, angles).astype(jnp.bfloat16)
    value_low = value_proj.astype(jnp.bfloat16)
    prev_key, prev_value, prev_pos, prev_ids = shifted(
        (key_rot, value_low, positions, seq_ids), "ctx", 1
    )
    prev_ids = jnp.where(ctx_index > 0, prev_ids, -1)
    keys_all = jnp.concatenate([prev_key, key_rot])
    values_all = jnp.concatenate([prev_value, value_low])
    pos_all = jnp.concatenate([prev_pos, positions])
    ids_all = jnp.concatenate([prev_ids, seq_ids])
    attended_parts = []
    lse_parts = []
    for block_idx in range(block_total):
        q_start = block_idx * block_rows
        k_start = tok_count + q_start - WINDOW
        masked, tanh_cap = block_scores(
            query_rot[q_start : q_start + block_rows],
            keys_all[k_start : k_start + key_span],
            positions[q_start : q_start + block_rows],
            seq_ids[q_start : q_start + block_rows],
            pos_all[k_start : k_start + key_span],
            ids_all[k_start : k_start + key_span],
        )
        row_max = jnp.max(masked, axis=-1, keepdims=True)
        exp_terms = jnp.exp(masked - row_max)
        row_total = jnp.sum(exp_terms, axis=-1, keepdims=True)
        prob_low = (exp_terms / row_total).astype(jnp.bfloat16)
        attended_parts.append(
            jnp.einsum(
                "hbs,sd->bhd",
                prob_low,
                values_all[k_start : k_start + key_span],
                preferred_element_type=jnp.float32,
            )
        )
        lse_parts.append(row_max + jnp.log(row_total))
    att_low = (
        jnp.concatenate(attended_parts).reshape(tok_count, head_local * HD).astype(jnp.bfloat16)
    )
    attn_part = jnp.dot(att_low, w_out, preferred_element_type=jnp.float32)
    attn_proj = lax.psum(attn_part, "wa")
    hidden_one = resid_in + rms_scale(attn_proj, norm_gains[1])
    ffn_in = rms_scale(hidden_one, norm_gains[2]).astype(jnp.bfloat16)
    gate_up = jnp.einsum("td,gdf->gtf", ffn_in, w_gateup, preferred_element_type=jnp.float32)
    inner_act = geglu(gate_up[0], gate_up[1]).astype(jnp.bfloat16)
    down_part = jnp.dot(inner_act, w_down, preferred_element_type=jnp.float32)
    down_proj = lax.psum(down_part, "wa")
    layer_out = hidden_one + rms_scale(down_proj, norm_gains[3])
    block_out = layer_out.astype(jnp.bfloat16)
    out_grad = cotangent.astype(jnp.float32)
    post_ffn_pull = jax.vjp(rms_scale, down_proj, norm_gains[3])[1]
    d_down, d_gain3 = post_ffn_pull(out_grad)
    d_down_low = d_down.astype(jnp.bfloat16)
    grad_down = jnp.dot(inner_act.T, d_down_low, preferred_element_type=jnp.float32)
    d_inner = jnp.dot(d_down_low, w_down.T, preferred_element_type=jnp.float32)
    act_pull = jax.vjp(geglu, gate_up[0], gate_up[1])[1]
    d_gate, d_up = act_pull(d_inner)
    d_gateup_low = jnp.stack([d_gate, d_up]).astype(jnp.bfloat16)
    grad_gateup = jnp.einsum(
        "td,gtf->gdf", ffn_in, d_gateup_low, preferred_element_type=jnp.float32
    )
    d_ffn_part = jnp.einsum(
        "gtf,gdf->td", d_gateup_low, w_gateup, preferred_element_type=jnp.float32
    )
    d_ffn = lax.psum(d_ffn_part, "wa")
    pre_ffn_pull = jax.vjp(rms_scale, hidden_one, norm_gains[2])[1]
    d_hidden_b, d_gain2 = pre_ffn_pull(d_ffn)
    d_hidden = out_grad + d_hidden_b
    post_attn_pull = jax.vjp(rms_scale, attn_proj, norm_gains[1])[1]
    d_attn, d_gain1 = post_attn_pull(d_hidden)
    d_attn_low = d_attn.astype(jnp.bfloat16)
    grad_out = jnp.dot(att_low.T, d_attn_low, preferred_element_type=jnp.float32)
    d_att_low = (
        jnp.dot(d_attn_low, w_out.T, preferred_element_type=jnp.float32)
        .astype(jnp.bfloat16)
        .reshape(tok_count, head_local, HD)
    )
    d_query_parts = []
    d_keys_all = jnp.zeros((2 * tok_count, HD), jnp.float32)
    d_values_all = jnp.zeros((2 * tok_count, HD), jnp.float32)
    for block_idx in range(block_total):
        q_start = block_idx * block_rows
        k_start = tok_count + q_start - WINDOW
        query_blk = query_rot[q_start : q_start + block_rows]
        key_blk = keys_all[k_start : k_start + key_span]
        value_blk = values_all[k_start : k_start + key_span]
        masked, tanh_cap = block_scores(
            query_blk,
            key_blk,
            positions[q_start : q_start + block_rows],
            seq_ids[q_start : q_start + block_rows],
            pos_all[k_start : k_start + key_span],
            ids_all[k_start : k_start + key_span],
        )
        prob_f32 = jnp.exp(masked - lse_parts[block_idx])
        prob_low = prob_f32.astype(jnp.bfloat16)
        d_att_blk = d_att_low[q_start : q_start + block_rows]
        d_probs = jnp.einsum(
            "bhd,sd->hbs", d_att_blk, value_blk, preferred_element_type=jnp.float32
        )
        inner_sum = jnp.sum(prob_f32 * d_probs, axis=-1, keepdims=True)
        d_raw = (prob_f32 * (d_probs - inner_sum) * (1.0 - tanh_cap * tanh_cap)).astype(
            jnp.bfloat16
        )
        d_query_parts.append(
            jnp.einsum("hbs,sd->bhd", d_raw, key_blk, preferred_element_type=jnp.float32)
        )
        d_key_blk = jnp.einsum("hbs,bhd->sd", d_raw, query_blk, preferred_element_type=jnp.float32)
        d_value_blk = jnp.einsum(
            "hbs,bhd->sd", prob_low, d_att_blk, preferred_element_type=jnp.float32
        )
        d_keys_all = d_keys_all.at[k_start : k_start + key_span].add(d_key_blk)
        d_values_all = d_values_all.at[k_start : k_start + key_span].add(d_value_blk)
    from_next = (
        shifted(d_keys_all[:tok_count].astype(jnp.bfloat16), "ctx", -1).astype(jnp.float32),
        shifted(d_values_all[:tok_count].astype(jnp.bfloat16), "ctx", -1).astype(jnp.float32),
    )
    d_key_own = d_keys_all[tok_count:] + from_next[0]
    d_value_own = d_values_all[tok_count:] + from_next[1]
    d_key_sum, d_value_sum = (
        lax.psum(d_key_own.astype(jnp.bfloat16), "wa").astype(jnp.float32),
        lax.psum(d_value_own.astype(jnp.bfloat16), "wa").astype(jnp.float32),
    )
    d_key_low = rotate_back(d_key_sum, angles).astype(jnp.bfloat16)
    d_value_low = d_value_sum.astype(jnp.bfloat16)
    d_query_rot = jnp.concatenate(d_query_parts)
    d_query_low = (
        (rotate_back(d_query_rot, angles) * HD ** (-0.5))
        .reshape(tok_count, head_local * HD)
        .astype(jnp.bfloat16)
    )
    half_kv = HD // wa_count
    key_half = take_block(d_key_low, 1, wa_index, half_kv)
    value_half = take_block(d_value_low, 1, wa_index, half_kv)
    w_key_half = take_block(w_keyval[0], 1, wa_index, half_kv)
    w_value_half = take_block(w_keyval[1], 1, wa_index, half_kv)
    grad_query = jnp.dot(normed.T, d_query_low, preferred_element_type=jnp.float32)
    grad_keyval = jnp.stack(
        [
            jnp.dot(normed.T, key_half, preferred_element_type=jnp.float32),
            jnp.dot(normed.T, value_half, preferred_element_type=jnp.float32),
        ]
    )
    d_normed_part = jnp.dot(d_query_low, w_query.T, preferred_element_type=jnp.float32)
    d_normed_part = d_normed_part + jnp.dot(
        key_half, w_key_half.T, preferred_element_type=jnp.float32
    )
    d_normed_part = d_normed_part + jnp.dot(
        value_half, w_value_half.T, preferred_element_type=jnp.float32
    )
    d_normed = lax.psum(d_normed_part.astype(jnp.bfloat16), "wa").astype(jnp.float32)
    pre_attn_pull = jax.vjp(rms_scale, resid_in, norm_gains[0])[1]
    d_tokens, d_gain0 = pre_attn_pull(d_normed)
    input_grad = d_hidden + d_tokens
    grad_gains = jnp.stack([d_gain0, d_gain1, d_gain2, d_gain3])
    sum_query, sum_keyval, sum_out, sum_gateup, sum_down, sum_gains = (
        lax.psum_scatter(grad_query, "ctx", scatter_dimension=0, tiled=True),
        lax.psum_scatter(grad_keyval, "ctx", scatter_dimension=1, tiled=True),
        lax.psum_scatter(grad_out, "ctx", scatter_dimension=1, tiled=True),
        lax.psum_scatter(grad_gateup, "ctx", scatter_dimension=1, tiled=True),
        lax.psum_scatter(grad_down, "ctx", scatter_dimension=1, tiled=True),
        lax.psum_scatter(grad_gains, "ctx", scatter_dimension=1, tiled=True),
    )
    new_mom_query = MOMENTUM * mom_query + sum_query
    new_mom_keyval = MOMENTUM * mom_keyval + sum_keyval
    new_mom_out = MOMENTUM * mom_out + sum_out
    new_mom_gateup = MOMENTUM * mom_gateup + sum_gateup
    new_mom_down = MOMENTUM * mom_down + sum_down
    new_gain_first = ADAM_ONE * gain_first + (1.0 - ADAM_ONE) * sum_gains
    new_gain_second = ADAM_TWO * gain_second + (1.0 - ADAM_TWO) * sum_gains * sum_gains
    gain_update = -GAIN_RATE * new_gain_first / (jnp.sqrt(new_gain_second) + ADAM_EPS)
    dev_count = ctx_count * wa_count
    me_flat = ctx_index * wa_count + wa_index
    shards = [
        new_mom_query,
        new_mom_keyval[0],
        new_mom_keyval[1],
        new_mom_out,
        new_mom_gateup[0],
        new_mom_gateup[1],
        new_mom_down,
    ]
    ctx_dims = [0, 0, 0, 1, 0, 0, 1]
    full_shapes = [(D, HQ), (D, HD), (D, HD), (HQ, D), (D, FF), (D, FF), (FF, D)]
    elem_counts = [part_mat.shape[0] * part_mat.shape[1] for part_mat in shards]
    owners = [
        mat_idx * ctx_count // MATRIX_COUNT * wa_count + mat_idx % wa_count
        for mat_idx in range(MATRIX_COUNT)
    ]
    own_index = jnp.int32(MATRIX_COUNT)
    for mat_idx in range(MATRIX_COUNT):
        own_index = jnp.where(me_flat == owners[mat_idx], mat_idx, own_index)
    flat_parts = [part_mat.reshape(1, -1) for part_mat in shards]
    gathered = (
        lax.all_gather(flat_parts[0], ("ctx", "wa"), axis=0, tiled=True),
        lax.all_gather(flat_parts[1], ("ctx", "wa"), axis=0, tiled=True),
        lax.all_gather(flat_parts[2], ("ctx", "wa"), axis=0, tiled=True),
        lax.all_gather(flat_parts[3], ("ctx", "wa"), axis=0, tiled=True),
        lax.all_gather(flat_parts[4], ("ctx", "wa"), axis=0, tiled=True),
        lax.all_gather(flat_parts[5], ("ctx", "wa"), axis=0, tiled=True),
        lax.all_gather(flat_parts[6], ("ctx", "wa"), axis=0, tiled=True),
    )
    offsets = [sum(elem_counts[:mat_idx]) for mat_idx in range(MATRIX_COUNT)]
    total_cols = sum(elem_counts)
    branches = [
        partial(
            owner_tiles,
            mat_idx=mat_idx,
            ctx_dim=ctx_dims[mat_idx],
            row_count=full_shapes[mat_idx][0],
            col_count=full_shapes[mat_idx][1],
            ctx_count=ctx_count,
            wa_count=wa_count,
            offset=offsets[mat_idx],
            total_cols=total_cols,
            from_slots=False,
        )
        for mat_idx in range(MATRIX_COUNT)
    ]
    branches.append(partial(empty_tiles, dev_count=dev_count, total_cols=total_cols))
    back_tiles = lax.switch(own_index, branches, gathered)
    own_row = lax.psum_scatter(back_tiles, ("ctx", "wa"), scatter_dimension=0, tiled=True)
    upd_parts = [
        own_row[0, offsets[mat_idx] : offsets[mat_idx] + elem_counts[mat_idx]].reshape(
            shards[mat_idx].shape
        )
        for mat_idx in range(MATRIX_COUNT)
    ]
    upd_query = upd_parts[0]
    upd_keyval = jnp.stack([upd_parts[1], upd_parts[2]])
    upd_out = upd_parts[3]
    upd_gateup = jnp.stack([upd_parts[4], upd_parts[5]])
    upd_down = upd_parts[6]
    return (
        block_out,
        input_grad,
        sum_query,
        sum_keyval,
        sum_out,
        sum_gateup,
        sum_down,
        sum_gains,
        new_mom_query,
        new_mom_keyval,
        new_mom_out,
        new_mom_gateup,
        new_mom_down,
        upd_query,
        upd_keyval,
        upd_out,
        upd_gateup,
        upd_down,
        new_gain_first,
        new_gain_second,
        gain_update,
    )


def solution(mesh):
    in_specs = (
        P("ctx", None),
        P("ctx", None),
        P("ctx"),
        P(None, "wa"),
        P(),
        P("wa", None),
        P(None, None, "wa"),
        P("wa", None),
        P(),
        P("ctx", "wa"),
        P(None, "ctx", "wa"),
        P("wa", "ctx"),
        P(None, "ctx", "wa"),
        P("wa", "ctx"),
        P(None, "ctx"),
        P(None, "ctx"),
    )
    out_specs = (
        P("ctx", None),
        P("ctx", None),
        P("ctx", "wa"),
        P(None, "ctx", "wa"),
        P("wa", "ctx"),
        P(None, "ctx", "wa"),
        P("wa", "ctx"),
        P(None, "ctx"),
        P("ctx", "wa"),
        P(None, "ctx", "wa"),
        P("wa", "ctx"),
        P(None, "ctx", "wa"),
        P("wa", "ctx"),
        P("ctx", "wa"),
        P(None, "ctx", "wa"),
        P("wa", "ctx"),
        P(None, "ctx", "wa"),
        P("wa", "ctx"),
        P(None, "ctx"),
        P(None, "ctx"),
        P(None, "ctx"),
    )
    return jax.shard_map(
        per_device, mesh=mesh, in_specs=in_specs, out_specs=out_specs, check_vma=False
    )
```

profile of v0, /device:TPU:15, one launch (start us, length us, event | category | flops | bytes accessed | tf_op | source)
XLA Modules:
  0.0 1818.3 jit_solution(3074576783912477502)
XLA Ops:
  64.5 23.8 %all-reduce.21.cloned.1.call-done = f32[1024,640]{1,0:T(8,128)} async-done(((f32[1024,640]{1,0:T(8,128)}), f32[1024,640]{1,0:T(8,128)}) %all-reduce.21.cloned.1.call-update) | async-done | bytes 2621456 | tf_op jit(solution)/shard_map/psum | solution.py:257
  104.4 23.5 %all-reduce.23.cloned.1.call-done = f32[1024,640]{1,0:T(8,128)} async-done(((f32[1024,640]{1,0:T(8,128)}), f32[1024,640]{1,0:T(8,128)}) %all-reduce.23.cloned.1.call-update) | async-done | bytes 2621456 | tf_op jit(solution)/shard_map/psum | solution.py:263
  151.2 23.2 %all-reduce.25.cloned.1.call-done = f32[1024,640]{1,0:T(8,128)} async-done(((f32[1024,640]{1,0:T(8,128)}), f32[1024,640]{1,0:T(8,128)}) %all-reduce.25.cloned.1.call-update) | async-done | bytes 2621456 | tf_op jit(solution)/shard_map/psum | solution.py:281
  194.9 11.3 fusion.324
  224.2 11.5 add_convert_fusion.3
  236.1 11.1 fusion.321
  247.2 11.2 fusion.323
  271.8 8.3 fusion.291
  280.1 8.9 copy.316
  302.3 20.7 %reduce-scatter.6.cloned.1.call-done = f32[40,512]{1,0:T(8,128)} async-done(((f32[640,512]{1,0:T(8,128)}), f32[40,512]{1,0:T(8,128)}) %reduce-scatter.6.cloned.1.call-update) | async-done | bytes 81936 | tf_op jit(solution)/shard_map/reduce_scatter | solution.py:373
  324.8 76.2 %reduce-scatter.10.cloned.1.call-done = f32[512,40]{0,1:T(8,128)} async-done(((f32[512,640]{0,1:T(8,128)}), f32[512,40]{0,1:T(8,128)}) %reduce-scatter.10.cloned.1.call-update) | async-done | bytes 81936 | tf_op jit(solution)/shard_map/reduce_scatter | solution.py:375
  404.3 211.4 %all-reduce.29.cloned.1.call-done = f32[2,640,1024]{2,0,1:T(2,128)} async-done(((f32[2,640,1024]{2,0,1:T(2,128)}), f32[2,640,1024]{2,0,1:T(2,128)}) %all-reduce.29.cloned.1.call-update) | async-done | bytes 5242896
  619.6 60.3 %reduce-scatter.12.cloned.1.call-done = f32[1024,40]{0,1:T(8,128)} async-done(((f32[1024,640]{0,1:T(8,128)}), f32[1024,40]{0,1:T(8,128)}) %reduce-scatter.12.cloned.1.call-update) | async-done | bytes 163856 | tf_op jit(solution)/shard_map/reduce_scatter | solution.py:377
  687.6 65.7 %reduce-scatter.8.cloned.1.call-done = f32[2,40,128]{2,1,0:T(8,128)} async-done(((f32[2,640,128]{2,1,0:T(8,128)}), f32[2,40,128]{2,1,0:T(8,128)}) %reduce-scatter.8.cloned.1.call-update) | async-done | bytes 40976 | tf_op jit(solution)/shard_map/reduce_scatter | solution.py:374
  754.0 54.5 %all-gather.1 = f32[32,1,5120]{2,1,0:T(1,128)S(1)} all-gather(f32[1,1,5120]{2,1,0:T(1,128)S(1)} %bitcast.811), channel_id=1, replica_groups=mesh['ctx'=16,'wa'=2] {'ctx','wa'}, dimensions={0}, use_global_device_ids=true | all-gather | bytes 675840 | tf_op jit(solution)/shard_map/all_gather | solution.py:412
  808.6 41.6 %all-gather.2 = f32[32,1,5120]{2,1,0:T(1,128)} all-gather(f32[1,1,5120]{2,1,0:T(1,128)S(1)} %bitcast.810), channel_id=1, replica_groups=mesh['ctx'=16,'wa'=2] {'ctx','wa'}, dimensions={0}, use_global_device_ids=true | all-gather | bytes 675840 | tf_op jit(solution)/shard_map/all_gather | solution.py:413
  850.2 47.0 %all-gather.15.cloned.1.call-done = f32[32,1,20480]{2,1,0:T(1,128)} async-done(((f32[1,1,20480]{2,1,0:T(1,128)}), f32[32,1,20480]{2,1,0:T(1,128)}) %all-gather.15.cloned.1.call-update) | async-done | bytes 2621456 | tf_op jit(solution)/shard_map/all_gather | solution.py:414
  897.1 69.4 %all-gather.17.cloned.1.call-done = f32[32,1,40960]{2,1,0:T(1,128)} async-done(((f32[1,1,40960]{2,1,0:T(1,128)}), f32[32,1,40960]{2,1,0:T(1,128)}) %all-gather.17.cloned.1.call-update) | async-done | bytes 5242896 | tf_op jit(solution)/shard_map/all_gather | solution.py:415
  966.5 68.0 %all-gather.19.cloned.1.call-done = f32[32,1,40960]{2,1,0:T(1,128)} async-done(((f32[1,1,40960]{2,1,0:T(1,128)}), f32[32,1,40960]{2,1,0:T(1,128)}) %all-gather.19.cloned.1.call-update) | async-done | bytes 5242896 | tf_op jit(solution)/shard_map/all_gather | solution.py:416
  1034.5 67.3 %all-gather.21.cloned.1.call-done = f32[32,1,40960]{2,1,0:T(1,128)} async-done(((f32[1,1,40960]{2,1,0:T(1,128)}), f32[32,1,40960]{2,1,0:T(1,128)}) %all-gather.21.cloned.1.call-update) | async-done | bytes 5242896 | tf_op jit(solution)/shard_map/all_gather | solution.py:417
  1101.8 41.8 %conditional.1 = (f32[32,174080]{1,0:T(8,128)}) conditional(s32[]{:T(128)} %clamp.3, (f32[32,1,20480]{2,1,0:T(1,128)}) %tuple.83, (f32[32,1,5120]{2,1,0:T(1,128)S(1)}) %tuple.84, (f32[32,1,5120]{2,1,0:T(1,128)}) %tuple.85, (f32[32,1,20480]{2,1,0:T(1,128)}) %tuple.86, (f32[32,1,40960]{2,1,0:T(1,128)}) %tuple.87, ...), branch_computations={%region_30.0_spmd, %region_33.0_spmd, %region_36.0_spmd, %region_3... | conditional | flops 116442644480 | bytes 496304480 | solution.py:437
  1135.6 7.8 broadcast.831
  1149.0 242.8 %all-reduce.10 = f32[4,640]{1,0:T(4,128)S(1)} all-reduce(f32[4,640]{1,0:T(4,128)S(1)} %pad_maximum_fusion.16), channel_id=7, replica_groups=mesh['ctx'=16,'wa'=2] {'ctx'}, use_global_device_ids=true, to_apply=%region_29.30.clone | all-reduce | flops 2560 | bytes 20480
  1397.3 401.9 %all-reduce.31.cloned.1.call-done = f32[32,174080]{1,0:T(8,128)} async-done(((f32[32,174080]{1,0:T(8,128)}), f32[32,174080]{1,0:T(8,128)}) %all-reduce.31.cloned.1.call-update) | async-done | bytes 22282256
  (299 shorter events, 201.2 us)
Async XLA Ops:
  7.2 81.1 %all-reduce.21.cloned.1.call-start = ((), (), s32[]{:S(2)}) async-start(), calls=%async_computation.4 | async-start | bytes 5242880 | tf_op jit(solution)/shard_map/psum | solution.py:257
  7.3 45.1 %collective-permute-start.2 = (s32[1024]{0:T(1024)S(1)}, s32[1024]{0:T(1024)S(1)}, u32[]{:S(2)}, u32[]{:S(2)}) collective-permute-start(s32[1024]{0:T(1024)S(1)} %iota_add_fusion), channel_id=1, source_target_pairs={{0,2},{2,4},{4,6},{6,8},{8,10},{10,12},{12,14},{14,16},{16,18},{18... | collective-permute-start | bytes 12296 | tf_op jit(solution)/shard_map/ppermute | solution.py:37
  10.5 41.9 %collective-permute-start.1 = (s32[1024]{0:T(1024)}, s32[1024]{0:T(1024)S(1)}, u32[]{:S(2)}, u32[]{:S(2)}) collective-permute-start(s32[1024]{0:T(1024)} %param.48), channel_id=1, source_target_pairs={{0,2},{2,4},{4,6},{6,8},{8,10},{10,12},{12,14},{14,16},{16,18},{18... | collective-permute-start | bytes 12296 | tf_op jit(solution)/shard_map/ppermute | solution.py:37
  22.5 30.9 %collective-permute-start.3 = (bf16[1024,256]{0,1:T(8,128)(2,1)}, bf16[1024,256]{0,1:T(8,128)(2,1)}, u32[]{:S(2)}, u32[]{:S(2)}) collective-permute-start(bf16[1024,256]{0,1:T(8,128)(2,1)} %pad_maximum_fusion.13), channel_id=1, source_target_pairs={{0,2},{2,4},{4,6},{6,8},{8,10},{10,12},{12,14},{14,16},{16,18},{18... | collective-permute-start | bytes 1572872 | tf_op jit(solution)/shard_map/ppermute | solution.py:37
  27.1 30.3 %collective-permute-start = (bf16[1024,256]{1,0:T(8,128)(2,1)}, bf16[1024,256]{1,0:T(8,128)(2,1)}, u32[]{:S(2)}, u32[]{:S(2)}) collective-permute-start(bf16[1024,256]{1,0:T(8,128)(2,1)} %convolution_convert_fusion.1), channel_id=1, source_target_pairs={{0,2},{2,4},{4,6},{6,8},{8,10},{10,12},{12,14},{14,16},{16,18},{18... | collective-permute-start | bytes 1572872 | tf_op jit(solution)/shard_map/ppermute | solution.py:37
  64.1 63.8 %all-reduce.23.cloned.1.call-start = ((), (), s32[]{:S(2)}) async-start(), calls=%async_computation.5 | async-start | bytes 5242880 | tf_op jit(solution)/shard_map/psum | solution.py:263
  104.4 70.1 %all-reduce.25.cloned.1.call-start = ((), (), s32[]{:S(2)}) async-start(), calls=%async_computation.6 | async-start | bytes 5242880 | tf_op jit(solution)/shard_map/psum | solution.py:281
  151.0 144.1 %all-reduce.33.cloned.1.call-start = ((), (), s32[]{:S(2)}) async-start(), calls=%async_computation.19 | async-start | bytes 2097152 | tf_op jit(solution)/shard_map/psum | solution.py:337
  189.1 25.6 %collective-permute-start.5 = (bf16[1024,256]{1,0:T(8,128)(2,1)}, bf16[1024,256]{1,0:T(8,128)(2,1)}, u32[]{:S(2)}, u32[]{:S(2)}) collective-permute-start(bf16[1024,256]{1,0:T(8,128)(2,1)} %pad_convert_fusion), channel_id=1, source_target_pairs={{2,0},{4,2},{6,4},{8,6},{10,8},{12,10},{14,12},{16,14},{18,16},{20... | collective-permute-start | bytes 1572872 | tf_op jit(solution)/shard_map/ppermute | solution.py:37
  207.4 16.8 collective-permute-start.4
  235.7 87.4 %reduce-scatter.6.cloned.1.call-start = ((), (), s32[]{:S(2)}) async-start(), calls=%async_computation.8 | async-start | bytes 1392640 | tf_op jit(solution)/shard_map/reduce_scatter | solution.py:373
  267.9 133.0 %reduce-scatter.10.cloned.1.call-start = ((), (), s32[]{:S(2)}) async-start(), calls=%async_computation.10 | async-start | bytes 1392640 | tf_op jit(solution)/shard_map/reduce_scatter | solution.py:375
  271.6 344.0 %all-reduce.29.cloned.1.call-start = ((), (), s32[]{:S(2)}) async-start(), calls=%async_computation.17 | async-start | bytes 10485760
  289.0 390.9 %reduce-scatter.12.cloned.1.call-start = ((), (), s32[]{:S(2)}) async-start(), calls=%async_computation.11 | async-start | bytes 2785280 | tf_op jit(solution)/shard_map/reduce_scatter | solution.py:377
  295.0 458.2 %reduce-scatter.8.cloned.1.call-start = ((), (), s32[]{:S(2)}) async-start(), calls=%async_computation.9 | async-start | bytes 696320 | tf_op jit(solution)/shard_map/reduce_scatter | solution.py:374
  301.4 378.5 %copy-start.63 = (f32[1024,40]{0,1:T(8,128)S(1)}, f32[1024,40]{0,1:T(8,128)}, u32[]{:S(2)}) copy-start(f32[1024,40]{0,1:T(8,128)} %param.59) | copy-start | bytes 491524
  302.3 547.9 %all-gather.13.cloned.1.call-start = ((), (), s32[]{:S(2)}) async-start(), calls=%async_computation.12 | async-start | bytes 2703360 | tf_op jit(solution)/shard_map/all_gather | solution.py:411
  324.7 572.4 %all-gather.15.cloned.1.call-start = ((), (), s32[]{:S(2)}) async-start(), calls=%async_computation.13 | async-start | bytes 2703360 | tf_op jit(solution)/shard_map/all_gather | solution.py:414
  403.0 563.5 %all-gather.17.cloned.1.call-start = ((), (), s32[]{:S(2)}) async-start(), calls=%async_computation.14 | async-start | bytes 5406720 | tf_op jit(solution)/shard_map/all_gather | solution.py:415
  618.8 415.7 %all-gather.19.cloned.1.call-start = ((), (), s32[]{:S(2)}) async-start(), calls=%async_computation.15 | async-start | bytes 5406720 | tf_op jit(solution)/shard_map/all_gather | solution.py:416
  619.5 482.2 %all-gather.21.cloned.1.call-start = ((), (), s32[]{:S(2)}) async-start(), calls=%async_computation.16 | async-start | bytes 5406720 | tf_op jit(solution)/shard_map/all_gather | solution.py:417
  682.2 464.1 %all-reduce.27.cloned.1.call-start = ((), (), s32[]{:S(2)}) async-start(), calls=%async_computation.7 | async-start | bytes 2621440 | tf_op jit(solution)/shard_map/psum | solution.py:367
  687.5 1111.7 %all-reduce.31.cloned.1.call-start = ((), (), s32[]{:S(2)}) async-start(), calls=%async_computation.18 | async-start | bytes 44564480
  1392.4 419.1 %copy-start.1 = (bf16[2,640,1024]{2,1,0:T(8,128)(2,1)S(1)}, bf16[2,640,1024]{2,1,0:T(8,128)(2,1)}, u32[]{:S(2)}) copy-start(bf16[2,640,1024]{2,1,0:T(8,128)(2,1)} %param.52) | copy-start | bytes 7864324
  (68 other events, 3187.9 us)
Sparse Core Ops, SparseCore 0:
  64.2 24.0 all-reduce.20
  104.5 23.3 all-reduce.22
  151.1 23.3 all-reduce.24
  235.8 21.0 all-reduce.32
  268.1 54.9 reduce-scatter.5
  325.7 75.2 reduce-scatter.9
  406.7 208.8 all-reduce.28
  618.5 61.3 reduce-scatter.11
  682.7 70.4 reduce-scatter.7
  756.9 79.3 all-gather.12
  840.1 57.0 all-gather.14
  900.8 65.6 all-gather.16
  970.3 64.1 all-gather.18
  1037.6 64.1 all-gather.20
  1104.1 19.5 all-reduce.26
  1143.8 655.2 all-reduce.30
where the time goes:
time: 1830 us; the launch traced here: 1820 us
  waiting for transfers between devices  1170 us (64%)
  blocking collectives  339 us (19%)
  matrix products  122 us (7%)
  local copies, waits for them, and re-layouts  65.6 us (4%)
  other arithmetic  56.9 us (3%)
  loops' own time  34 us (2%)
  starting transfers between devices  19.7 us (1%)
    unnamed x18, waiting for transfers between devices  614 us
    unnamed x1, blocking collectives  243 us
    reduce_scatter x1, waiting for transfers between devices, per_device(): lax.psum_scatter(grad_out, 'ctx', scatter_dimension=1, tiled=True)  76.2 us
    all_gather x1, waiting for transfers between devices, per_device(): lax.all_gather(flat_parts[4], ('ctx', 'wa'), axis=0, tiled=True)  69.4 us
    all_gather x1, waiting for transfers between devices, per_device(): lax.all_gather(flat_parts[5], ('ctx', 'wa'), axis=0, tiled=True)  68 us
    all_gather x1, waiting for transfers between devices, per_device(): lax.all_gather(flat_parts[6], ('ctx', 'wa'), axis=0, tiled=True)  67.3 us
    reduce_scatter x1, waiting for transfers between devices, per_device(): lax.psum_scatter(grad_keyval, 'ctx', scatter_dimension=1, tiled=True)  65.7 us
    reduce_scatter x1, waiting for transfers between devices, per_device(): lax.psum_scatter(grad_down, 'ctx', scatter_dimension=1, tiled=True)  60.3 us
  transfers between devices with their start and end apart: 22, of which 14 were waited for; matrix products, arithmetic and copies ran while one was open for 9% of the time, Pallas kernels for 0%

commit v1 on v0

--- a/solution.py
+++ b/solution.py
@@ -4,6 +4,8 @@
 import jax
 import jax.numpy as jnp
 from jax import lax
+from jax.experimental import pallas as pl
+from jax.experimental.pallas import tpu as pltpu
 from jax.sharding import PartitionSpec as P
 
 D = 640
@@ -105,76 +107,438 @@
     return (masked, tanh_cap)
 
 
-def orthogonalize(matrix):
-    flipped = matrix.shape[0] > matrix.shape[1]
-    iterate = matrix.T if flipped else matrix
-    iterate = iterate / (jnp.sqrt(jnp.sum(iterate * iterate)) + 1e-07)
-    for sweep in range(NS_STEPS):
-        gram_mat = jnp.dot(iterate, iterate.T, precision=HIGHEST_PREC)
-        poly_mat = QUINTIC_B * gram_mat + QUINTIC_C * jnp.dot(
-            gram_mat, gram_mat, precision=HIGHEST_PREC
-        )
-        iterate = QUINTIC_A * iterate + jnp.dot(poly_mat, iterate, precision=HIGHEST_PREC)
-    return iterate.T if flipped else iterate
-
-
-def muon_update(matrix):
-    return (
-        -MUON_RATE * 0.2 * math.sqrt(max(matrix.shape[0], matrix.shape[1])) * orthogonalize(matrix)
-    )
-
-
 def take_block(array_in, along_dim, block_index, block_size):
     return lax.dynamic_slice_in_dim(array_in, block_index * block_size, block_size, along_dim)
 
 
-def split_blocks(matrix, ctx_dim, ctx_count, wa_count):
-    row_count, col_count = matrix.shape
-    if ctx_dim == 0:
-        tile_grid = matrix.reshape(
-            ctx_count, row_count // ctx_count, wa_count, col_count // wa_count
-        ).transpose(0, 2, 1, 3)
-    else:
-        tile_grid = matrix.reshape(
-            wa_count, row_count // wa_count, ctx_count, col_count // ctx_count
-        ).transpose(2, 0, 1, 3)
-    return tile_grid.reshape(ctx_count * wa_count, -1)
-
-
-def join_blocks(tile_rows, ctx_dim, row_count, col_count, ctx_count, wa_count):
-    if ctx_dim == 0:
-        tile_grid = tile_rows.reshape(
-            ctx_count, wa_count, row_count // ctx_count, col_count // wa_count
-        ).transpose(0, 2, 1, 3)
-    else:
-        tile_grid = tile_rows.reshape(
-            ctx_count, wa_count, row_count // wa_count, col_count // ctx_count
-        ).transpose(1, 2, 0, 3)
-    return tile_grid.reshape(row_count, col_count)
-
-
-def owner_tiles(
-    operand,
-    mat_idx,
-    ctx_dim,
-    row_count,
-    col_count,
+MESH = pl.DeviceIdType.MESH
+BF = jnp.bfloat16
+F32 = jnp.float32
+IN_COUNT = 4
+NAMES = ("down", "gate", "up", "out", "query", "key", "value")
+WIDTHS = (FF, FF, FF, HQ, HQ, HD, HD)
+OWNERS = (7, 4, 8, 5, 11, 9, 10)
+CHUNK_SETS = ((0,), (1,), (2,), (3, 4, 5, 6))
+TILE = 256
+
+
+def layout(wa_count):
+    halves = [w // wa_count for w in WIDTHS]
+    offs = [sum(halves[:i]) for i in range(len(halves))]
+    return halves, offs, sum(halves)
+
+
+def dot32(a, b):
+    return jnp.dot(a, b, preferred_element_type=F32)
+
+
+def eye_mask(n):
+    return (
+        lax.broadcasted_iota(jnp.int32, (n, n), 0) == lax.broadcasted_iota(jnp.int32, (n, n), 1)
+    )
+
+
+def pad_rows(v, rows):
+    if v.shape[0] == rows:
+        return v
+    return jnp.concatenate([v, jnp.zeros((rows - v.shape[0], v.shape[1]), v.dtype)], axis=0)
+
+
+def split_into(v, hi, lo):
+    top = v.astype(BF)
+    hi[...] = top
+    lo[...] = (v - top.astype(F32)).astype(BF)
+
+
+def mm3(h1, l1, h2, l2):
+    return dot32(h1[...], h2[...]) + dot32(h1[...], l2[...]) + dot32(l1[...], h2[...])
+
+
+def tail_kernel(
     ctx_count,
     wa_count,
-    offset,
-    total_cols,
-    from_slots,
+    g_ref,
+    mom_ref,
+    sum_ref,
+    nm_ref,
+    upd_ref,
+    own,
+    pr,
+    s3,
+    ls,
+    lr,
+    mb,
+    xb,
+    xf,
+    xc,
+    ob,
+    ub,
+    am,
+    ah,
+    al,
+    ph,
+    plo,
+    qh,
+    ql,
+    own_sem,
+    psend,
+    precv,
+    lsend,
+    lrecv,
+    gsend,
+    grecv,
+    usend,
+    urecv,
 ):
-    elem_count = row_count * col_count // (ctx_count * wa_count)
-    tile_src = operand[:, :elem_count] if from_slots else operand[mat_idx]
-    matrix = join_blocks(tile_src, ctx_dim, row_count, col_count, ctx_count, wa_count)
-    tile_rows = split_blocks(muon_update(matrix), ctx_dim, ctx_count, wa_count)
-    placed = jnp.zeros((ctx_count * wa_count, total_cols), jnp.float32)
-    return placed.at[:, offset : offset + elem_count].set(tile_rows)
-
-
-def empty_tiles(operand, dev_count, total_cols):
-    return jnp.zeros((dev_count, total_cols), jnp.float32)
+    c = lax.axis_index("ctx")
+    w = lax.axis_index("wa")
+    n_in = IN_COUNT
+    n_out = ctx_count // n_in
+    n_dev = ctx_count * wa_count
+    p = lax.rem(c, n_in)
+    z = lax.div(c, n_in)
+    rows = D // ctx_count
+    rp = xb.shape[1]
+    halves, offs, cols = layout(wa_count)
+    chunks = [(offs[s[0]], sum(halves[m] for m in s)) for s in CHUNK_SETS]
+    me = c * wa_count + w
+
+    barrier = pltpu.get_barrier_semaphore()
+
+    def greet(i, carry):
+        other = lax.rem(me + i, n_dev)
+        pl.semaphore_signal(
+            barrier,
+            inc=1,
+            device_id=(lax.div(other, wa_count), lax.rem(other, wa_count)),
+            device_id_type=MESH,
+        )
+        return carry
+
+    lax.fori_loop(1, n_dev, greet, 0)
+    pl.semaphore_wait(barrier, n_dev - 1)
+
+    def plane_copy(ci, k):
+        off, wid = chunks[ci]
+        q = lax.rem(p + k, n_in)
+        return pltpu.make_async_remote_copy(
+            g_ref.at[q, :, pl.ds(off, wid)],
+            pr.at[k - 1, :, pl.ds(off, wid)],
+            psend.at[ci, k - 1],
+            precv.at[ci, k - 1],
+            device_id=(z * n_in + q, w),
+            device_id_type=MESH,
+        )
+
+    def own_copy(ci):
+        off, wid = chunks[ci]
+        return pltpu.make_async_copy(
+            g_ref.at[p, :, pl.ds(off, wid)], own.at[:, pl.ds(off, wid)], own_sem.at[ci]
+        )
+
+    def line_copy(ci, k):
+        off, wid = chunks[ci]
+        j = lax.rem(z + k, n_out)
+        return pltpu.make_async_remote_copy(
+            ls.at[j, :, pl.ds(off, wid)],
+            lr.at[k - 1, :, pl.ds(off, wid)],
+            lsend.at[ci, k - 1],
+            lrecv.at[ci, k - 1],
+            device_id=(j * n_in + p, w),
+            device_id_type=MESH,
+        )
+
+    def gather_remote(m):
+        return pltpu.make_async_remote_copy(
+            mb.at[:, pl.ds(offs[m], halves[m])],
+            xb.at[c, :, pl.ds(pl.multiple_of(w * halves[m], 128), halves[m])],
+            gsend.at[m],
+            grecv,
+            device_id=(OWNERS[m], 0),
+            device_id_type=MESH,
+        )
+
+    def gather_local(m):
+        return pltpu.make_async_copy(
+            mb.at[:, pl.ds(offs[m], halves[m])],
+            xb.at[c, :, pl.ds(pl.multiple_of(w * halves[m], 128), halves[m])],
+            grecv,
+        )
+
+    for ci in range(len(chunks)):
+        own_copy(ci).start()
+        for k in range(1, n_in):
+            plane_copy(ci, k).start()
+
+    for ci, (off, wid) in enumerate(chunks):
+        own_copy(ci).wait()
+        for k in range(1, n_in):
+            plane_copy(ci, k).wait_recv()
+
+        def plane_sum(t, carry, off=off):
+            cs = pl.ds(pl.multiple_of(off + t * TILE, TILE), TILE)
+            s = own[:, cs].astype(F32)
+            for k in range(n_in - 1):
+                s = s + pr[k, :, cs].astype(F32)
+            for j in range(n_out):
+                slab = s[j * rows : (j + 1) * rows]
+                s3[j, :, cs] = slab
+                ls[j, :, cs] = pad_rows(slab, rp).astype(BF)
+            return carry
+
+        lax.fori_loop(0, wid // TILE, plane_sum, 0)
+        for k in range(1, n_out):
+            line_copy(ci, k).start()
+
+    for ci, (off, wid) in enumerate(chunks):
+        for k in range(1, n_out):
+            line_copy(ci, k).wait_recv()
+
+        def line_sum(t, carry, off=off):
+            cs = pl.ds(pl.multiple_of(off + t * TILE, TILE), TILE)
+            s = s3[z, :, cs]
+            for k in range(n_out - 1):
+                s = s + lr[k, :, cs][:rows].astype(F32)
+            sum_ref[:, cs] = s
+            nm = MOMENTUM * mom_ref[:, cs] + s
+            nm_ref[:, cs] = nm
+            mb[:, cs] = pad_rows(nm, rp).astype(BF)
+            return carry
+
+        lax.fori_loop(0, wid // TILE, line_sum, 0)
+        for m in CHUNK_SETS[ci]:
+            mine = me == OWNERS[m] * wa_count
+
+            @pl.when(mine)
+            def _(m=m):
+                gather_local(m).start()
+
+            @pl.when(jnp.logical_not(mine))
+            def _(m=m):
+                gather_remote(m).start()
+
+    is_owner = me == OWNERS[0] * wa_count
+    for m in range(1, MATRIX_COUNT):
+        is_owner = jnp.logical_or(is_owner, me == OWNERS[m] * wa_count)
+    is_small = jnp.logical_or(me == OWNERS[5] * wa_count, me == OWNERS[6] * wa_count)
+    is_wide = me == OWNERS[0] * wa_count
+    for m in (1, 2):
+        is_wide = jnp.logical_or(is_wide, me == OWNERS[m] * wa_count)
+    tiles = jnp.where(is_small, HD // TILE, jnp.where(is_wide, FF // TILE, HQ // TILE))
+
+    for m in range(MATRIX_COUNT):
+
+        @pl.when(me == OWNERS[m] * wa_count)
+        def _(m=m):
+            whole = xb.at[:, :, pl.ds(0, halves[m] * wa_count)]
+            pltpu.make_async_copy(whole, whole, grecv).wait()
+
+    @pl.when(is_owner)
+    def _():
+        am[...] = jnp.zeros_like(am)
+
+        def gram(t, carry):
+            cs = pl.ds(pl.multiple_of(t * TILE, TILE), TILE)
+            for i in range(ctx_count):
+                xf[i * rows : (i + 1) * rows, :] = xb[i, :, cs][:rows].astype(F32)
+            x = xf[...].astype(BF)
+            xc[:, cs] = x
+
+            @pl.when(jnp.logical_not(is_small))
+            def _():
+                am[...] += lax.dot_general(
+                    x, x, (((1,), (1,)), ((), ())), preferred_element_type=F32
+                )
+
+            @pl.when(is_small)
+            def _():
+                am[0:HD, 0:HD] = lax.dot_general(
+                    x, x, (((0,), (0,)), ((), ())), preferred_element_type=F32
+                )
+
+            return carry
+
+        lax.fori_loop(0, tiles, gram, 0)
+        diag = eye_mask(D)
+        norm2 = jnp.sum(jnp.where(diag, am[...], 0.0), keepdims=True)
+        inv = 1.0 / (jnp.sqrt(norm2) + 1e-07)
+        am[...] = am[...] * (inv * inv)
+
+        def poly():
+            split_into(am[...], ah, al)
+            return (
+                QUINTIC_B * am[...]
+                + QUINTIC_C * mm3(ah, al, ah, al)
+                + jnp.where(eye_mask(D), QUINTIC_A, 0.0)
+            )
+
+        def advance():
+            b = mm3(ph, plo, ah, al)
+            split_into(b, ah, al)
+            am[...] = mm3(ah, al, ph, plo)
+
+        first = poly()
+        split_into(first, ph, plo)
+        split_into(first, qh, ql)
+        advance()
+
+        def sweep(i, carry):
+            split_into(poly(), ph, plo)
+            split_into(mm3(ph, plo, qh, ql), qh, ql)
+
+            @pl.when(i < NS_STEPS - 2)
+            def _():
+                advance()
+
+            return carry
+
+        lax.fori_loop(0, NS_STEPS - 1, sweep, 0)
+        wide_rate = -MUON_RATE * 0.2 * math.sqrt(FF)
+        mid_rate = -MUON_RATE * 0.2 * math.sqrt(HQ)
+        low_rate = -MUON_RATE * 0.2 * math.sqrt(D)
+        rate = jnp.where(is_small, low_rate, jnp.where(is_wide, wide_rate, mid_rate))
+        scale = rate * inv
+
+        def back(t, carry):
+            cs = pl.ds(pl.multiple_of(t * TILE, TILE), TILE)
+
+            @pl.when(jnp.logical_not(is_small))
+            def _():
+                xf[...] = dot32(qh[...], xc[:, cs]) * scale
+
+            @pl.when(is_small)
+            def _():
+                xf[...] = dot32(xc[:, cs], qh[0:HD, 0:HD]) * scale
+
+            for i in range(ctx_count):
+                ob[i, :, cs] = pad_rows(xf[i * rows : (i + 1) * rows, :], rp).astype(BF)
+            return carry
+
+        lax.fori_loop(0, tiles, back, 0)
+
+    for m in range(MATRIX_COUNT):
+
+        def pieces(t, m=m):
+            i = lax.div(t, wa_count)
+            v = lax.rem(t, wa_count)
+            src = ob.at[i, :, pl.ds(pl.multiple_of(v * halves[m], 128), halves[m])]
+            return i, v, src
+
+        def remote_piece(t, m=m):
+            i, v, src = pieces(t, m)
+            return pltpu.make_async_remote_copy(
+                src,
+                ub.at[:, pl.ds(offs[m], halves[m])],
+                usend.at[t],
+                urecv.at[m],
+                device_id=(i, v),
+                device_id_type=MESH,
+            )
+
+        def local_piece(t, m=m):
+            i, v, src = pieces(t, m)
+            return pltpu.make_async_copy(src, ub.at[:, pl.ds(offs[m], halves[m])], urecv.at[m])
+
+        owner_flat = OWNERS[m] * wa_count
+
+        @pl.when(me == owner_flat)
+        def _(m=m, owner_flat=owner_flat, remote_piece=remote_piece, local_piece=local_piece):
+            def send(t, carry):
+                remote_piece(lax.rem(owner_flat + t, n_dev)).start()
+                return carry
+
+            local_piece(owner_flat).start()
+            lax.fori_loop(1, n_dev, send, 0)
+
+    for m in range(MATRIX_COUNT):
+        piece = ub.at[:, pl.ds(offs[m], halves[m])]
+        pltpu.make_async_copy(piece, piece, urecv.at[m]).wait()
+    for t in range(cols // TILE):
+        cs = slice(t * TILE, (t + 1) * TILE)
+        upd_ref[:, cs] = ub[:, cs][:rows].astype(F32)
+
+    for ci in range(len(chunks)):
+        for k in range(1, n_in):
+            plane_copy(ci, k).wait_send()
+        for k in range(1, n_out):
+            line_copy(ci, k).wait_send()
+    for m in range(MATRIX_COUNT):
+
+        @pl.when(me != OWNERS[m] * wa_count)
+        def _(m=m):
+            gather_remote(m).wait_send()
+
+        owner_flat = OWNERS[m] * wa_count
+
+        @pl.when(me == owner_flat)
+        def _(m=m, owner_flat=owner_flat):
+            def done(t, carry):
+                o = lax.rem(owner_flat + t, n_dev)
+                i, v = lax.div(o, wa_count), lax.rem(o, wa_count)
+                pltpu.make_async_remote_copy(
+                    ob.at[i, :, pl.ds(pl.multiple_of(v * halves[m], 128), halves[m])],
+                    ub.at[:, pl.ds(offs[m], halves[m])],
+                    usend.at[o],
+                    urecv.at[m],
+                    device_id=(i, v),
+                    device_id_type=MESH,
+                ).wait_send()
+                return carry
+
+            lax.fori_loop(1, n_dev, done, 0)
+
+
+def run_tail(grads, moments, ctx_count, wa_count):
+    n_in = IN_COUNT
+    n_out = ctx_count // n_in
+    rows = D // ctx_count
+    rp = -(-rows // 16) * 16
+    cols = layout(wa_count)[2]
+    n_ch = len(CHUNK_SETS)
+    n_dev = ctx_count * wa_count
+    square = lambda dt: pltpu.VMEM((D, D), dt)
+    dma = pltpu.SemaphoreType.DMA
+    shard = jax.ShapeDtypeStruct((rows, cols), F32)
+    in_vmem = pl.BlockSpec(memory_space=pltpu.VMEM)
+    return pl.pallas_call(
+        partial(tail_kernel, ctx_count, wa_count),
+        out_shape=(shard, shard, shard),
+        in_specs=[pl.BlockSpec(memory_space=pl.ANY), in_vmem],
+        out_specs=(in_vmem, in_vmem, in_vmem),
+        scratch_shapes=[
+            pltpu.VMEM((D // n_in, cols), BF),
+            pltpu.VMEM((n_in - 1, D // n_in, cols), BF),
+            pltpu.VMEM((n_out, rows, cols), F32),
+            pltpu.VMEM((n_out, rp, cols), BF),
+            pltpu.VMEM((n_out - 1, rp, cols), BF),
+            pltpu.VMEM((rp, cols), BF),
+            pltpu.VMEM((ctx_count, rp, FF), BF),
+            pltpu.VMEM((D, TILE), F32),
+            pltpu.VMEM((D, FF), BF),
+            pltpu.VMEM((ctx_count, rp, FF), BF),
+            pltpu.VMEM((rp, cols), BF),
+            square(F32),
+            square(BF),
+            square(BF),
+            square(BF),
+            square(BF),
+            square(BF),
+            square(BF),
+            dma((n_ch,)),
+            dma((n_ch, n_in - 1)),
+            dma((n_ch, n_in - 1)),
+            dma((n_ch, n_out - 1)),
+            dma((n_ch, n_out - 1)),
+            dma((MATRIX_COUNT,)),
+            dma,
+            dma((n_dev,)),
+            dma((MATRIX_COUNT,)),
+        ],
+        compiler_params=pltpu.CompilerParams(
+            collective_id=0, has_side_effects=True, vmem_limit_bytes=60 << 20
+        ),
+        name="tail",
+    )(grads, moments)
 
 
 def per_device(
@@ -369,84 +733,53 @@
     d_tokens, d_gain0 = pre_attn_pull(d_normed)
     input_grad = d_hidden + d_tokens
     grad_gains = jnp.stack([d_gain0, d_gain1, d_gain2, d_gain3])
-    sum_query, sum_keyval, sum_out, sum_gateup, sum_down, sum_gains = (
-        lax.psum_scatter(grad_query, "ctx", scatter_dimension=0, tiled=True),
-        lax.psum_scatter(grad_keyval, "ctx", scatter_dimension=1, tiled=True),
-        lax.psum_scatter(grad_out, "ctx", scatter_dimension=1, tiled=True),
-        lax.psum_scatter(grad_gateup, "ctx", scatter_dimension=1, tiled=True),
-        lax.psum_scatter(grad_down, "ctx", scatter_dimension=1, tiled=True),
-        lax.psum_scatter(grad_gains, "ctx", scatter_dimension=1, tiled=True),
-    )
-    new_mom_query = MOMENTUM * mom_query + sum_query
-    new_mom_keyval = MOMENTUM * mom_keyval + sum_keyval
-    new_mom_out = MOMENTUM * mom_out + sum_out
-    new_mom_gateup = MOMENTUM * mom_gateup + sum_gateup
-    new_mom_down = MOMENTUM * mom_down + sum_down
+    stack = jnp.concatenate(
+        [
+            grad_down.T,
+            grad_gateup[0],
+            grad_gateup[1],
+            grad_out.T,
+            grad_query,
+            grad_keyval[0],
+            grad_keyval[1],
+        ],
+        axis=1,
+    ).astype(jnp.bfloat16)
+    cols = stack.shape[1]
+    rows = D // ctx_count
+    stack = (
+        stack.reshape(ctx_count // IN_COUNT, IN_COUNT, rows, cols)
+        .transpose(1, 0, 2, 3)
+        .reshape(IN_COUNT, D // IN_COUNT, cols)
+    )
+    moments = jnp.concatenate(
+        [
+            mom_down.T,
+            mom_gateup[0],
+            mom_gateup[1],
+            mom_out.T,
+            mom_query,
+            mom_keyval[0],
+            mom_keyval[1],
+        ],
+        axis=1,
+    )
+    sums, fresh, updates = run_tail(stack, moments, ctx_count, wa_count)
+    halves, offs, _ = layout(wa_count)
+
+    def unstack(flat):
+        down, gate, up, out, query, key, value = [
+            flat[:, o : o + h] for o, h in zip(offs, halves)
+        ]
+        return (query, jnp.stack([key, value]), out.T, jnp.stack([gate, up]), down.T)
+
+    sum_query, sum_keyval, sum_out, sum_gateup, sum_down = unstack(sums)
+    new_mom_query, new_mom_keyval, new_mom_out, new_mom_gateup, new_mom_down = unstack(fresh)
+    upd_query, upd_keyval, upd_out, upd_gateup, upd_down = unstack(updates)
+    sum_gains = lax.psum_scatter(grad_gains, "ctx", scatter_dimension=1, tiled=True)
     new_gain_first = ADAM_ONE * gain_first + (1.0 - ADAM_ONE) * sum_gains
     new_gain_second = ADAM_TWO * gain_second + (1.0 - ADAM_TWO) * sum_gains * sum_gains
     gain_update = -GAIN_RATE * new_gain_first / (jnp.sqrt(new_gain_second) + ADAM_EPS)
-    dev_count = ctx_count * wa_count
-    me_flat = ctx_index * wa_count + wa_index
-    shards = [
-        new_mom_query,
-        new_mom_keyval[0],
-        new_mom_keyval[1],
-        new_mom_out,
-        new_mom_gateup[0],
-        new_mom_gateup[1],
-        new_mom_down,
-    ]
-    ctx_dims = [0, 0, 0, 1, 0, 0, 1]
-    full_shapes = [(D, HQ), (D, HD), (D, HD), (HQ, D), (D, FF), (D, FF), (FF, D)]
-    elem_counts = [part_mat.shape[0] * part_mat.shape[1] for part_mat in shards]
-    owners = [
-        mat_idx * ctx_count // MATRIX_COUNT * wa_count + mat_idx % wa_count
-        for mat_idx in range(MATRIX_COUNT)
-    ]
-    own_index = jnp.int32(MATRIX_COUNT)
-    for mat_idx in range(MATRIX_COUNT):
-        own_index = jnp.where(me_flat == owners[mat_idx], mat_idx, own_index)
-    flat_parts = [part_mat.reshape(1, -1) for part_mat in shards]
-    gathered = (
-        lax.all_gather(flat_parts[0], ("ctx", "wa"), axis=0, tiled=True),
-        lax.all_gather(flat_parts[1], ("ctx", "wa"), axis=0, tiled=True),
-        lax.all_gather(flat_parts[2], ("ctx", "wa"), axis=0, tiled=True),
-        lax.all_gather(flat_parts[3], ("ctx", "wa"), axis=0, tiled=True),
-        lax.all_gather(flat_parts[4], ("ctx", "wa"), axis=0, tiled=True),
-        lax.all_gather(flat_parts[5], ("ctx", "wa"), axis=0, tiled=True),
-        lax.all_gather(flat_parts[6], ("ctx", "wa"), axis=0, tiled=True),
-    )
-    offsets = [sum(elem_counts[:mat_idx]) for mat_idx in range(MATRIX_COUNT)]
-    total_cols = sum(elem_counts)
-    branches = [
-        partial(
-            owner_tiles,
-            mat_idx=mat_idx,
-            ctx_dim=ctx_dims[mat_idx],
-            row_count=full_shapes[mat_idx][0],
-            col_count=full_shapes[mat_idx][1],
-            ctx_count=ctx_count,
-            wa_count=wa_count,
-            offset=offsets[mat_idx],
-            total_cols=total_cols,
-            from_slots=False,
-        )
-        for mat_idx in range(MATRIX_COUNT)
-    ]
-    branches.append(partial(empty_tiles, dev_count=dev_count, total_cols=total_cols))
-    back_tiles = lax.switch(own_index, branches, gathered)
-    own_row = lax.psum_scatter(back_tiles, ("ctx", "wa"), scatter_dimension=0, tiled=True)
-    upd_parts = [
-        own_row[0, offsets[mat_idx] : offsets[mat_idx] + elem_counts[mat_idx]].reshape(
-            shards[mat_idx].shape
-        )
-        for mat_idx in range(MATRIX_COUNT)
-    ]
-    upd_query = upd_parts[0]
-    upd_keyval = jnp.stack([upd_parts[1], upd_parts[2]])
-    upd_out = upd_parts[3]
-    upd_gateup = jnp.stack([upd_parts[4], upd_parts[5]])
-    upd_down = upd_parts[6]
     return (
         block_out,
         input_grad,

time: 1830 us -> 590 us (0.32)
  the two profiles are of different devices: /device:TPU:15 before, /device:TPU:0 now
where the time goes in v1:
time: 590 us; the launch traced here: 584 us
  Pallas kernels  150 us (25%)
  matrix products  122 us (21%)
  blocking collectives  88.6 us (15%)
  local copies, waits for them, and re-layouts  74.1 us (13%)
  waiting for transfers between devices  57.8 us (10%)
  other arithmetic  56.3 us (10%)
  starting transfers between devices  20.2 us (3%)
  between operations  16 us (3%)
    pallas_call x1, Pallas kernels, run_tail(): pl.pallas_call(partial(tail_kernel, ctx_count, wa_count), out_shape=(shar...  150 us
    unnamed x1, blocking collectives  88.6 us
    unnamed x144, local copies, waits for them, and re-layouts  28.8 us
    psum x1, waiting for transfers between devices, per_device(): attn_proj = lax.psum(attn_part, 'wa')  21.9 us
    dot_general x2, matrix products, per_device(): jnp.einsum('hbs,sd->bhd', d_raw, key_blk, preferred_element_type=jnp.floa...  21.7 us
    ppermute x6, starting transfers between devices, shifted(): return lax.ppermute(block, axis, route)  19.2 us
    dot_general x2, matrix products, per_device(): jnp.einsum('hbs,bhd->sd', d_raw, query_blk, preferred_element_type=jnp.fl...  18.7 us
    psum x1, waiting for transfers between devices, per_device(): down_proj = lax.psum(down_part, 'wa')  18.6 us
  transfers between devices with their start and end apart: 11, of which 4 were waited for; matrix products, arithmetic and copies ran while one was open for 23% of the time, Pallas kernels for 0%

profile of v1, /device:TPU:0, one launch (start us, length us, event | category | flops | bytes accessed | tf_op | source)
XLA Modules:
  0.0 584.1 jit_solution(12835942632244236401)
XLA Ops:
  7.3 5.1 collective-permute-start.2
  21.2 4.3 collective-permute-start
  53.0 3.7 fusion.98
  68.4 21.9 %all-reduce.10.cloned.1.call-done = f32[1024,640]{1,0:T(8,128)} async-done(((f32[1024,640]{1,0:T(8,128)}), f32[1024,640]{1,0:T(8,128)}) %all-reduce.10.cloned.1.call-update) | async-done | bytes 2621456 | tf_op jit(solution)/shard_map/psum | solution.py:621
  95.0 3.5 convolution_bitcast_fusion
  101.7 4.2 fusion.49
  110.8 18.6 %all-reduce.12.cloned.1.call-done = f32[1024,640]{1,0:T(8,128)} async-done(((f32[1024,640]{1,0:T(8,128)}), f32[1024,640]{1,0:T(8,128)}) %all-reduce.12.cloned.1.call-update) | async-done | bytes 2621456 | tf_op jit(solution)/shard_map/psum | solution.py:627
  131.6 4.2 fusion.38
  137.9 7.4 %fusion.69 = (bf16[1,1024,1024]{2,1,0:T(8,128)(2,1)S(1)}, bf16[1,1024,1024]{2,1,0:T(8,128)(2,1)S(1)}) fusion(f32[2,1024,1024]{2,1,0:T(8,128)} %copy-done.63, bf16[1024,640]{1,0:T(8,128)(2,1)S(1)} %get-tuple-element.102, bf16[1024,640]{1,0:T(8,128)(2,1)S(1)} %copy-done.62), kind=kOutput, calls=%fused_computation.126 | convolution fusion | flops 1367343104 | bytes 15204352 | tf_op jit(solution)/shard_map/dot_general | solution.py:635
  147.3 4.9 fusion.70
  169.4 7.2 %convert_bitcast_fusion = bf16[2,640,1024]{2,1,0:T(8,128)(2,1)} fusion(bf16[1,1024,1024]{2,1,0:T(8,128)(2,1)} %copy-done.65, bf16[1,1024,1024]{2,1,0:T(8,128)(2,1)} %copy-done.64, f32[1024,640]{1,0:T(8,128)S(1)} %copy-done.6, f32[640]{0:T(1024)S(1)} %copy-done.44, f32[1024]{0:T(1024)S(1)} %fusion.156), kind=kOutput, calls=%fused_computation.88 | convolution fusion | flops 2689728512 | bytes 9443840 | tf_op jit(solution)/shard_map/td,gtf->gdf/dot_general | solution.py:639
  176.6 6.5 %fusion.78 = bf16[4,4,40,4352]{3,2,1,0:T(8,128)(2,1)} fusion(bf16[4,4,40,1024]{3,2,1,0:T(8,128)(2,1)S(1)} %bitcast.386, f32[2,1024,1024]{2,1,0:T(8,128)} %copy-done.63), kind=kOutput, calls=%fused_computation.133 | convolution fusion | flops 1353318400 | bytes 11010048 | tf_op jit(solution)/shard_map/dot_general | solution.py:634
  199.5 3.7 fusion.147
  203.2 9.2 %fusion.90 = f32[1024,256]{0,1:T(8,128)} fusion(f32[1024,512,2]{1,0,2:T(8,128)} %fusion.147, f32[1024,512,2]{1,0,2:T(8,128)} %copy-done.19, f32[2,512]{1,0:T(2,128)S(1)} %log_add_fusion.1, pred[512,1024]{0,1:T(8,128)(4,1)S(1)} %copy-done.24, bf16[1024,2,256]{2,0,1:T(8,128)(2,1)S(1)} %copy-done.29), kind=kOutput, calls=%fused_computation.140 | convolution fusion | flops 552601600 | bytes 19406848 | tf_op jit(solution)/shard_map/hbs,bhd->sd/dot_general | solution.py:688
  215.0 3.8 fusion.128
  222.2 8.3 %collective-permute-done.4 = bf16[1024,256]{0,1:T(8,128)(2,1)} collective-permute-done((bf16[1024,256]{0,1:T(8,128)(2,1)S(1)}, bf16[1024,256]{0,1:T(8,128)(2,1)}, u32[]{:S(2)}, u32[]{:S(2)}) %collective-permute-start.4) | collective-permute-done | bytes 524320 | tf_op jit(solution)/shard_map/ppermute | solution.py:39
  230.5 9.5 %add_convert_fusion.3 = bf16[1024,256]{0,1:T(8,128)(2,1)} fusion(bf16[1024,256]{0,1:T(8,128)(2,1)} %collective-permute-done.4, f32[1024,512,2]{1,0,2:T(8,128)} %fusion.128, f32[1024,512,2]{1,0,2:T(8,128)} %copy-done.17, f32[2,512]{1,0:T(2,128)S(1)} %log_add_fusion, pred[512,1024]{0,1:T(8,128)(4,1)S(1)} %copy-done.22, f32[1024,256]{0,1:T(8,128)} %fusion.90, ...), kind=kOutput, calls=%fused_computation.162 | convolution fusion | flops 553650176 | bytes 20455424 | tf_op jit(solution)/shard_map/hbs,bhd->sd/dot_general | solution.py:688
  240.3 10.7 %fusion.87 = f32[512,2,256]{2,0,1:T(8,128)} fusion(f32[1024,512,2]{1,0,2:T(8,128)} %fusion.128, f32[1024,512,2]{1,0,2:T(8,128)} %copy-done.17, f32[2,512]{1,0:T(2,128)S(1)} %log_add_fusion, pred[512,1024]{0,1:T(8,128)(4,1)S(1)} %copy-done.22, bf16[1024,128]{0,1:T(8,128)(2,1)S(1)} %copy-done.34, bf16[1024,128]{0,1:T(8,128)(2,1)S(1)} %get-tuple-element.112), kind=kOutput, calls=%fused_computation.137 | convolution fusion | flops 553650176 | bytes 10489856 | tf_op jit(solution)/shard_map/hbs,sd->bhd/dot_general | solution.py:686
  251.1 10.9 %fusion.89 = f32[512,2,256]{2,0,1:T(8,128)} fusion(f32[1024,512,2]{1,0,2:T(8,128)} %fusion.147, f32[1024,512,2]{1,0,2:T(8,128)} %copy-done.19, f32[2,512]{1,0:T(2,128)S(1)} %log_add_fusion.1, pred[512,1024]{0,1:T(8,128)(4,1)S(1)} %copy-done.24, bf16[1024,256]{0,1:T(8,128)(2,1)} %collective-permute-done.3, bf16[1024,128]{0,1:T(8,128)(2,1)S(1)} %copy-done.34, ...), kind=kOutput, calls=%fused_computation.139 | convolution fusion | flops 554174464 | bytes 11014144 | tf_op jit(solution)/shard_map/hbs,sd->bhd/dot_general | solution.py:686
  290.6 8.8 %all-reduce.16.cloned.1.call-done = bf16[1024,640]{1,0:T(8,128)(2,1)} async-done(((bf16[1024,640]{1,0:T(8,128)(2,1)}), bf16[1024,640]{1,0:T(8,128)(2,1)}) %all-reduce.16.cloned.1.call-update) | async-done | bytes 1310736 | tf_op jit(solution)/shard_map/psum | solution.py:731
  302.5 4.6 fusion.228
  313.2 5.4 copy.121
  318.6 149.7 %tail.1 = (f32[40,4352]{1,0:T(8,128)}, f32[40,4352]{1,0:T(8,128)}, f32[40,4352]{1,0:T(8,128)}) custom-call(bf16[4,160,4352]{2,1,0:T(8,128)(2,1)} %bitcast.368, f32[40,4352]{1,0:T(8,128)} %constant_dynamic-update-slice_fusion.4.mom_ref), custom_call_target="tpu_custom_call" | custom-call | tf_op jit(solution)/shard_map/tail/pallas_call | solution.py:503
  481.3 88.6 %all-reduce.2 = f32[4,640]{1,0:T(4,128)} all-reduce(f32[4,640]{1,0:T(4,128)S(1)} %pad_maximum_fusion.19), channel_id=2, replica_groups=mesh['ctx'=16,'wa'=2] {'ctx'}, use_global_device_ids=true, to_apply=%region_24.25.clone | all-reduce | flops 2560 | bytes 20480
  (259 shorter events, 163.4 us)
Async XLA Ops:
  7.2 87.7 %copy-start = (bf16[2,640,1024]{2,1,0:T(8,128)(2,1)S(1)}, bf16[2,640,1024]{2,1,0:T(8,128)(2,1)}, u32[]{:S(2)}) copy-start(bf16[2,640,1024]{2,1,0:T(8,128)(2,1)} %param.30) | copy-start | bytes 7864324
  7.2 18.3 %copy-start.39 = (bf16[2,640,256]{2,1,0:T(8,128)(2,1)S(1)}, bf16[2,640,256]{2,1,0:T(8,128)(2,1)}, u32[]{:S(2)}) copy-start(bf16[2,640,256]{2,1,0:T(8,128)(2,1)} %param.28) | copy-start | bytes 1966084
  7.2 83.1 %all-reduce.10.cloned.1.call-start = ((), (), s32[]{:S(2)}) async-start(), calls=%async_computation | async-start | bytes 5242880 | tf_op jit(solution)/shard_map/psum | solution.py:621
  7.3 18.3 %copy-start.11 = (bf16[1024,640]{1,0:T(8,128)(2,1)S(1)}, bf16[1024,640]{1,0:T(8,128)(2,1)}, u32[]{:S(2)}) copy-start(bf16[1024,640]{1,0:T(8,128)(2,1)} %param.24) | copy-start | bytes 3932164
  7.3 49.5 %collective-permute-start.2 = (s32[1024]{0:T(1024)S(1)}, s32[1024]{0:T(1024)S(1)}, u32[]{:S(2)}, u32[]{:S(2)}) collective-permute-start(s32[1024]{0:T(1024)S(1)} %iota_add_fusion), channel_id=1, source_target_pairs={{0,2},{2,4},{4,6},{6,8},{8,10},{10,12},{12,14},{14,16},{16,18},{18... | collective-permute-start | bytes 12296 | tf_op jit(solution)/shard_map/ppermute | solution.py:39
  12.4 44.3 %collective-permute-start.1 = (s32[1024]{0:T(1024)}, s32[1024]{0:T(1024)S(1)}, u32[]{:S(2)}, u32[]{:S(2)}) collective-permute-start(s32[1024]{0:T(1024)} %param.26), channel_id=1, source_target_pairs={{0,2},{2,4},{4,6},{6,8},{8,10},{10,12},{12,14},{14,16},{16,18},{18... | collective-permute-start | bytes 12296 | tf_op jit(solution)/shard_map/ppermute | solution.py:39
  18.4 76.6 %copy-start.43 = (f32[640]{0:T(1024)}, f32[640]{0:T(1024)S(1)}, u32[]{:S(2)}) copy-start(f32[640]{0:T(1024)S(1)} %get-tuple-element.86) | copy-start | bytes 7684
  21.2 40.5 %collective-permute-start = (bf16[1024,256]{1,0:T(8,128)(2,1)}, bf16[1024,256]{1,0:T(8,128)(2,1)}, u32[]{:S(2)}, u32[]{:S(2)}) collective-permute-start(bf16[1024,256]{1,0:T(8,128)(2,1)} %convolution_convert_fusion.3), channel_id=1, source_target_pairs={{0,2},{2,4},{4,6},{6,8},{8,10},{10,12},{12,14},{14,16},{16,18},{18... | collective-permute-start | bytes 1572872 | tf_op jit(solution)/shard_map/ppermute | solution.py:39
  30.4 27.3 %collective-permute-start.3 = (bf16[1024,256]{0,1:T(8,128)(2,1)}, bf16[1024,256]{0,1:T(8,128)(2,1)}, u32[]{:S(2)}, u32[]{:S(2)}) collective-permute-start(bf16[1024,256]{0,1:T(8,128)(2,1)} %pad_maximum_fusion.12), channel_id=1, source_target_pairs={{0,2},{2,4},{4,6},{6,8},{8,10},{10,12},{12,14},{14,16},{16,18},{18... | collective-permute-start | bytes 1572872 | tf_op jit(solution)/shard_map/ppermute | solution.py:39
  68.2 61.3 %all-reduce.12.cloned.1.call-start = ((), (), s32[]{:S(2)}) async-start(), calls=%async_computation.1 | async-start | bytes 5242880 | tf_op jit(solution)/shard_map/psum | solution.py:627
  105.9 77.2 %all-reduce.14.cloned.1.call-start = ((), (), s32[]{:S(2)}) async-start(), calls=%async_computation.2 | async-start | bytes 5242880 | tf_op jit(solution)/shard_map/psum | solution.py:645
  152.3 17.1 %copy-start.6 = (f32[1024,640]{1,0:T(8,128)S(1)}, f32[1024,640]{1,0:T(8,128)}, u32[]{:S(2)}) copy-start(f32[1024,640]{1,0:T(8,128)} %copy-done.4) | copy-start | bytes 7864324
  152.3 117.8 %all-reduce.18.cloned.1.call-start = ((), (), s32[]{:S(2)}) async-start(), calls=%async_computation.4 | async-start | bytes 2097152 | tf_op jit(solution)/shard_map/psum | solution.py:701
  153.4 16.0 %copy-start.44 = (f32[640]{0:T(1024)S(1)}, f32[640]{0:T(1024)}, u32[]{:S(2)}) copy-start(f32[640]{0:T(1024)} %copy-done.43) | copy-start | bytes 7684
  198.0 20.8 %collective-permute-start.5 = (bf16[1024,256]{1,0:T(8,128)(2,1)}, bf16[1024,256]{1,0:T(8,128)(2,1)}, u32[]{:S(2)}, u32[]{:S(2)}) collective-permute-start(bf16[1024,256]{1,0:T(8,128)(2,1)} %pad_convert_fusion), channel_id=1, source_target_pairs={{2,0},{4,2},{6,4},{8,6},{10,8},{12,10},{14,12},{16,14},{18,16},{20... | collective-permute-start | bytes 1572872 | tf_op jit(solution)/shard_map/ppermute | solution.py:39
  213.6 16.9 %collective-permute-start.4 = (bf16[1024,256]{0,1:T(8,128)(2,1)S(1)}, bf16[1024,256]{0,1:T(8,128)(2,1)}, u32[]{:S(2)}, u32[]{:S(2)}) collective-permute-start(bf16[1024,256]{0,1:T(8,128)(2,1)S(1)} %pad_convert_fusion.1), channel_id=1, source_target_pairs={{2,0},{4,2},{6,4},{8,6},{10,8},{12,10},{14,12},{16,14},{18,16},{20... | collective-permute-start | bytes 1572872 | tf_op jit(solution)/shard_map/ppermute | solution.py:39
  222.2 18.2 %copy-start.34 = (bf16[1024,128]{0,1:T(8,128)(2,1)S(1)}, bf16[1024,128]{0,1:T(8,128)(2,1)}, u32[]{:S(2)}) copy-start(bf16[1024,128]{0,1:T(8,128)(2,1)} %copy-done.32) | copy-start | bytes 786436
  240.0 59.4 %all-reduce.16.cloned.1.call-start = ((), (), s32[]{:S(2)}) async-start(), calls=%async_computation.3 | async-start | bytes 2621440 | tf_op jit(solution)/shard_map/psum | solution.py:731
  287.5 15.0 %copy-start.46 = (f32[1024]{0:T(1024)S(1)}, f32[1024]{0:T(1024)}, u32[]{:S(2)}) copy-start(f32[1024]{0:T(1024)} %copy-done.45) | copy-start | bytes 12292
  287.5 15.0 %copy-start.10 = (f32[1024,640]{1,0:T(8,128)S(1)}, f32[1024,640]{1,0:T(8,128)}, u32[]{:S(2)}) copy-start(f32[1024,640]{1,0:T(8,128)} %copy-done.9) | copy-start | bytes 7864324
  318.5 162.8 %copy-start.56 = (f32[1,640]{1,0:T(1,128)S(1)}, f32[1,640]{1,0:T(1,128)}, u32[]{:S(2)}) copy-start(f32[1,640]{1,0:T(1,128)} %reshape.470) | copy-start | bytes 7684
  318.5 162.8 %copy-start.57 = (f32[1,640]{1,0:T(1,128)S(1)}, f32[1,640]{1,0:T(1,128)}, u32[]{:S(2)}) copy-start(f32[1,640]{1,0:T(1,128)} %reshape.469) | copy-start | bytes 7684
  318.5 162.8 %copy-start.58 = (f32[1,640]{1,0:T(1,128)S(1)}, f32[1,640]{1,0:T(1,128)}, u32[]{:S(2)}) copy-start(f32[1,640]{1,0:T(1,128)} %reshape.468) | copy-start | bytes 7684
  318.5 258.5 %copy-start.1 = (bf16[2,640,1024]{2,1,0:T(8,128)(2,1)S(1)}, bf16[2,640,1024]{2,1,0:T(8,128)(2,1)}, u32[]{:S(2)}) copy-start(bf16[2,640,1024]{2,1,0:T(8,128)(2,1)} %param.30) | copy-start | bytes 7864324
  (53 other events, 252.0 us)
Sparse Core Ops, SparseCore 0:
  68.3 21.9 all-reduce.9
  106.1 23.3 all-reduce.11
  152.4 23.3 all-reduce.13
  240.2 21.9 all-reduce.17
  277.1 22.3 all-reduce.15

commit v2 on v1

--- a/solution.py
+++ b/solution.py
@@ -3,6 +3,7 @@
 
 import jax
 import jax.numpy as jnp
+import numpy as np
 from jax import lax
 from jax.experimental import pallas as pl
 from jax.experimental.pallas import tpu as pltpu
@@ -20,7 +21,6 @@
 EPS_NORM = 1e-06
 ROPE_BASE = 10000.0
 MOMENTUM = 0.95
-MUON_RATE = 0.2
 ADAM_ONE = 0.9
 ADAM_TWO = 0.95
 ADAM_EPS = 1e-08
@@ -28,88 +28,8 @@
 QUINTIC_A = 3.4445
 QUINTIC_B = -4.775
 QUINTIC_C = 2.0315
-MASK_FILL = -1e30
-HIGHEST_PREC = lax.Precision.HIGHEST
 MATRIX_COUNT = 7
-
-
-def shifted(block, axis, distance):
-    devices = range(lax.axis_size(axis))
-    route = [(i - distance, i) for i in devices if i - distance in devices]
-    return lax.ppermute(block, axis, route)
-
-
-def rms_scale(activation, gain_row):
-    return (
-        activation
-        * lax.rsqrt(jnp.mean(activation * activation, axis=-1, keepdims=True) + EPS_NORM)
-        * (1.0 + gain_row)
-    )
-
-
-def geglu(gate_pre, up_proj):
-    return jax.nn.gelu(gate_pre, approximate=True) * up_proj
-
-
-def inverse_freq():
-    return jnp.power(ROPE_BASE, -2.0 * jnp.arange(HD // 2, dtype=jnp.float32) / HD)
-
-
-def angle_tables(vectors, angles):
-    cosine_tab = jnp.cos(angles)
-    sine_tab = jnp.sin(angles)
-    if vectors.ndim == 3:
-        cosine_tab = cosine_tab[:, None, :]
-        sine_tab = sine_tab[:, None, :]
-    return (cosine_tab, sine_tab)
-
-
-def rotate(vectors, angles):
-    half_dim = vectors.shape[-1] // 2
-    cosine_tab, sine_tab = angle_tables(vectors, angles)
-    left_part = vectors[..., :half_dim]
-    right_part = vectors[..., half_dim:]
-    return jnp.concatenate(
-        [
-            left_part * cosine_tab - right_part * sine_tab,
-            right_part * cosine_tab + left_part * sine_tab,
-        ],
-        axis=-1,
-    )
-
-
-def rotate_back(grads_rot, angles):
-    half_dim = grads_rot.shape[-1] // 2
-    cosine_tab, sine_tab = angle_tables(grads_rot, angles)
-    left_part = grads_rot[..., :half_dim]
-    right_part = grads_rot[..., half_dim:]
-    return jnp.concatenate(
-        [
-            left_part * cosine_tab + right_part * sine_tab,
-            right_part * cosine_tab - left_part * sine_tab,
-        ],
-        axis=-1,
-    )
-
-
-def local_positions(seq_ids, ctx_index):
-    tok_count = seq_ids.shape[0]
-    begin_at = ctx_index * tok_count
-    return begin_at + jnp.arange(tok_count, dtype=jnp.int32)
-
-
-def block_scores(query_blk, key_blk, query_pos, query_ids, key_pos, key_ids):
-    raw_scores = jnp.einsum("bhd,sd->hbs", query_blk, key_blk, preferred_element_type=jnp.float32)
-    tanh_cap = jnp.tanh(raw_scores / SOFT_CAP)
-    pos_gap = query_pos[:, None] - key_pos[None, :]
-    allowed = (query_ids[:, None] == key_ids[None, :]) & (pos_gap >= 0) & (pos_gap < WINDOW)
-    masked = jnp.where(allowed[None], SOFT_CAP * tanh_cap, MASK_FILL)
-    return (masked, tanh_cap)
-
-
-def take_block(array_in, along_dim, block_index, block_size):
-    return lax.dynamic_slice_in_dim(array_in, block_index * block_size, block_size, along_dim)
-
+MUON_RATE = 0.2
 
 MESH = pl.DeviceIdType.MESH
 BF = jnp.bfloat16
@@ -159,9 +79,11 @@
     wa_count,
     g_ref,
     mom_ref,
+    dg_ref,
     sum_ref,
     nm_ref,
     upd_ref,
+    gs_ref,
     own,
     pr,
     s3,
@@ -189,6 +111,10 @@
     grecv,
     usend,
     urecv,
+    dgs,
+    dgr,
+    dsend,
+    drecv,
 ):
     c = lax.axis_index("ctx")
     w = lax.axis_index("wa")
@@ -270,6 +196,26 @@
         for k in range(1, n_in):
             plane_copy(ci, k).start()
 
+    for i in range(ctx_count):
+        dgs[i, :, 0:rows] = dg_ref[:, i * rows : (i + 1) * rows]
+
+    def gain_copy(t):
+        i, v = lax.div(t, wa_count), lax.rem(t, wa_count)
+        return pltpu.make_async_remote_copy(
+            dgs.at[i], dgr.at[me], dsend.at[t], drecv, device_id=(i, v), device_id_type=MESH
+        )
+
+    def gain_send(t, carry):
+        gain_copy(lax.rem(me + t, n_dev)).start()
+        return carry
+
+    def gain_sent(t, carry):
+        gain_copy(lax.rem(me + t, n_dev)).wait_send()
+        return carry
+
+    pltpu.make_async_copy(dgs.at[c], dgr.at[me], drecv).start()
+    lax.fori_loop(1, n_dev, gain_send, 0)
+
     for ci, (off, wid) in enumerate(chunks):
         own_copy(ci).wait()
         for k in range(1, n_in):
@@ -317,6 +263,8 @@
             def _(m=m):
                 gather_remote(m).start()
 
+    pltpu.make_async_copy(dgr, dgr, drecv).wait()
+    gs_ref[...] = jnp.sum(dgr[...], axis=0)
     is_owner = me == OWNERS[0] * wa_count
     for m in range(1, MATRIX_COUNT):
         is_owner = jnp.logical_or(is_owner, me == OWNERS[m] * wa_count)
@@ -457,6 +405,7 @@
         cs = slice(t * TILE, (t + 1) * TILE)
         upd_ref[:, cs] = ub[:, cs][:rows].astype(F32)
 
+    lax.fori_loop(1, n_dev, gain_sent, 0)
     for ci in range(len(chunks)):
         for k in range(1, n_in):
             plane_copy(ci, k).wait_send()
@@ -488,7 +437,7 @@
             lax.fori_loop(1, n_dev, done, 0)
 
 
-def run_tail(grads, moments, ctx_count, wa_count):
+def run_tail(grads, moments, gain_grads, ctx_count, wa_count):
     n_in = IN_COUNT
     n_out = ctx_count // n_in
     rows = D // ctx_count
@@ -502,9 +451,9 @@
     in_vmem = pl.BlockSpec(memory_space=pltpu.VMEM)
     return pl.pallas_call(
         partial(tail_kernel, ctx_count, wa_count),
-        out_shape=(shard, shard, shard),
-        in_specs=[pl.BlockSpec(memory_space=pl.ANY), in_vmem],
-        out_specs=(in_vmem, in_vmem, in_vmem),
+        out_shape=(shard, shard, shard, jax.ShapeDtypeStruct((8, 128), F32)),
+        in_specs=[pl.BlockSpec(memory_space=pl.ANY), in_vmem, in_vmem],
+        out_specs=(in_vmem,) * 4,
         scratch_shapes=[
             pltpu.VMEM((D // n_in, cols), BF),
             pltpu.VMEM((n_in - 1, D // n_in, cols), BF),
@@ -533,12 +482,569 @@
             dma,
             dma((n_dev,)),
             dma((MATRIX_COUNT,)),
+            pltpu.VMEM((ctx_count, 8, 128), F32),
+            pltpu.VMEM((n_dev, 8, 128), F32),
+            dma((n_dev,)),
+            dma,
         ],
         compiler_params=pltpu.CompilerParams(
             collective_id=0, has_side_effects=True, vmem_limit_bytes=60 << 20
         ),
         name="tail",
-    )(grads, moments)
+    )(grads, moments, gain_grads)
+
+
+class Refs:
+    pass
+
+
+def dot_nt(a, b):
+    return lax.dot_general(a, b, (((1,), (1,)), ((), ())), preferred_element_type=F32)
+
+
+def dot_tn(a, b):
+    return lax.dot_general(a, b, (((0,), (0,)), ((), ())), preferred_element_type=F32)
+
+
+def aligned(start, size):
+    return pl.ds(pl.multiple_of(start, size), size)
+
+
+def norm_parts(v, gain):
+    r = lax.rsqrt(jnp.mean(v * v, axis=-1, keepdims=True) + EPS_NORM)
+    return r, v * r, 1.0 + gain
+
+
+def norm_back(v, gain, e):
+    r, zed, g1 = norm_parts(v, gain)
+    e1 = e * g1
+    dv = r * (e1 - zed * jnp.mean(e1 * zed, axis=-1, keepdims=True))
+    return dv, jnp.sum(e * zed, axis=0, keepdims=True)
+
+
+def layer_scratch(tok):
+    v = pltpu.VMEM
+    dma = pltpu.SemaphoreType.DMA
+    cols = sum(WIDTHS) // 2
+    heads = HQ // HD
+    tiles = tok // TILE
+    win = WINDOW + TILE
+    return dict(
+        wq=v((2, D, HQ // 2), BF),
+        wo=v((HQ, D), BF),
+        wg=v((2, D, FF // 2), BF),
+        wu=v((2, D, FF // 2), BF),
+        wd=v((FF, D), BF),
+        tk=v((tok, D), BF),
+        ct=v((tok, D), BF),
+        xa=v((tok, D), BF),
+        xat=v((D, tok), BF),
+        fit=v((D, tok), BF),
+        ddn=v((tok, D), BF),
+        ddnt=v((D, tok), BF),
+        cs=v((tok, HD // 2), F32),
+        sn=v((tok, HD // 2), F32),
+        ka=v((WINDOW + tok, HD), BF),
+        va=v((WINDOW + tok, HD), BF),
+        idown=v((8, tok), jnp.int32),
+        idprev=v((8, tok), jnp.int32),
+        qs=v((tiles * heads, TILE, HD), BF),
+        mk=v((tiles, TILE, win), BF),
+        ps=v((tiles * heads, TILE, win), F32),
+        ts=v((tiles * heads, TILE, win), BF),
+        att=v((tok, HQ), BF),
+        ao=v((tok, D), F32),
+        h1=v((tok, D), F32),
+        dn=v((tok, D), F32),
+        dh1=v((tok, D), F32),
+        yb=v((tok, D), BF),
+        hid=v((2, tok, FF // 2), BF),
+        a1=v((2, tok, FF // 2), BF),
+        a2=v((2, tok, FF // 2), BF),
+        datt=v((tok, HQ), BF),
+        dka=v((WINDOW + tok, HD), F32),
+        dva=v((WINDOW + tok, HD), F32),
+        dks=v((2, tok, HD), BF),
+        dkr=v((2, tok, HD), BF),
+        dkv=v((2, tok, HD), BF),
+        sb=v((IN_COUNT, D // IN_COUNT, cols), BF),
+        gb=v((IN_COUNT, D // IN_COUNT, cols), BF),
+        wsend=dma((5,)),
+        wrecv=dma((5,)),
+        wown=dma((5,)),
+        ksend=dma((3,)),
+        krecv=dma((3,)),
+        dsend=dma((2,)),
+        drecv=dma((2,)),
+        csend=dma((MATRIX_COUNT, 4)),
+        crecv=dma((MATRIX_COUNT, 4)),
+        osend=dma((2,)),
+        orecv=dma((2,)),
+        oown=dma((2,)),
+        tsem=dma((2,)),
+    )
+
+
+def layer_phases(s, ctx_count, wa_count):
+    c = lax.axis_index("ctx")
+    w = lax.axis_index("wa")
+    other = 1 - w
+    flat = c * wa_count + w
+    n_dev = ctx_count * wa_count
+    tok = s.xa.shape[0]
+    rows = D // ctx_count
+    n_out = ctx_count // IN_COUNT
+    heads = HQ // HD
+    tiles = tok // TILE
+    win = WINDOW + TILE
+    half_ff = FF // 2
+    halves, offs, cols = layout(wa_count)
+    step = 128
+    partner = (c, other)
+    follow = jnp.minimum(flat + 1, n_dev - 1)
+    ahead = jnp.maximum(flat - 1, 0)
+    next_id = (lax.div(follow, wa_count), lax.rem(follow, wa_count))
+    prev_id = (lax.div(ahead, wa_count), lax.rem(ahead, wa_count))
+    order = [zz * IN_COUNT + pp for pp in range(IN_COUNT) for zz in range(n_out)]
+
+    def remote(src, dst, send, recv, where):
+        return pltpu.make_async_remote_copy(
+            src, dst, send, recv, device_id=where, device_id_type=MESH
+        )
+
+    def permuted(v):
+        t = v.astype(BF).astype(F32).T
+        return jnp.concatenate([t[i * rows : (i + 1) * rows] for i in order], axis=0).astype(BF)
+
+    def per_rows(body):
+        def run(i, carry):
+            body(aligned(i * step, step))
+            return carry
+
+        lax.fori_loop(0, tok // step, run, 0)
+
+    out_rows = aligned(w * tok, tok)
+    tok_in = pltpu.make_async_copy(s.tok_ref.at[out_rows], s.tk, s.tsem.at[0])
+    cot_in = pltpu.make_async_copy(s.cot_ref.at[out_rows], s.ct, s.tsem.at[1])
+    tok_in.start()
+    cot_in.start()
+
+    wk_refs = (
+        (s.wq_ref, s.wq.at[w]),
+        (s.wo_ref, s.wo.at[aligned(w * (HQ // 2), HQ // 2)]),
+        (s.wgu_ref.at[0], s.wg.at[w]),
+        (s.wgu_ref.at[1], s.wu.at[w]),
+        (s.wd_ref, s.wd.at[aligned(w * half_ff, half_ff)]),
+    )
+    w_far = [remote(a, b, s.wsend.at[i], s.wrecv.at[i], partner) for i, (a, b) in enumerate(wk_refs)]
+    w_own = [pltpu.make_async_copy(a, b, s.wown.at[i]) for i, (a, b) in enumerate(wk_refs)]
+    for far, own in zip(w_far, w_own):
+        far.start()
+        own.start()
+
+    def weights_ready(i):
+        w_own[i].wait()
+        w_far[i].wait_recv()
+
+    tok_in.wait()
+
+    def first(rs):
+        x = s.tk[rs].astype(F32)
+        _, zed, g1 = norm_parts(x, s.gain_ref[0:1])
+        n = zed * g1
+        s.xa[rs] = n.astype(BF)
+        s.xat[:, rs] = permuted(n)
+
+    per_rows(first)
+
+    cb, sb_ = s.cosb_ref[pl.ds(flat, 1), :], s.sinb_ref[pl.ds(flat, 1), :]
+    s.cs[...] = cb * s.cosi_ref[...] - sb_ * s.sini_ref[...]
+    s.sn[...] = sb_ * s.cosi_ref[...] + cb * s.sini_ref[...]
+    hh = HD // 2
+
+    def turn(v, cosine, sine):
+        a, b = v[:, :hh], v[:, hh:]
+        return jnp.concatenate([a * cosine - b * sine, b * cosine + a * sine], axis=1)
+
+    def turn_back(v, cosine, sine):
+        a, b = v[:, :hh], v[:, hh:]
+        return jnp.concatenate([a * cosine + b * sine, b * cosine - a * sine], axis=1)
+
+    s.ka[WINDOW:, :] = turn(dot32(s.xa[...], s.wkv_ref[0]), s.cs[...], s.sn[...]).astype(BF)
+    s.va[WINDOW:, :] = dot32(s.xa[...], s.wkv_ref[1]).astype(BF)
+    s.idown[...] = jnp.broadcast_to(s.ids_ref[pl.ds(w, 1), :], (8, tok))
+
+    halo = [
+        remote(s.ka.at[pl.ds(tok, WINDOW)], s.ka.at[pl.ds(0, WINDOW)], s.ksend.at[0], s.krecv.at[0], next_id),
+        remote(s.va.at[pl.ds(tok, WINDOW)], s.va.at[pl.ds(0, WINDOW)], s.ksend.at[1], s.krecv.at[1], next_id),
+        remote(s.idown, s.idprev, s.ksend.at[2], s.krecv.at[2], next_id),
+    ]
+
+    @pl.when(flat < n_dev - 1)
+    def _():
+        for cp in halo:
+            cp.start()
+
+    weights_ready(0)
+
+    def project(h, carry):
+        v, u = lax.div(h, heads // 2), lax.rem(h, heads // 2)
+        q = dot32(s.xa[...], s.wq[v, :, aligned(u * HD, HD)])
+        q = (turn(q, s.cs[...], s.sn[...]) * HD ** (-0.5)).astype(BF)
+        for a in range(tiles):
+            s.qs[a * heads + h] = q[a * TILE : (a + 1) * TILE]
+        return carry
+
+    lax.fori_loop(0, heads, project, 0)
+
+    @pl.when(flat > 0)
+    def _():
+        for cp in halo:
+            cp.wait_recv()
+
+    @pl.when(flat == 0)
+    def _():
+        s.ka[0:WINDOW, :] = jnp.zeros((WINDOW, HD), BF)
+        s.va[0:WINDOW, :] = jnp.zeros((WINDOW, HD), BF)
+        s.idprev[...] = jnp.full((8, tok), -1, jnp.int32)
+
+    row_ids = jnp.concatenate([s.idprev[0:1, :], s.idown[0:1, :]], axis=1)
+    own_col = jnp.broadcast_to(s.idown[0:1, :], (128, tok)).T[:, 0:1]
+    gap = lax.broadcasted_iota(jnp.int32, (TILE, win), 1) - lax.broadcasted_iota(
+        jnp.int32, (TILE, win), 0
+    )
+    for a in range(tiles):
+        same = own_col[a * TILE : (a + 1) * TILE] == row_ids[:, a * TILE : a * TILE + win]
+        ok = jnp.logical_and(same, jnp.logical_and(gap > 0, gap <= WINDOW))
+        s.mk[a] = jnp.where(ok, 1.0, 0.0).astype(BF)
+
+    def attend(i, carry):
+        a, h = lax.div(i, heads), lax.rem(i, heads)
+        ks = pl.ds(pl.multiple_of(a * TILE, TILE), win)
+        t = jnp.tanh(dot_nt(s.qs[i], s.ka[ks, :]) * (1.0 / SOFT_CAP))
+        e = jnp.exp(SOFT_CAP * t) * s.mk[a].astype(F32)
+        pr = e * (1.0 / jnp.sum(e, axis=-1, keepdims=True))
+        s.ps[i] = pr
+        s.ts[i] = (1.0 - t * t).astype(BF)
+        o = dot32(pr.astype(BF), s.va[ks, :])
+        s.att[aligned(a * TILE, TILE), aligned(h * HD, HD)] = o.astype(BF)
+        return carry
+
+    lax.fori_loop(0, tiles * heads, attend, 0)
+
+    weights_ready(1)
+    s.ao[...] = dot32(s.att[...], s.wo[...])
+
+    def second(rs):
+        _, zed, g1 = norm_parts(s.ao[rs], s.gain_ref[1:2])
+        h = s.tk[rs].astype(F32) + zed * g1
+        s.h1[rs] = h
+        _, zed, g1 = norm_parts(h, s.gain_ref[2:3])
+        n = zed * g1
+        s.xa[rs] = n.astype(BF)
+        s.fit[:, rs] = permuted(n)
+
+    per_rows(second)
+
+    weights_ready(2)
+    weights_ready(3)
+    root = 0.7978845608028654
+
+    def forward(i, carry):
+        v, u = lax.div(i, 4), lax.rem(i, 4)
+        us = aligned(u * TILE, TILE)
+        gt = dot32(s.xa[...], s.wg[v, :, us])
+        up = dot32(s.xa[...], s.wu[v, :, us])
+        g2 = gt * gt
+        th = jnp.tanh(root * gt * (1.0 + 0.044715 * g2))
+        lift = 0.5 * (1.0 + th)
+        act = gt * lift
+        slope = lift + 0.5 * gt * (1.0 - th * th) * (root * (1.0 + 3.0 * 0.044715 * g2))
+        s.hid[v, :, us] = (act * up).astype(BF)
+        s.a1[v, :, us] = (up * slope).astype(BF)
+        s.a2[v, :, us] = act.astype(BF)
+        return carry
+
+    lax.fori_loop(0, 8, forward, 0)
+    weights_ready(4)
+    s.dn[...] = dot32(s.hid[0], s.wd[:half_ff]) + dot32(s.hid[1], s.wd[half_ff:])
+    s.dg_ref[...] = jnp.zeros_like(s.dg_ref)
+
+    def third(rs):
+        dn = s.dn[rs]
+        _, zed, g1 = norm_parts(dn, s.gain_ref[3:4])
+        s.yb[rs] = (s.h1[rs] + zed * g1).astype(BF)
+        dv, dg = norm_back(dn, s.gain_ref[3:4], s.ct[rs].astype(F32))
+        s.dg_ref[3:4] += dg
+        s.ddn[rs] = dv.astype(BF)
+        s.ddnt[:, rs] = permuted(dv)
+
+    cot_in.wait()
+    per_rows(third)
+    y_far = remote(s.yb, s.y_ref.at[out_rows], s.osend.at[0], s.orecv.at[0], partner)
+    y_own = pltpu.make_async_copy(s.yb, s.y_ref.at[out_rows], s.oown.at[0])
+    y_far.start()
+    y_own.start()
+
+    def part(m, u, width):
+        return pl.ds(pl.multiple_of(offs[m] + u * width, 128), width)
+
+    def exchange(m, u, width):
+        ps = part(m, u, width)
+        return remote(s.sb.at[:, :, ps], s.gb.at[:, :, ps], s.csend.at[m, u], s.crecv.at[m, u], partner)
+
+    def give(m, u, width, value):
+        s.sb[:, :, part(m, u, width)] = value.astype(BF).reshape(IN_COUNT, D // IN_COUNT, width)
+        exchange(m, u, width).start()
+
+    def keep(m, u, width, value):
+        ps = part(m, u, width)
+        exchange(m, u, width).wait_recv()
+        total = value.reshape(IN_COUNT, D // IN_COUNT, width) + s.gb[:, :, ps].astype(F32)
+        s.gb[:, :, ps] = total.astype(BF)
+
+    def ffn_back(v, put):
+        def run(u, carry):
+            us = aligned(u * TILE, TILE)
+            dh = dot_nt(s.ddn[...], s.wd[aligned((v * 4 + u) * TILE, TILE), :])
+            dgt = (dh * s.a1[v, :, us].astype(F32)).astype(BF)
+            dup = (dh * s.a2[v, :, us].astype(F32)).astype(BF)
+            s.a1[v, :, us] = dgt
+            s.a2[v, :, us] = dup
+            put(0, u, TILE, dot32(s.ddnt[...], s.hid[v, :, us]))
+            put(1, u, TILE, dot32(s.fit[...], dgt))
+            put(2, u, TILE, dot32(s.fit[...], dup))
+            return carry
+
+        lax.fori_loop(0, 4, run, 0)
+
+    ffn_back(other, give)
+    ffn_back(w, keep)
+    s.chunk_done(0)
+    s.chunk_done(1)
+    s.chunk_done(2)
+    s.dn[...] = (
+        dot_nt(s.a1[0], s.wg[0])
+        + dot_nt(s.a1[1], s.wg[1])
+        + dot_nt(s.a2[0], s.wu[0])
+        + dot_nt(s.a2[1], s.wu[1])
+    )
+
+    def fourth(rs):
+        dv, dg = norm_back(s.h1[rs], s.gain_ref[2:3], s.dn[rs])
+        s.dg_ref[2:3] += dg
+        dh = s.ct[rs].astype(F32) + dv
+        s.dh1[rs] = dh
+        dv, dg = norm_back(s.ao[rs], s.gain_ref[1:2], dh)
+        s.dg_ref[1:2] += dg
+        s.ddn[rs] = dv.astype(BF)
+        s.ddnt[:, rs] = permuted(dv)
+
+    per_rows(fourth)
+
+    def out_back(v, put):
+        def run(u, carry):
+            hs = aligned((v * 2 + u) * HD, HD)
+            s.datt[:, hs] = dot_nt(s.ddn[...], s.wo[hs, :]).astype(BF)
+            put(3, u, HD, dot32(s.ddnt[...], s.att[:, hs]))
+            return carry
+
+        lax.fori_loop(0, 2, run, 0)
+
+    out_back(other, give)
+    out_back(w, keep)
+
+    s.dka[...] = jnp.zeros_like(s.dka)
+    s.dva[...] = jnp.zeros_like(s.dva)
+
+    def attend_back(i, carry):
+        a, h = lax.div(i, heads), lax.rem(i, heads)
+        ks = pl.ds(pl.multiple_of(a * TILE, TILE), win)
+        qr = aligned(a * TILE, TILE)
+        hs = aligned(h * HD, HD)
+        do = s.datt[qr, hs]
+        pr = s.ps[i]
+        s.dva[ks, :] += dot_tn(pr.astype(BF), do)
+        dp = dot_nt(do, s.va[ks, :])
+        inner = jnp.sum(pr * dp, axis=-1, keepdims=True)
+        ds = (pr * (dp - inner) * s.ts[i].astype(F32)).astype(BF)
+        s.dka[ks, :] += dot_tn(ds, s.qs[i])
+        dq = dot32(ds, s.ka[ks, :])
+        s.datt[qr, hs] = (turn_back(dq, s.cs[qr], s.sn[qr]) * HD ** (-0.5)).astype(BF)
+        return carry
+
+    lax.fori_loop(0, tiles * heads, attend_back, 0)
+
+    s.dks[0] = s.dka[0:WINDOW, :].astype(BF)
+    s.dks[1] = s.dva[0:WINDOW, :].astype(BF)
+    d_halo = [
+        remote(s.dks.at[i], s.dkr.at[i], s.dsend.at[i], s.drecv.at[i], prev_id) for i in range(2)
+    ]
+
+    @pl.when(flat > 0)
+    def _():
+        for cp in d_halo:
+            cp.start()
+
+    def query_back(v, put):
+        def run(u, carry):
+            hs = aligned((v * 2 + u) * HD, HD)
+            put(4, u, HD, dot32(s.xat[...], s.datt[:, hs]))
+            return carry
+
+        lax.fori_loop(0, 2, run, 0)
+
+    query_back(other, give)
+    s.dn[...] = dot_nt(s.datt[:, : HQ // 2], s.wq[0]) + dot_nt(s.datt[:, HQ // 2 :], s.wq[1])
+    query_back(w, keep)
+
+    @pl.when(flat < n_dev - 1)
+    def _():
+        for cp in d_halo:
+            cp.wait_recv()
+
+    @pl.when(flat == n_dev - 1)
+    def _():
+        s.dkr[...] = jnp.zeros_like(s.dkr)
+
+    dk = s.dka[tok:, :] + s.dkr[0].astype(F32)
+    s.dkv[0] = turn_back(dk, s.cs[...], s.sn[...]).astype(BF)
+    s.dkv[1] = (s.dva[tok:, :] + s.dkr[1].astype(F32)).astype(BF)
+    kvw = HD // 2
+    for i in range(2):
+        give(5 + i, 0, kvw, dot32(s.xat[...], s.dkv[i, :, aligned(other * kvw, kvw)]))
+    for i in range(2):
+        keep(5 + i, 0, kvw, dot32(s.xat[...], s.dkv[i, :, aligned(w * kvw, kvw)]))
+    s.chunk_done(3)
+    s.dn[...] += dot_nt(s.dkv[0], s.wkv_ref[0]) + dot_nt(s.dkv[1], s.wkv_ref[1])
+
+    def fifth(rs):
+        dv, dg = norm_back(s.tk[rs].astype(F32), s.gain_ref[0:1], s.dn[rs])
+        s.dg_ref[0:1] += dg
+        s.h1[rs] = s.dh1[rs] + dv
+
+    per_rows(fifth)
+    x_far = remote(s.h1, s.x_ref.at[out_rows], s.osend.at[1], s.orecv.at[1], partner)
+    x_own = pltpu.make_async_copy(s.h1, s.x_ref.at[out_rows], s.oown.at[1])
+    x_far.start()
+    x_own.start()
+
+    def finish():
+        for cp in w_far:
+            cp.wait_send()
+
+        @pl.when(flat < n_dev - 1)
+        def _():
+            for cp in halo:
+                cp.wait_send()
+
+        @pl.when(flat > 0)
+        def _():
+            for cp in d_halo:
+                cp.wait_send()
+
+        for m, count, width in ((0, 4, TILE), (1, 4, TILE), (2, 4, TILE), (3, 2, HD), (4, 2, HD), (5, 1, kvw), (6, 1, kvw)):
+            for u in range(count):
+                exchange(m, u, width).wait_send()
+        y_own.wait()
+        x_own.wait()
+        y_far.wait()
+        x_far.wait()
+
+    return finish
+
+
+LAYER_INPUTS = (
+    "tok_ref",
+    "cot_ref",
+    "ids_ref",
+    "gain_ref",
+    "wkv_ref",
+    "cosi_ref",
+    "sini_ref",
+    "cosb_ref",
+    "sinb_ref",
+    "wq_ref",
+    "wo_ref",
+    "wgu_ref",
+    "wd_ref",
+)
+
+
+def layer_kernel(ctx_count, wa_count, names, *refs):
+    s = Refs()
+    for name, ref in zip(names, refs):
+        setattr(s, name, ref)
+    s.chunk_done = lambda ci: None
+    c = lax.axis_index("ctx")
+    w = lax.axis_index("wa")
+    flat = c * wa_count + w
+    n_dev = ctx_count * wa_count
+    barrier = pltpu.get_barrier_semaphore()
+
+    def greet(i, carry):
+        other = lax.rem(flat + i, n_dev)
+        pl.semaphore_signal(
+            barrier,
+            inc=1,
+            device_id=(lax.div(other, wa_count), lax.rem(other, wa_count)),
+            device_id_type=MESH,
+        )
+        return carry
+
+    lax.fori_loop(1, n_dev, greet, 0)
+    pl.semaphore_wait(barrier, n_dev - 1)
+    finish = layer_phases(s, ctx_count, wa_count)
+    out = pltpu.make_async_copy(s.gb, s.g_ref, s.gout)
+    out.start()
+    finish()
+    out.wait()
+
+
+def rotation_tables(tok, n_dev):
+    freq = ROPE_BASE ** (-2.0 * np.arange(HD // 2) / HD)
+    inner = np.arange(tok)[:, None] * freq[None, :]
+    base = (np.arange(n_dev) * tok)[:, None] * freq[None, :]
+    return [jnp.asarray(f(a), F32) for a in (inner, base) for f in (np.cos, np.sin)]
+
+
+def run_layer(tokens, cotangent, seq_ids, gains, wkv, wq, wo, wgu, wd, ctx_count, wa_count):
+    block = tokens.shape[0]
+    tok = block // wa_count
+    n_dev = ctx_count * wa_count
+    scratch = layer_scratch(tok)
+    scratch["gout"] = pltpu.SemaphoreType.DMA
+    names = LAYER_INPUTS + ("y_ref", "x_ref", "g_ref", "dg_ref") + tuple(scratch)
+    any_space = pl.BlockSpec(memory_space=pl.ANY)
+    vmem = pl.BlockSpec(memory_space=pltpu.VMEM)
+    cols = layout(wa_count)[2]
+    return pl.pallas_call(
+        partial(layer_kernel, ctx_count, wa_count, names),
+        out_shape=(
+            jax.ShapeDtypeStruct((block, D), BF),
+            jax.ShapeDtypeStruct((block, D), F32),
+            jax.ShapeDtypeStruct((IN_COUNT, D // IN_COUNT, cols), BF),
+            jax.ShapeDtypeStruct((8, D), F32),
+        ),
+        in_specs=[any_space] * 2 + [vmem] * 7 + [any_space] * 4,
+        out_specs=(any_space, any_space, any_space, vmem),
+        scratch_shapes=list(scratch.values()),
+        compiler_params=pltpu.CompilerParams(
+            collective_id=1, has_side_effects=True, vmem_limit_bytes=61 << 20
+        ),
+        name="layer",
+    )(
+        tokens,
+        cotangent,
+        seq_ids.reshape(wa_count, tok),
+        gains,
+        wkv,
+        *rotation_tables(tok, n_dev),
+        wq,
+        wo,
+        wgu,
+        wd,
+    )
 
 
 def per_device(
@@ -559,198 +1065,20 @@
     gain_first,
     gain_second,
 ):
-    ctx_index = lax.axis_index("ctx")
-    wa_index = lax.axis_index("wa")
     ctx_count = lax.axis_size("ctx")
     wa_count = lax.axis_size("wa")
-    tok_count = tokens.shape[0]
-    head_local = w_query.shape[1] // HD
-    block_rows = min(512, tok_count)
-    key_span = block_rows + WINDOW
-    block_total = tok_count // block_rows
-    positions = local_positions(seq_ids, ctx_index)
-    angles = positions.astype(jnp.float32)[:, None] * inverse_freq()[None, :]
-    resid_in = tokens.astype(jnp.float32)
-    normed = rms_scale(resid_in, norm_gains[0]).astype(jnp.bfloat16)
-    query_proj = jnp.dot(normed, w_query, preferred_element_type=jnp.float32)
-    key_proj = jnp.dot(normed, w_keyval[0], preferred_element_type=jnp.float32)
-    value_proj = jnp.dot(normed, w_keyval[1], preferred_element_type=jnp.float32)
-    query_rot = (
-        rotate(query_proj.reshape(tok_count, head_local, HD), angles) * HD ** (-0.5)
-    ).astype(jnp.bfloat16)
-    key_rot = rotate(key_proj, angles).astype(jnp.bfloat16)
-    value_low = value_proj.astype(jnp.bfloat16)
-    prev_key, prev_value, prev_pos, prev_ids = shifted(
-        (key_rot, value_low, positions, seq_ids), "ctx", 1
-    )
-    prev_ids = jnp.where(ctx_index > 0, prev_ids, -1)
-    keys_all = jnp.concatenate([prev_key, key_rot])
-    values_all = jnp.concatenate([prev_value, value_low])
-    pos_all = jnp.concatenate([prev_pos, positions])
-    ids_all = jnp.concatenate([prev_ids, seq_ids])
-    attended_parts = []
-    lse_parts = []
-    for block_idx in range(block_total):
-        q_start = block_idx * block_rows
-        k_start = tok_count + q_start - WINDOW
-        masked, tanh_cap = block_scores(
-            query_rot[q_start : q_start + block_rows],
-            keys_all[k_start : k_start + key_span],
-            positions[q_start : q_start + block_rows],
-            seq_ids[q_start : q_start + block_rows],
-            pos_all[k_start : k_start + key_span],
-            ids_all[k_start : k_start + key_span],
-        )
-        row_max = jnp.max(masked, axis=-1, keepdims=True)
-        exp_terms = jnp.exp(masked - row_max)
-        row_total = jnp.sum(exp_terms, axis=-1, keepdims=True)
-        prob_low = (exp_terms / row_total).astype(jnp.bfloat16)
-        attended_parts.append(
-            jnp.einsum(
-                "hbs,sd->bhd",
-                prob_low,
-                values_all[k_start : k_start + key_span],
-                preferred_element_type=jnp.float32,
-            )
-        )
-        lse_parts.append(row_max + jnp.log(row_total))
-    att_low = (
-        jnp.concatenate(attended_parts).reshape(tok_count, head_local * HD).astype(jnp.bfloat16)
-    )
-    attn_part = jnp.dot(att_low, w_out, preferred_element_type=jnp.float32)
-    attn_proj = lax.psum(attn_part, "wa")
-    hidden_one = resid_in + rms_scale(attn_proj, norm_gains[1])
-    ffn_in = rms_scale(hidden_one, norm_gains[2]).astype(jnp.bfloat16)
-    gate_up = jnp.einsum("td,gdf->gtf", ffn_in, w_gateup, preferred_element_type=jnp.float32)
-    inner_act = geglu(gate_up[0], gate_up[1]).astype(jnp.bfloat16)
-    down_part = jnp.dot(inner_act, w_down, preferred_element_type=jnp.float32)
-    down_proj = lax.psum(down_part, "wa")
-    layer_out = hidden_one + rms_scale(down_proj, norm_gains[3])
-    block_out = layer_out.astype(jnp.bfloat16)
-    out_grad = cotangent.astype(jnp.float32)
-    post_ffn_pull = jax.vjp(rms_scale, down_proj, norm_gains[3])[1]
-    d_down, d_gain3 = post_ffn_pull(out_grad)
-    d_down_low = d_down.astype(jnp.bfloat16)
-    grad_down = jnp.dot(inner_act.T, d_down_low, preferred_element_type=jnp.float32)
-    d_inner = jnp.dot(d_down_low, w_down.T, preferred_element_type=jnp.float32)
-    act_pull = jax.vjp(geglu, gate_up[0], gate_up[1])[1]
-    d_gate, d_up = act_pull(d_inner)
-    d_gateup_low = jnp.stack([d_gate, d_up]).astype(jnp.bfloat16)
-    grad_gateup = jnp.einsum(
-        "td,gtf->gdf", ffn_in, d_gateup_low, preferred_element_type=jnp.float32
-    )
-    d_ffn_part = jnp.einsum(
-        "gtf,gdf->td", d_gateup_low, w_gateup, preferred_element_type=jnp.float32
-    )
-    d_ffn = lax.psum(d_ffn_part, "wa")
-    pre_ffn_pull = jax.vjp(rms_scale, hidden_one, norm_gains[2])[1]
-    d_hidden_b, d_gain2 = pre_ffn_pull(d_ffn)
-    d_hidden = out_grad + d_hidden_b
-    post_attn_pull = jax.vjp(rms_scale, attn_proj, norm_gains[1])[1]
-    d_attn, d_gain1 = post_attn_pull(d_hidden)
-    d_attn_low = d_attn.astype(jnp.bfloat16)
-    grad_out = jnp.dot(att_low.T, d_attn_low, preferred_element_type=jnp.float32)
-    d_att_low = (
-        jnp.dot(d_attn_low, w_out.T, preferred_element_type=jnp.float32)
-        .astype(jnp.bfloat16)
-        .reshape(tok_count, head_local, HD)
-    )
-    d_query_parts = []
-    d_keys_all = jnp.zeros((2 * tok_count, HD), jnp.float32)
-    d_values_all = jnp.zeros((2 * tok_count, HD), jnp.float32)
-    for block_idx in range(block_total):
-        q_start = block_idx * block_rows
-        k_start = tok_count + q_start - WINDOW
-        query_blk = query_rot[q_start : q_start + block_rows]
-        key_blk = keys_all[k_start : k_start + key_span]
-        value_blk = values_all[k_start : k_start + key_span]
-        masked, tanh_cap = block_scores(
-            query_blk,
-            key_blk,
-            positions[q_start : q_start + block_rows],
-            seq_ids[q_start : q_start + block_rows],
-            pos_all[k_start : k_start + key_span],
-            ids_all[k_start : k_start + key_span],
-        )
-        prob_f32 = jnp.exp(masked - lse_parts[block_idx])
-        prob_low = prob_f32.astype(jnp.bfloat16)
-        d_att_blk = d_att_low[q_start : q_start + block_rows]
-        d_probs = jnp.einsum(
-            "bhd,sd->hbs", d_att_blk, value_blk, preferred_element_type=jnp.float32
-        )
-        inner_sum = jnp.sum(prob_f32 * d_probs, axis=-1, keepdims=True)
-        d_raw = (prob_f32 * (d_probs - inner_sum) * (1.0 - tanh_cap * tanh_cap)).astype(
-            jnp.bfloat16
-        )
-        d_query_parts.append(
-            jnp.einsum("hbs,sd->bhd", d_raw, key_blk, preferred_element_type=jnp.float32)
-        )
-        d_key_blk = jnp.einsum("hbs,bhd->sd", d_raw, query_blk, preferred_element_type=jnp.float32)
-        d_value_blk = jnp.einsum(
-            "hbs,bhd->sd", prob_low, d_att_blk, preferred_element_type=jnp.float32
-        )
-        d_keys_all = d_keys_all.at[k_start : k_start + key_span].add(d_key_blk)
-        d_values_all = d_values_all.at[k_start : k_start + key_span].add(d_value_blk)
-    from_next = (
-        shifted(d_keys_all[:tok_count].astype(jnp.bfloat16), "ctx", -1).astype(jnp.float32),
-        shifted(d_values_all[:tok_count].astype(jnp.bfloat16), "ctx", -1).astype(jnp.float32),
-    )
-    d_key_own = d_keys_all[tok_count:] + from_next[0]
-    d_value_own = d_values_all[tok_count:] + from_next[1]
-    d_key_sum, d_value_sum = (
-        lax.psum(d_key_own.astype(jnp.bfloat16), "wa").astype(jnp.float32),
-        lax.psum(d_value_own.astype(jnp.bfloat16), "wa").astype(jnp.float32),
-    )
-    d_key_low = rotate_back(d_key_sum, angles).astype(jnp.bfloat16)
-    d_value_low = d_value_sum.astype(jnp.bfloat16)
-    d_query_rot = jnp.concatenate(d_query_parts)
-    d_query_low = (
-        (rotate_back(d_query_rot, angles) * HD ** (-0.5))
-        .reshape(tok_count, head_local * HD)
-        .astype(jnp.bfloat16)
-    )
-    half_kv = HD // wa_count
-    key_half = take_block(d_key_low, 1, wa_index, half_kv)
-    value_half = take_block(d_value_low, 1, wa_index, half_kv)
-    w_key_half = take_block(w_keyval[0], 1, wa_index, half_kv)
-    w_value_half = take_block(w_keyval[1], 1, wa_index, half_kv)
-    grad_query = jnp.dot(normed.T, d_query_low, preferred_element_type=jnp.float32)
-    grad_keyval = jnp.stack(
-        [
-            jnp.dot(normed.T, key_half, preferred_element_type=jnp.float32),
-            jnp.dot(normed.T, value_half, preferred_element_type=jnp.float32),
-        ]
-    )
-    d_normed_part = jnp.dot(d_query_low, w_query.T, preferred_element_type=jnp.float32)
-    d_normed_part = d_normed_part + jnp.dot(
-        key_half, w_key_half.T, preferred_element_type=jnp.float32
-    )
-    d_normed_part = d_normed_part + jnp.dot(
-        value_half, w_value_half.T, preferred_element_type=jnp.float32
-    )
-    d_normed = lax.psum(d_normed_part.astype(jnp.bfloat16), "wa").astype(jnp.float32)
-    pre_attn_pull = jax.vjp(rms_scale, resid_in, norm_gains[0])[1]
-    d_tokens, d_gain0 = pre_attn_pull(d_normed)
-    input_grad = d_hidden + d_tokens
-    grad_gains = jnp.stack([d_gain0, d_gain1, d_gain2, d_gain3])
-    stack = jnp.concatenate(
-        [
-            grad_down.T,
-            grad_gateup[0],
-            grad_gateup[1],
-            grad_out.T,
-            grad_query,
-            grad_keyval[0],
-            grad_keyval[1],
-        ],
-        axis=1,
-    ).astype(jnp.bfloat16)
-    cols = stack.shape[1]
-    rows = D // ctx_count
-    stack = (
-        stack.reshape(ctx_count // IN_COUNT, IN_COUNT, rows, cols)
-        .transpose(1, 0, 2, 3)
-        .reshape(IN_COUNT, D // IN_COUNT, cols)
+    block_out, input_grad, stack, grad_gains = run_layer(
+        tokens,
+        cotangent,
+        seq_ids,
+        norm_gains,
+        w_keyval,
+        w_query,
+        w_out,
+        w_gateup,
+        w_down,
+        ctx_count,
+        wa_count,
     )
     moments = jnp.concatenate(
         [
@@ -764,7 +1092,7 @@
         ],
         axis=1,
     )
-    sums, fresh, updates = run_tail(stack, moments, ctx_count, wa_count)
+    sums, fresh, updates, sum_gains = run_tail(stack, moments, grad_gains, ctx_count, wa_count)
     halves, offs, _ = layout(wa_count)
 
     def unstack(flat):
@@ -776,7 +1104,7 @@
     sum_query, sum_keyval, sum_out, sum_gateup, sum_down = unstack(sums)
     new_mom_query, new_mom_keyval, new_mom_out, new_mom_gateup, new_mom_down = unstack(fresh)
     upd_query, upd_keyval, upd_out, upd_gateup, upd_down = unstack(updates)
-    sum_gains = lax.psum_scatter(grad_gains, "ctx", scatter_dimension=1, tiled=True)
+    sum_gains = sum_gains[:4, : D // ctx_count]
     new_gain_first = ADAM_ONE * gain_first + (1.0 - ADAM_ONE) * sum_gains
     new_gain_second = ADAM_TWO * gain_second + (1.0 - ADAM_TWO) * sum_gains * sum_gains
     gain_update = -GAIN_RATE * new_gain_first / (jnp.sqrt(new_gain_second) + ADAM_EPS)

time: 590 us -> 265 us (0.45)
  the two profiles are of different devices: /device:TPU:0 before, /device:TPU:15 now
where the time goes in v2:
time: 265 us
  Pallas kernels  242 us (91%)
  local copies, waits for them, and re-layouts  16.1 us (6%)
  other arithmetic  5.48 us (2%)
    pallas_call x1, Pallas kernels, run_tail(): pl.pallas_call(partial(tail_kernel, ctx_count, wa_count), out_shape=(shar...  163 us
    pallas_call x1, Pallas kernels, run_layer(): pl.pallas_call(partial(layer_kernel, ctx_count, wa_count, names), out_sha...  79.7 us
    unnamed x24, local copies, waits for them, and re-layouts  8.32 us

profile of v2, /device:TPU:15, one launch (start us, length us, event | category | flops | bytes accessed | tf_op | source)
XLA Modules:
  0.0 264.8 jit_solution(7153481538358000449)
XLA Ops:
  0.7 1.3 reshape.45.refs_2_
  2.0 0.9 bitcast_dynamic-update-slice_fusion.2
  2.9 0.9 bitcast_dynamic-update-slice_fusion.1
  3.8 0.9 bitcast_dynamic-update-slice_fusion
  4.8 0.9 bitcast_dynamic-update-slice_fusion.3
  5.7 0.9 constant_dynamic-update-slice_fusion
  6.6 79.7 %layer.1 = (bf16[1024,640]{1,0:T(8,128)(2,1)}, f32[1024,640]{1,0:T(8,128)}, bf16[4,160,4352]{2,1,0:T(8,128)(2,1)}, f32[8,640]{1,0:T(8,128)}) custom-call(bf16[1024,640]{1,0:T(8,128)(2,1)} %refs_0_.1, bf16[1024,640]{1,0:T(8,128)(2,1)} %refs_1_.1, s32[2,512]{1,0:T(2,128)} %reshape.45.refs_2_, f32[4,640]{1,0:T(4,128)} %refs_3_.1, bf16[2,640,256]{2,1,0:T(8,128)(2,1)} %refs_4_.1, ...), custom_call_target="tpu_custom_call" | custom-call | tf_op jit(solution)/shard_map/layer/pallas_call | solution.py:1021
  86.3 162.8 %tail.1 = (f32[40,4352]{1,0:T(8,128)}, f32[40,4352]{1,0:T(8,128)}, f32[40,4352]{1,0:T(8,128)}, f32[8,128]{1,0:T(8,128)}) custom-call(bf16[4,160,4352]{2,1,0:T(8,128)(2,1)} %get-tuple-element.31.g_ref, f32[40,4352]{1,0:T(8,128)} %copy-done.2, f32[8,640]{1,0:T(8,128)} %get-tuple-element.32.dg_ref), custom_call_target="tpu_custom_call" | custom-call | tf_op jit(solution)/shard_map/tail/pallas_call | solution.py:452
  249.1 1.4 add_divide_fusion
  250.5 0.8 slice_bitcast_fusion.17
  251.3 0.6 pad_maximum_fusion.3
  251.9 0.8 slice_bitcast_fusion.13
  252.7 0.6 pad_maximum_fusion.5
  253.3 0.6 pad_maximum_fusion.4
  254.0 1.6 slice_bitcast_fusion.11
  255.5 1.8 slice_bitcast_fusion.6
  257.3 0.7 pad_maximum_fusion
  258.1 0.7 slice_bitcast_fusion.9
  258.8 0.8 slice_bitcast_fusion
  259.6 0.7 pad_maximum_fusion.2
  260.4 0.7 pad_maximum_fusion.1
  261.1 1.1 copy.49
  262.2 1.2 copy-done
  263.4 1.5 copy.50
  (17 shorter events, 0.0 us)
Async XLA Ops:
  0.7 5.9 %copy-start.5 = (f32[2,40,128]{2,1,0:T(8,128)S(1)}, f32[2,40,128]{2,1,0:T(8,128)}, u32[]{:S(2)}) copy-start(f32[2,40,128]{2,1,0:T(8,128)} %param.30) | copy-start | bytes 122884
  6.6 79.7 %copy-start.2 = (f32[40,4352]{1,0:T(8,128)}, f32[40,4352]{1,0:T(8,128)S(1)}, u32[]{:S(2)}) copy-start(f32[40,4352]{1,0:T(8,128)S(1)} %bitcast_dynamic-update-slice_fusion.4.mom_ref) | copy-start | bytes 2088964
  86.3 162.8 %copy-start.6 = (f32[4,40]{1,0:T(4,128)S(1)}, f32[4,40]{1,0:T(4,128)}, u32[]{:S(2)}) copy-start(f32[4,40]{1,0:T(4,128)} %param.35) | copy-start | bytes 1924
  86.3 162.8 %copy-start.7 = (f32[4,40]{1,0:T(4,128)S(1)}, f32[4,40]{1,0:T(4,128)}, u32[]{:S(2)}) copy-start(f32[4,40]{1,0:T(4,128)} %param.34) | copy-start | bytes 1924
  249.1 9.0 %copy-start.3 = (f32[40,4352]{1,0:T(8,128)S(1)}, f32[40,4352]{1,0:T(8,128)}, u32[]{:S(2)}) copy-start(f32[40,4352]{1,0:T(8,128)} %get-tuple-element.35) | copy-start | bytes 2088964
  249.1 9.0 %copy-start.4 = (f32[40,4352]{1,0:T(8,128)S(1)}, f32[40,4352]{1,0:T(8,128)}, u32[]{:S(2)}) copy-start(f32[40,4352]{1,0:T(8,128)} %get-tuple-element.36) | copy-start | bytes 2088964
  258.8 2.3 copy-start.1
  261.1 2.2 copy-start

commit v3 on v2

v3 whole, which is shorter than its diff:
```python
from functools import partial
import math

import jax
import jax.numpy as jnp
import numpy as np
from jax import lax
from jax.experimental import pallas as pl
from jax.experimental.pallas import tpu as pltpu
from jax.sharding import PartitionSpec as P

D = 640
FF = 2048
HD = 256
WINDOW = 512
SOFT_CAP = 10
NS_STEPS = 5
HQ = 1024


EPS_NORM = 1e-06
ROPE_BASE = 10000.0
MOMENTUM = 0.95
ADAM_ONE = 0.9
ADAM_TWO = 0.95
ADAM_EPS = 1e-08
GAIN_RATE = 0.1
QUINTIC_A = 3.4445
QUINTIC_B = -4.775
QUINTIC_C = 2.0315
MATRIX_COUNT = 7
MUON_RATE = 0.2

MESH = pl.DeviceIdType.MESH
BF = jnp.bfloat16
F32 = jnp.float32
IN_COUNT = 4
NAMES = ("down", "gate", "up", "out", "query", "key", "value")
WIDTHS = (FF, FF, FF, HQ, HQ, HD, HD)
OWNERS = (7, 4, 8, 5, 11, 9, 10)
CHUNK_SETS = ((0,), (1,), (2,), (3, 4), (5, 6))
TILE = 256


def layout(wa_count):
    halves = [w // wa_count for w in WIDTHS]
    offs = [sum(halves[:i]) for i in range(len(halves))]
    return halves, offs, sum(halves)


def dot32(a, b):
    return jnp.dot(a, b, preferred_element_type=F32)


def eye_mask(n):
    return (
        lax.broadcasted_iota(jnp.int32, (n, n), 0) == lax.broadcasted_iota(jnp.int32, (n, n), 1)
    )


def pad_rows(v, rows):
    if v.shape[0] == rows:
        return v
    return jnp.concatenate([v, jnp.zeros((rows - v.shape[0], v.shape[1]), v.dtype)], axis=0)


def split_into(v, hi, lo):
    top = v.astype(BF)
    hi[...] = top
    lo[...] = (v - top.astype(F32)).astype(BF)


SYM_TILES = ((0, 256), (256, 512), (512, 640))


def sym_tiles(out, block):
    for a, b in SYM_TILES:
        v = block(a, b)
        out[a:, a:b] = v
        if b < D:
            out[a:b, b:] = v[b - a :].T


def prod3(h1, l1, h2, l2):
    return lambda a, b: (
        dot32(h1[a:], h2[:, a:b]) + dot32(h1[a:], l2[:, a:b]) + dot32(l1[a:], h2[:, a:b])
    )


def tail_scratch(ctx_count, wa_count):
    v = pltpu.VMEM
    dma = pltpu.SemaphoreType.DMA
    n_in = IN_COUNT
    n_out = ctx_count // n_in
    rows = D // ctx_count
    rp = -(-rows // 16) * 16
    n_dev = ctx_count * wa_count
    n_ch = len(CHUNK_SETS)
    cols = layout(wa_count)[2]
    return dict(
        mb=v((rp, cols), BF),
        xb=v((ctx_count, rp, FF), BF),
        am=v((D, D), F32),
        dg_ref=v((8, D), F32),
        dgs=v((ctx_count, 8, 128), F32),
        dgr=v((n_dev, 8, 128), F32),
        psend=dma((n_ch, n_in - 1)),
        precv=dma((n_ch, n_in - 1)),
        lsend=dma((n_ch, n_out - 1)),
        lrecv=dma((n_ch, n_out - 1)),
        gsend=dma((MATRIX_COUNT,)),
        grecv=dma,
        usend=dma((n_dev,)),
        urecv=dma((MATRIX_COUNT,)),
        gnsend=dma((n_dev,)),
        gnrecv=dma,
        msem=dma((MATRIX_COUNT,)),
        pfree=pltpu.SemaphoreType.REGULAR,
        lfree=pltpu.SemaphoreType.REGULAR,
    )


def tail_phases(s, ctx_count, wa_count):
    c = lax.axis_index("ctx")
    w = lax.axis_index("wa")
    n_in = IN_COUNT
    n_out = ctx_count // n_in
    n_dev = ctx_count * wa_count
    p = lax.rem(c, n_in)
    z = lax.div(c, n_in)
    rows = D // ctx_count
    rp = s.xb.shape[1]
    block = D // n_in
    halves, offs, cols = layout(wa_count)
    chunks = [(offs[m[0]], sum(halves[i] for i in m)) for m in CHUNK_SETS]
    me = c * wa_count + w
    per = ctx_count // 2

    def plane_slot(ci, k):
        i = min(ci, 4) * (n_in - 1) + (k - 1 if ci < 4 else 0)
        buf = (s.wg, s.wu)[i // 8]
        lanes = pl.ds(0, chunks[ci][1]) if ci < 4 else pl.ds((k - 1) * TILE, TILE)
        return buf.at[i % 8 // 4, pl.ds(i % 4 * block, block), lanes]

    def line_slot(base, ci, j):
        wid = chunks[ci][1]
        if ci < 4:
            start = ci % 2 * 256 + j * rp
            return s.ffb.at[base * 2 + ci // 2, pl.ds(pl.multiple_of(start, 16), rp), pl.ds(0, wid)]
        return s.ffb.at[4 + base, pl.ds(pl.multiple_of(j * rp, 16), rp), pl.ds(0, wid)]

    def plane_copy(ci, k):
        off, wid = chunks[ci]
        q = lax.rem(p + k, n_in)
        return pltpu.make_async_remote_copy(
            s.gb.at[q, :, pl.ds(off, wid)],
            plane_slot(ci, k),
            s.psend.at[ci, k - 1],
            s.precv.at[ci, k - 1],
            device_id=(z * n_in + q, w),
            device_id_type=MESH,
        )

    def line_copy(ci, k):
        j = lax.rem(z + k, n_out)
        return pltpu.make_async_remote_copy(
            line_slot(0, ci, j),
            line_slot(1, ci, k - 1),
            s.lsend.at[ci, k - 1],
            s.lrecv.at[ci, k - 1],
            device_id=(j * n_in + p, w),
            device_id_type=MESH,
        )

    def buffers_free():
        for k in range(1, n_in):
            pl.semaphore_signal(
                s.pfree,
                inc=1,
                device_id=(z * n_in + lax.rem(p + k, n_in), w),
                device_id_type=MESH,
            )
        for k in range(1, n_out):
            pl.semaphore_signal(
                s.lfree,
                inc=1,
                device_id=(lax.rem(z + k, n_out) * n_in + p, w),
                device_id_type=MESH,
            )

    def plane_start(ci):
        for k in range(1, n_in):
            plane_copy(ci, k).start()

    def first_sends():
        pl.semaphore_wait(s.pfree, n_in - 1)
        for ci in range(3):
            plane_start(ci)

    def plane_finish(ci):
        off, wid = chunks[ci]
        for k in range(1, n_in):
            plane_copy(ci, k).wait_recv()

        def plane_sum(t, carry):
            cs = aligned(off + t * TILE, TILE)
            here = aligned(t * TILE, TILE)
            total = s.gb[p, :, cs].astype(F32)
            for k in range(1, n_in):
                total = total + plane_slot(ci, k)[:, here].astype(F32)
            for j in range(n_out):
                slab = total[j * rows : (j + 1) * rows]

                @pl.when(z == j)
                def _():
                    s.sum_ref[:, cs] = slab

                line_slot(0, ci, j)[:, here] = pad_rows(slab, rp).astype(BF)
            return carry

        lax.fori_loop(0, wid // TILE, plane_sum, 0)
        if ci == 0:
            pl.semaphore_wait(s.lfree, n_out - 1)
        for k in range(1, n_out):
            line_copy(ci, k).start()

    def gather_copy(m, local):
        src = s.mb.at[:, pl.ds(offs[m], halves[m])]
        dst = s.xb.at[c, :, pl.ds(pl.multiple_of(w * halves[m], 128), halves[m])]
        if local:
            return pltpu.make_async_copy(src, dst, s.grecv)
        return pltpu.make_async_remote_copy(
            src, dst, s.gsend.at[m], s.grecv, device_id=(OWNERS[m], 0), device_id_type=MESH
        )

    def line_finish(ci):
        off, wid = chunks[ci]
        for k in range(1, n_out):
            line_copy(ci, k).wait_recv()

        def line_sum(t, carry):
            cs = aligned(off + t * TILE, TILE)
            here = aligned(t * TILE, TILE)
            total = s.sum_ref[:, cs]
            for k in range(n_out - 1):
                total = total + line_slot(1, ci, k)[:, here][:rows].astype(F32)
            s.sum_ref[:, cs] = total
            fresh = MOMENTUM * s.nm_ref[:, cs] + total
            s.nm_ref[:, cs] = fresh
            s.mb[:, cs] = pad_rows(fresh, rp).astype(BF)
            return carry

        lax.fori_loop(0, wid // TILE, line_sum, 0)
        for m in CHUNK_SETS[ci]:
            mine = me == OWNERS[m] * wa_count

            @pl.when(mine)
            def _():
                gather_copy(m, True).start()

            @pl.when(jnp.logical_not(mine))
            def _():
                gather_copy(m, False).start()

    s.buffers_free = buffers_free
    s.first_sends = first_sends
    s.plane_start = plane_start
    s.plane_finish = plane_finish

    sources = (
        s.md_ref,
        s.mgu_ref.at[0],
        s.mgu_ref.at[1],
        s.mo_ref,
        s.mq_ref,
        s.mkv_ref.at[0],
        s.mkv_ref.at[1],
    )
    moms = [
        pltpu.make_async_copy(src, s.nm_ref.at[:, pl.ds(offs[m], halves[m])], s.msem.at[m])
        for m, src in enumerate(sources)
    ]
    for cp in moms:
        cp.start()

    def rest():
        for i in range(ctx_count):
            s.dgs[i, :, 0:rows] = s.dg_ref[:, i * rows : (i + 1) * rows]

        def gain_copy(t):
            i, v = lax.div(t, wa_count), lax.rem(t, wa_count)
            return pltpu.make_async_remote_copy(
                s.dgs.at[i],
                s.dgr.at[me],
                s.gnsend.at[t],
                s.gnrecv,
                device_id=(i, v),
                device_id_type=MESH,
            )

        def gain_send(t, carry):
            gain_copy(lax.rem(me + t, n_dev)).start()
            return carry

        def gain_sent(t, carry):
            gain_copy(lax.rem(me + t, n_dev)).wait_send()
            return carry

        for cp in moms:
            cp.wait()
        plane_finish(2)
        line_finish(0)
        line_finish(1)
        plane_finish(3)
        plane_finish(4)
        line_finish(2)
        pltpu.make_async_copy(s.dgs.at[c], s.dgr.at[me], s.gnrecv).start()
        lax.fori_loop(1, n_dev, gain_send, 0)
        line_finish(3)
        line_finish(4)
        for ci in range(len(chunks)):
            for k in range(1, n_in):
                plane_copy(ci, k).wait_send()
            for k in range(1, n_out):
                line_copy(ci, k).wait_send()
        solve()
        pltpu.make_async_copy(s.dgr, s.dgr, s.gnrecv).wait()
        s.gs_ref[...] = jnp.sum(s.dgr[...], axis=0)
        lax.fori_loop(1, n_dev, gain_sent, 0)
        updates_back()

    def owned_by(*which):
        hit = me == OWNERS[which[0]] * wa_count
        for m in which[1:]:
            hit = jnp.logical_or(hit, me == OWNERS[m] * wa_count)
        return hit

    def solve():
        is_owner = owned_by(*range(MATRIX_COUNT))
        is_small = owned_by(5, 6)
        is_wide = owned_by(0, 1, 2)
        tiles = jnp.where(is_small, HD // TILE, jnp.where(is_wide, FF // TILE, HQ // TILE))
        am, xf = s.am, s.dka.at[pl.ds(0, D)]
        ah = s.wd.at[pl.ds(0, D)]
        al = s.wd.at[pl.ds(D, D)]
        ph = s.wd.at[pl.ds(2 * D, D)]
        plo = s.wo.at[pl.ds(0, D)]
        qh = s.wu.at[0, :, pl.ds(0, D)]

        def tile_of(t):
            return s.wg.at[lax.div(t, 4), :, aligned(lax.rem(t, 4) * TILE, TILE)]

        for m in range(MATRIX_COUNT):

            @pl.when(me == OWNERS[m] * wa_count)
            def _(m=m):
                whole = s.xb.at[:, :, pl.ds(0, halves[m] * wa_count)]
                pltpu.make_async_copy(whole, whole, s.grecv).wait()

        @pl.when(is_owner)
        def _():
            am[...] = jnp.zeros_like(am)

            def gram(t, carry):
                cs = aligned(t * TILE, TILE)
                for i in range(ctx_count):
                    xf[i * rows : (i + 1) * rows, :] = s.xb[i, :, cs][:rows].astype(F32)
                x = xf[...].astype(BF)
                tile_of(t)[...] = x

                @pl.when(jnp.logical_not(is_small))
                def _():
                    for a, b in SYM_TILES:
                        am[a:, a:b] += dot_nt(x[a:], x[a:b])

                @pl.when(is_small)
                def _():
                    am[0:HD, 0:HD] = dot_tn(x, x)

                return carry

            lax.fori_loop(0, tiles, gram, 0)
            norm2 = jnp.sum(jnp.where(eye_mask(D), am[...], 0.0), keepdims=True)
            inv = 1.0 / (jnp.sqrt(norm2) + 1e-07)
            inv2 = inv * inv
            sym_tiles(am, lambda a, b: am[a:, a:b] * inv2)

            def shifted(a, b, square):
                rest = QUINTIC_B * am[a:, a:b] + QUINTIC_C * square
                top = rest[: b - a] + jnp.where(eye_mask(b - a), QUINTIC_A, 0.0)
                return jnp.concatenate([top, rest[b - a :]], axis=0) if b < D else top

            def poly():
                split_into(am[...], ah, al)
                square = prod3(ah, al, ah, al)
                sym_tiles(am, lambda a, b: shifted(a, b, square(a, b)))

            def advance():
                sym_tiles(am, prod3(ph, plo, ah, al))
                split_into(am[...], ah, al)
                sym_tiles(am, prod3(ah, al, ph, plo))

            def grow():
                sym_tiles(am, lambda a, b: dot32(ph[a:], qh[:, a:b]))
                qh[...] = am[...].astype(BF)

            poly()
            split_into(am[...], ph, plo)
            qh[...] = ph[...]
            advance()

            def sweep(i, carry):
                poly()
                split_into(am[...], ph, plo)
                grow()
                advance()
                return carry

            lax.fori_loop(0, NS_STEPS - 2, sweep, 0)
            ah[...] = am[...].astype(BF)
            sym_tiles(am, lambda a, b: shifted(a, b, dot32(ah[a:], ah[:, a:b])))
            ph[...] = am[...].astype(BF)
            grow()
            rates = [-MUON_RATE * 0.2 * math.sqrt(n) for n in (D, FF, HQ)]
            rate = jnp.where(is_small, rates[0], jnp.where(is_wide, rates[1], rates[2]))
            scale = rate * inv

            def put(v, lanes, value):
                for i in range(ctx_count):
                    s.ffb[v * 2 + i // per, i % per * rp : (i % per + 1) * rp, lanes] = pad_rows(
                        value[i * rows : (i + 1) * rows], rp
                    ).astype(BF)

            def back(v, t):
                @pl.when(jnp.logical_not(is_small))
                def _():
                    whole = v * jnp.where(is_wide, 4, 2) + t
                    xf[...] = dot32(qh[...], tile_of(whole)[...]) * scale
                    put(v, aligned(t * TILE, TILE), xf)

                @pl.when(is_small)
                def _():
                    xf[...] = dot32(tile_of(t)[...], s.wu[0, 0:HD, 0:HD]) * scale
                    for half in range(2):
                        lanes = slice(half * (HD // 2), (half + 1) * (HD // 2))
                        put(half, pl.ds(0, HD // 2), xf[:, lanes])

            for v in range(2):
                count = jnp.where(is_small, 1 - v, jnp.where(is_wide, 4, 2))

                def run(t, carry, v=v):
                    back(v, t)
                    return carry

                lax.fori_loop(0, count, run, 0)
                for m in range(MATRIX_COUNT):

                    @pl.when(me == OWNERS[m] * wa_count)
                    def _(m=m, v=v):
                        def send(i, carry):
                            there = lax.rem(c + i, ctx_count)
                            update_copy(m, there * wa_count + v, False).start()
                            return carry

                        if v == 0:
                            update_copy(m, c * wa_count, True).start()
                            lax.fori_loop(1, ctx_count, send, 0)
                        else:
                            lax.fori_loop(0, ctx_count, send, 0)

    def update_copy(m, t, local):
        i, v = lax.div(t, wa_count), lax.rem(t, wa_count)
        start = pl.multiple_of(lax.rem(i, per) * rp, 16)
        src = s.ffb.at[v * 2 + lax.div(i, per), pl.ds(start, rp), pl.ds(0, halves[m])]
        dst = s.ub.at[:, pl.ds(offs[m], halves[m])]
        if local:
            return pltpu.make_async_copy(src, dst, s.urecv.at[m])
        return pltpu.make_async_remote_copy(
            src, dst, s.usend.at[t], s.urecv.at[m], device_id=(i, v), device_id_type=MESH
        )

    def updates_back():
        for m in range(MATRIX_COUNT):
            piece = s.ub.at[:, pl.ds(offs[m], halves[m])]
            pltpu.make_async_copy(piece, piece, s.urecv.at[m]).wait()

        for m in range(MATRIX_COUNT):
            owner = OWNERS[m] * wa_count

            @pl.when(me != owner)
            def _(m=m):
                gather_copy(m, False).wait_send()

            @pl.when(me == owner)
            def _(m=m, owner=owner):
                def done(t, carry):
                    update_copy(m, lax.rem(owner + t, n_dev), False).wait_send()
                    return carry

                lax.fori_loop(1, n_dev, done, 0)

    return rest


class Refs:
    pass


def dot_nt(a, b):
    return lax.dot_general(a, b, (((1,), (1,)), ((), ())), preferred_element_type=F32)


def dot_tn(a, b):
    return lax.dot_general(a, b, (((0,), (0,)), ((), ())), preferred_element_type=F32)


def aligned(start, size):
    return pl.ds(pl.multiple_of(start, size), size)


def norm_parts(v, gain):
    r = lax.rsqrt(jnp.mean(v * v, axis=-1, keepdims=True) + EPS_NORM)
    return r, v * r, 1.0 + gain


def norm_back(v, gain, e):
    r, zed, g1 = norm_parts(v, gain)
    e1 = e * g1
    dv = r * (e1 - zed * jnp.mean(e1 * zed, axis=-1, keepdims=True))
    return dv, jnp.sum(e * zed, axis=0, keepdims=True)


def layer_scratch(tok):
    v = pltpu.VMEM
    dma = pltpu.SemaphoreType.DMA
    cols = sum(WIDTHS) // 2
    heads = HQ // HD
    tiles = tok // TILE
    win = WINDOW + TILE
    return dict(
        wq=v((2, D, HQ // 2), BF),
        wo=v((HQ, D), BF),
        wg=v((2, D, FF // 2), BF),
        wu=v((2, D, FF // 2), BF),
        wd=v((FF, D), BF),
        tk=v((tok, D), BF),
        ct=v((tok, D), BF),
        xa=v((tok, D), BF),
        xat=v((D, tok), BF),
        fit=v((D, tok), BF),
        ddn=v((tok, D), BF),
        ddnt=v((D, tok), BF),
        cs=v((tok, HD // 2), F32),
        sn=v((tok, HD // 2), F32),
        ka=v((WINDOW + tok, HD), BF),
        va=v((WINDOW + tok, HD), BF),
        idown=v((8, tok), jnp.int32),
        idprev=v((8, tok), jnp.int32),
        qs=v((tiles * heads, TILE, HD), BF),
        ps=v((tiles * heads, TILE, win), BF),
        ts=v((tiles * heads, TILE, win), BF),
        att=v((tok, HQ), BF),
        ao=v((tok, D), F32),
        h1=v((tok, D), F32),
        dn=v((tok, D), F32),
        ffb=v((6, tok, FF // 2), BF),
        datt=v((tok, HQ), BF),
        dka=v((WINDOW + tok, HD), F32),
        dva=v((WINDOW + tok, HD), F32),
        dks=v((2, tok, HD), BF),
        dkr=v((2, tok, HD), BF),
        dkv=v((2, tok, HD), BF),
        sb=v((6, IN_COUNT, D // IN_COUNT, TILE), BF),
        gb=v((IN_COUNT, D // IN_COUNT, cols), BF),
        wsend=dma((5,)),
        wrecv=dma((5,)),
        wown=dma((5,)),
        ksend=dma((3,)),
        krecv=dma((3,)),
        dsend=dma((2,)),
        drecv=dma((2,)),
        csend=dma((MATRIX_COUNT, 4)),
        crecv=dma((MATRIX_COUNT, 4)),
        osend=dma((2,)),
        orecv=dma((2,)),
        oown=dma((2,)),
        tsem=dma((4,)),
    )


def layer_phases(s, ctx_count, wa_count):
    c = lax.axis_index("ctx")
    w = lax.axis_index("wa")
    other = 1 - w
    flat = c * wa_count + w
    n_dev = ctx_count * wa_count
    tok = s.xa.shape[0]
    rows = D // ctx_count
    n_out = ctx_count // IN_COUNT
    heads = HQ // HD
    tiles = tok // TILE
    win = WINDOW + TILE
    half_ff = FF // 2
    halves, offs, cols = layout(wa_count)
    step = 128
    partner = (c, other)
    follow = jnp.minimum(flat + 1, n_dev - 1)
    ahead = jnp.maximum(flat - 1, 0)
    next_id = (lax.div(follow, wa_count), lax.rem(follow, wa_count))
    prev_id = (lax.div(ahead, wa_count), lax.rem(ahead, wa_count))
    order = [zz * IN_COUNT + pp for pp in range(IN_COUNT) for zz in range(n_out)]

    def remote(src, dst, send, recv, where):
        return pltpu.make_async_remote_copy(
            src, dst, send, recv, device_id=where, device_id_type=MESH
        )

    def permuted(v):
        t = v.astype(BF).astype(F32).T
        return jnp.concatenate([t[i * rows : (i + 1) * rows] for i in order], axis=0).astype(BF)

    def per_rows(body):
        def run(i, carry):
            body(aligned(i * step, step))
            return carry

        lax.fori_loop(0, tok // step, run, 0)

    out_rows = aligned(w * tok, tok)
    tok_in = pltpu.make_async_copy(s.tok_ref.at[out_rows], s.tk, s.tsem.at[0])
    cot_in = pltpu.make_async_copy(s.cot_ref.at[out_rows], s.ct, s.tsem.at[1])
    tables = [
        pltpu.make_async_copy(s.cosi_ref, s.cs, s.tsem.at[2]),
        pltpu.make_async_copy(s.sini_ref, s.sn, s.tsem.at[3]),
    ]
    tok_in.start()
    for cp in tables:
        cp.start()
    cot_in.start()

    wk_refs = (
        (s.wq_ref, s.wq.at[w]),
        (s.wo_ref, s.wo.at[aligned(w * (HQ // 2), HQ // 2)]),
        (s.wgu_ref.at[0], s.wg.at[w]),
        (s.wgu_ref.at[1], s.wu.at[w]),
        (s.wd_ref, s.wd.at[aligned(w * half_ff, half_ff)]),
    )
    w_far = [remote(a, b, s.wsend.at[i], s.wrecv.at[i], partner) for i, (a, b) in enumerate(wk_refs)]
    w_own = [pltpu.make_async_copy(a, b, s.wown.at[i]) for i, (a, b) in enumerate(wk_refs)]
    for far, own in zip(w_far, w_own):
        far.start()
        own.start()

    def weights_ready(i):
        w_own[i].wait()
        w_far[i].wait_recv()

    tok_in.wait()

    def first(rs):
        x = s.tk[rs].astype(F32)
        _, zed, g1 = norm_parts(x, s.gain_ref[0:1])
        n = zed * g1
        s.xa[rs] = n.astype(BF)
        s.xat[:, rs] = permuted(n)

    per_rows(first)

    cb, sb_ = s.cosb_ref[pl.ds(flat, 1), :], s.sinb_ref[pl.ds(flat, 1), :]
    for cp in tables:
        cp.wait()
    cosi, sini = s.cs[...], s.sn[...]
    s.cs[...] = cb * cosi - sb_ * sini
    s.sn[...] = sb_ * cosi + cb * sini
    hh = HD // 2

    def turn(v, cosine, sine):
        a, b = v[:, :hh], v[:, hh:]
        return jnp.concatenate([a * cosine - b * sine, b * cosine + a * sine], axis=1)

    def turn_back(v, cosine, sine):
        a, b = v[:, :hh], v[:, hh:]
        return jnp.concatenate([a * cosine + b * sine, b * cosine - a * sine], axis=1)

    s.ka[WINDOW:, :] = turn(dot32(s.xa[...], s.wkv_ref[0]), s.cs[...], s.sn[...]).astype(BF)
    s.va[WINDOW:, :] = dot32(s.xa[...], s.wkv_ref[1]).astype(BF)
    s.idown[...] = jnp.broadcast_to(s.ids_ref[pl.ds(w, 1), :], (8, tok))

    halo = [
        remote(s.ka.at[pl.ds(tok, WINDOW)], s.ka.at[pl.ds(0, WINDOW)], s.ksend.at[0], s.krecv.at[0], next_id),
        remote(s.va.at[pl.ds(tok, WINDOW)], s.va.at[pl.ds(0, WINDOW)], s.ksend.at[1], s.krecv.at[1], next_id),
        remote(s.idown, s.idprev, s.ksend.at[2], s.krecv.at[2], next_id),
    ]

    @pl.when(flat < n_dev - 1)
    def _():
        for cp in halo:
            cp.start()

    weights_ready(0)

    def project(h, carry):
        v, u = lax.div(h, heads // 2), lax.rem(h, heads // 2)
        q = dot32(s.xa[...], s.wq[v, :, aligned(u * HD, HD)])
        q = (turn(q, s.cs[...], s.sn[...]) * HD ** (-0.5)).astype(BF)
        for a in range(tiles):
            s.qs[a * heads + h] = q[a * TILE : (a + 1) * TILE]
        return carry

    lax.fori_loop(0, heads, project, 0)

    @pl.when(flat > 0)
    def _():
        for cp in halo:
            cp.wait_recv()

    @pl.when(flat == 0)
    def _():
        s.ka[0:WINDOW, :] = jnp.zeros((WINDOW, HD), BF)
        s.va[0:WINDOW, :] = jnp.zeros((WINDOW, HD), BF)
        s.idprev[...] = jnp.full((8, tok), -1, jnp.int32)

    row_ids = jnp.concatenate([s.idprev[0:1, :], s.idown[0:1, :]], axis=1)
    own_col = jnp.broadcast_to(s.idown[0:1, :], (128, tok)).T[:, 0:1]
    gap = lax.broadcasted_iota(jnp.int32, (TILE, win), 1) - lax.broadcasted_iota(
        jnp.int32, (TILE, win), 0
    )
    for a in range(tiles):
        same = own_col[a * TILE : (a + 1) * TILE] == row_ids[:, a * TILE : a * TILE + win]
        ok = jnp.logical_and(same, jnp.logical_and(gap > 0, gap <= WINDOW))
        s.ffb[a, 0:TILE, 0:win] = jnp.where(ok, 1.0, 0.0).astype(BF)

    def attend(i, carry):
        a, h = lax.div(i, heads), lax.rem(i, heads)
        ks = pl.ds(pl.multiple_of(a * TILE, TILE), win)
        t = jnp.tanh(dot_nt(s.qs[i], s.ka[ks, :]) * (1.0 / SOFT_CAP))
        e = jnp.exp(SOFT_CAP * t) * s.ffb[a, 0:TILE, 0:win].astype(F32)
        pr = e * (1.0 / jnp.sum(e, axis=-1, keepdims=True))
        pr = pr.astype(BF)
        s.ps[i] = pr
        s.ts[i] = (1.0 - t * t).astype(BF)
        o = dot32(pr, s.va[ks, :])
        s.att[aligned(a * TILE, TILE), aligned(h * HD, HD)] = o.astype(BF)
        return carry

    lax.fori_loop(0, tiles * heads, attend, 0)

    weights_ready(1)
    s.ao[...] = dot32(s.att[...], s.wo[...])

    def second(rs):
        _, zed, g1 = norm_parts(s.ao[rs], s.gain_ref[1:2])
        h = s.tk[rs].astype(F32) + zed * g1
        s.h1[rs] = h
        _, zed, g1 = norm_parts(h, s.gain_ref[2:3])
        n = zed * g1
        s.xa[rs] = n.astype(BF)
        s.fit[:, rs] = permuted(n)

    per_rows(second)

    weights_ready(2)
    weights_ready(3)
    root = 0.7978845608028654

    def forward(i, carry):
        v, u = lax.div(i, 4), lax.rem(i, 4)
        us = aligned(u * TILE, TILE)
        gt = dot32(s.xa[...], s.wg[v, :, us])
        up = dot32(s.xa[...], s.wu[v, :, us])
        g2 = gt * gt
        th = jnp.tanh(root * gt * (1.0 + 0.044715 * g2))
        lift = 0.5 * (1.0 + th)
        act = gt * lift
        slope = lift + 0.5 * gt * (1.0 - th * th) * (root * (1.0 + 3.0 * 0.044715 * g2))
        s.ffb[v, :, us] = (act * up).astype(BF)
        s.ffb[2 + v, :, us] = (up * slope).astype(BF)
        s.ffb[4 + v, :, us] = act.astype(BF)
        return carry

    lax.fori_loop(0, 8, forward, 0)
    weights_ready(4)
    s.dn[...] = dot32(s.ffb[0], s.wd[:half_ff]) + dot32(s.ffb[1], s.wd[half_ff:])
    s.dg_ref[...] = jnp.zeros_like(s.dg_ref)

    def third(rs):
        dn = s.dn[rs]
        _, zed, g1 = norm_parts(dn, s.gain_ref[3:4])
        s.xa[rs] = (s.h1[rs] + zed * g1).astype(BF)
        dv, dg = norm_back(dn, s.gain_ref[3:4], s.ct[rs].astype(F32))
        s.dg_ref[3:4] += dg
        s.ddn[rs] = dv.astype(BF)
        s.ddnt[:, rs] = permuted(dv)

    cot_in.wait()
    per_rows(third)
    y_far = remote(s.xa, s.y_ref.at[out_rows], s.osend.at[0], s.orecv.at[0], partner)
    y_own = pltpu.make_async_copy(s.xa, s.y_ref.at[out_rows], s.oown.at[0])
    y_far.start()
    y_own.start()

    def part(m, u, width):
        return pl.ds(pl.multiple_of(offs[m] + u * width, 128), width)

    def slot(m, u):
        return lax.rem(u, 2) * 3 + m if m < 3 else (0, 2, 4, 5)[m - 3] + u

    def exchange(m, u, width):
        return remote(
            s.sb.at[slot(m, u), :, :, pl.ds(0, width)],
            s.gb.at[:, :, part(m, u, width)],
            s.csend.at[m, u],
            s.crecv.at[m, u],
            partner,
        )

    def give(m, u, width, value):
        if m < 3:

            @pl.when(u >= 2)
            def _():
                exchange(m, u - 2, width).wait_send()

        s.sb[slot(m, u), :, :, 0:width] = value.astype(BF).reshape(
            IN_COUNT, D // IN_COUNT, width
        )
        exchange(m, u, width).start()

    def keep(m, u, width, value):
        ps = part(m, u, width)
        exchange(m, u, width).wait_recv()
        total = value.reshape(IN_COUNT, D // IN_COUNT, width) + s.gb[:, :, ps].astype(F32)
        s.gb[:, :, ps] = total.astype(BF)

    def ffn_back(v, put):
        def run(u, carry):
            us = aligned(u * TILE, TILE)
            dh = dot_nt(s.ddn[...], s.wd[aligned((v * 4 + u) * TILE, TILE), :])
            dgt = (dh * s.ffb[2 + v, :, us].astype(F32)).astype(BF)
            dup = (dh * s.ffb[4 + v, :, us].astype(F32)).astype(BF)
            s.ffb[2 + v, :, us] = dgt
            s.ffb[4 + v, :, us] = dup
            put(0, u, TILE, dot32(s.ddnt[...], s.ffb[v, :, us]))
            put(1, u, TILE, dot32(s.fit[...], dgt))
            put(2, u, TILE, dot32(s.fit[...], dup))
            return carry

        lax.fori_loop(0, 4, run, 0)

    ffn_back(other, give)
    ffn_back(w, keep)
    s.dn[...] = (
        dot_nt(s.ffb[2], s.wg[0])
        + dot_nt(s.ffb[3], s.wg[1])
        + dot_nt(s.ffb[4], s.wu[0])
        + dot_nt(s.ffb[5], s.wu[1])
    )

    s.buffers_free()

    def fourth(rs):
        dv, dg = norm_back(s.h1[rs], s.gain_ref[2:3], s.dn[rs])
        s.dg_ref[2:3] += dg
        dh = s.ct[rs].astype(F32) + dv
        s.h1[rs] = dh
        dv, dg = norm_back(s.ao[rs], s.gain_ref[1:2], dh)
        s.dg_ref[1:2] += dg
        s.ddn[rs] = dv.astype(BF)
        s.ddnt[:, rs] = permuted(dv)

    per_rows(fourth)
    s.first_sends()
    for m in range(3):
        for u in (2, 3):
            exchange(m, u, TILE).wait_send()

    def out_back(v, put):
        def run(u, carry):
            hs = aligned((v * 2 + u) * HD, HD)
            s.datt[:, hs] = dot_nt(s.ddn[...], s.wo[hs, :]).astype(BF)
            put(3, u, HD, dot32(s.ddnt[...], s.att[:, hs]))
            return carry

        lax.fori_loop(0, 2, run, 0)

    out_back(other, give)
    out_back(w, keep)

    s.dka[...] = jnp.zeros_like(s.dka)
    s.dva[...] = jnp.zeros_like(s.dva)

    def attend_back(i, carry):
        a, h = lax.div(i, heads), lax.rem(i, heads)
        ks = pl.ds(pl.multiple_of(a * TILE, TILE), win)
        qr = aligned(a * TILE, TILE)
        hs = aligned(h * HD, HD)
        do = s.datt[qr, hs]
        pr = s.ps[i]
        s.dva[ks, :] += dot_tn(pr, do)
        dp = dot_nt(do, s.va[ks, :])
        pr = pr.astype(F32)
        inner = jnp.sum(pr * dp, axis=-1, keepdims=True)
        ds = (pr * (dp - inner) * s.ts[i].astype(F32)).astype(BF)
        s.dka[ks, :] += dot_tn(ds, s.qs[i])
        dq = dot32(ds, s.ka[ks, :])
        s.datt[qr, hs] = (turn_back(dq, s.cs[qr], s.sn[qr]) * HD ** (-0.5)).astype(BF)
        return carry

    lax.fori_loop(0, heads, attend_back, 0)
    s.plane_finish(0)
    lax.fori_loop(heads, tiles * heads, attend_back, 0)
    s.plane_finish(1)

    s.dks[0] = s.dka[0:WINDOW, :].astype(BF)
    s.dks[1] = s.dva[0:WINDOW, :].astype(BF)
    d_halo = [
        remote(s.dks.at[i], s.dkr.at[i], s.dsend.at[i], s.drecv.at[i], prev_id) for i in range(2)
    ]

    @pl.when(flat > 0)
    def _():
        for cp in d_halo:
            cp.start()

    def query_back(v, put):
        def run(u, carry):
            hs = aligned((v * 2 + u) * HD, HD)
            put(4, u, HD, dot32(s.xat[...], s.datt[:, hs]))
            return carry

        lax.fori_loop(0, 2, run, 0)

    query_back(other, give)
    s.dn[...] = dot_nt(s.datt[:, : HQ // 2], s.wq[0]) + dot_nt(s.datt[:, HQ // 2 :], s.wq[1])
    query_back(w, keep)
    s.plane_start(3)

    @pl.when(flat < n_dev - 1)
    def _():
        for cp in d_halo:
            cp.wait_recv()

    @pl.when(flat == n_dev - 1)
    def _():
        s.dkr[...] = jnp.zeros_like(s.dkr)

    dk = s.dka[tok:, :] + s.dkr[0].astype(F32)
    s.dkv[0] = turn_back(dk, s.cs[...], s.sn[...]).astype(BF)
    s.dkv[1] = (s.dva[tok:, :] + s.dkr[1].astype(F32)).astype(BF)
    kvw = HD // 2
    for i in range(2):
        give(5 + i, 0, kvw, dot32(s.xat[...], s.dkv[i, :, aligned(other * kvw, kvw)]))
    for i in range(2):
        keep(5 + i, 0, kvw, dot32(s.xat[...], s.dkv[i, :, aligned(w * kvw, kvw)]))
    s.plane_start(4)
    s.dn[...] += dot_nt(s.dkv[0], s.wkv_ref[0]) + dot_nt(s.dkv[1], s.wkv_ref[1])

    def fifth(rs):
        dv, dg = norm_back(s.tk[rs].astype(F32), s.gain_ref[0:1], s.dn[rs])
        s.dg_ref[0:1] += dg
        s.h1[rs] = s.h1[rs] + dv

    per_rows(fifth)
    x_far = remote(s.h1, s.x_ref.at[out_rows], s.osend.at[1], s.orecv.at[1], partner)
    x_own = pltpu.make_async_copy(s.h1, s.x_ref.at[out_rows], s.oown.at[1])
    x_far.start()
    x_own.start()

    def finish():
        for cp in w_far:
            cp.wait_send()

        @pl.when(flat < n_dev - 1)
        def _():
            for cp in halo:
                cp.wait_send()

        @pl.when(flat > 0)
        def _():
            for cp in d_halo:
                cp.wait_send()

        for m, count, width in ((3, 2, HD), (4, 2, HD), (5, 1, kvw), (6, 1, kvw)):
            for u in range(count):
                exchange(m, u, width).wait_send()
        y_own.wait()
        x_own.wait()
        y_far.wait()
        x_far.wait()

    return finish


LAYER_INPUTS = (
    "tok_ref",
    "cot_ref",
    "cosi_ref",
    "sini_ref",
    "mq_ref",
    "mkv_ref",
    "mgu_ref",
    "mo_ref",
    "md_ref",
    "ids_ref",
    "gain_ref",
    "wkv_ref",
    "cosb_ref",
    "sinb_ref",
    "wq_ref",
    "wo_ref",
    "wgu_ref",
    "wd_ref",
)
LAYER_OUTPUTS = ("y_ref", "x_ref", "sum_ref", "nm_ref", "ub", "gs_ref")
VMEM_BYTES = 63 << 20


def whole_kernel(ctx_count, wa_count, names, *refs):
    s = Refs()
    for name, ref in zip(names, refs):
        setattr(s, name, ref)
    c = lax.axis_index("ctx")
    w = lax.axis_index("wa")
    flat = c * wa_count + w
    n_dev = ctx_count * wa_count
    barrier = pltpu.get_barrier_semaphore()

    def greet(i, carry):
        other = lax.rem(flat + i, n_dev)
        pl.semaphore_signal(
            barrier,
            inc=1,
            device_id=(lax.div(other, wa_count), lax.rem(other, wa_count)),
            device_id_type=MESH,
        )
        return carry

    lax.fori_loop(1, n_dev, greet, 0)
    pl.semaphore_wait(barrier, n_dev - 1)
    tail = tail_phases(s, ctx_count, wa_count)
    finish = layer_phases(s, ctx_count, wa_count)
    tail()
    finish()


def rotation_tables(tok, n_dev):
    freq = ROPE_BASE ** (-2.0 * np.arange(HD // 2) / HD)
    inner = np.arange(tok)[:, None] * freq[None, :]
    base = (np.arange(n_dev) * tok)[:, None] * freq[None, :]
    return [jnp.asarray(f(a), F32) for a in (inner, base) for f in (np.cos, np.sin)]


def run_whole(
    tokens, cotangent, seq_ids, gains, wkv, moms, wq, wo, wgu, wd, ctx_count, wa_count
):
    block = tokens.shape[0]
    tok = block // wa_count
    n_dev = ctx_count * wa_count
    mom_query, mom_keyval, mom_out, mom_gateup, mom_down = moms
    cosi, sini, cosb, sinb = rotation_tables(tok, n_dev)
    scratch = layer_scratch(tok) | tail_scratch(ctx_count, wa_count)
    names = LAYER_INPUTS + LAYER_OUTPUTS + tuple(scratch)
    any_space = pl.BlockSpec(memory_space=pl.ANY)
    vmem = pl.BlockSpec(memory_space=pltpu.VMEM)
    cols = layout(wa_count)[2]
    shard = jax.ShapeDtypeStruct((D // ctx_count, cols), F32)
    return pl.pallas_call(
        partial(whole_kernel, ctx_count, wa_count, names),
        out_shape=(
            jax.ShapeDtypeStruct((block, D), BF),
            jax.ShapeDtypeStruct((block, D), F32),
            shard,
            shard,
            jax.ShapeDtypeStruct((-(-(D // ctx_count) // 16) * 16, cols), BF),
            jax.ShapeDtypeStruct((8, 128), F32),
        ),
        in_specs=[any_space] * 9 + [vmem] * 5 + [any_space] * 4,
        out_specs=(any_space, any_space, vmem, vmem, vmem, vmem),
        scratch_shapes=list(scratch.values()),
        compiler_params=pltpu.CompilerParams(
            collective_id=0, has_side_effects=True, vmem_limit_bytes=VMEM_BYTES
        ),
        name="whole",
    )(
        tokens,
        cotangent,
        cosi,
        sini,
        mom_query,
        mom_keyval,
        mom_gateup,
        mom_out.T,
        mom_down.T,
        seq_ids.reshape(wa_count, tok),
        gains,
        wkv,
        cosb,
        sinb,
        wq,
        wo,
        wgu,
        wd,
    )


def format_kernel(
    ctx_count,
    wa_count,
    sum_ref,
    nm_ref,
    ub_ref,
    gs_ref,
    first_ref,
    second_ref,
    y_ref,
    x_ref,
    *rest,
):
    outs, (ubv, gsv, fv, sv, sem) = rest[:21], rest[21:]
    y_out, x_out = outs[:2]
    rows = D // ctx_count
    halves, offs, _ = layout(wa_count)
    late = [
        pltpu.make_async_copy(src, dst, sem.at[i])
        for i, (src, dst) in enumerate(
            ((ub_ref, ubv), (gs_ref, gsv), (first_ref, fv), (second_ref, sv))
        )
    ]

    def places(group):
        query, keyval, out, gateup, down = group
        return (down, gateup.at[0], gateup.at[1], out, query, keyval.at[0], keyval.at[1])

    pairs = [(x_ref, x_out), (y_ref, y_out)]
    for src, group in ((sum_ref, outs[2:7]), (nm_ref, outs[8:13])):
        for m, dst in enumerate(places(group)):
            pairs.append((src.at[:, pl.ds(offs[m], halves[m])], dst))
    copies = [pltpu.make_async_copy(a, b, sem.at[4 + i]) for i, (a, b) in enumerate(pairs)]
    for cp in late + copies:
        cp.start()
    for cp in late:
        cp.wait()
    for m, dst in enumerate(places(outs[13:18])):
        dst[...] = ubv[0:rows, offs[m] : offs[m] + halves[m]].astype(F32)
    g = gsv[0:4, 0:rows]
    first = ADAM_ONE * fv[...] + (1.0 - ADAM_ONE) * g
    second = ADAM_TWO * sv[...] + (1.0 - ADAM_TWO) * g * g
    outs[7][...] = g
    outs[18][...] = first
    outs[19][...] = second
    outs[20][...] = -GAIN_RATE * first / (jnp.sqrt(second) + ADAM_EPS)
    for cp in copies:
        cp.wait()


def run_format(sums, fresh, updates, gsum, gain_first, gain_second, y, x, ctx_count, wa_count):
    rows = D // ctx_count
    halves = layout(wa_count)[0]
    down, gate, _, out, query, key, _ = halves
    f = lambda *shape: jax.ShapeDtypeStruct(shape, F32)
    weights = [f(rows, query), f(2, rows, key), f(rows, out), f(2, rows, gate), f(rows, down)]
    any_space = pl.BlockSpec(memory_space=pl.ANY)
    vmem = pl.BlockSpec(memory_space=pltpu.VMEM)
    gain = f(4, rows)
    shapes = [jax.ShapeDtypeStruct(y.shape, y.dtype), jax.ShapeDtypeStruct(x.shape, x.dtype)]
    shapes += weights + [gain] + weights + weights + [gain] * 3
    outs = pl.pallas_call(
        partial(format_kernel, ctx_count, wa_count),
        out_shape=shapes,
        in_specs=[any_space] * 8,
        out_specs=[any_space] * 7 + [vmem] + [any_space] * 5 + [vmem] * 8,
        scratch_shapes=[
            pltpu.VMEM(updates.shape, updates.dtype),
            pltpu.VMEM(gsum.shape, F32),
            pltpu.VMEM(gain_first.shape, F32),
            pltpu.VMEM(gain_second.shape, F32),
            pltpu.SemaphoreType.DMA((20,)),
        ],
        compiler_params=pltpu.CompilerParams(vmem_limit_bytes=VMEM_BYTES),
        name="format",
    )(sums, fresh, updates, gsum, gain_first, gain_second, y, x)
    return tuple(o.T if i in (4, 6, 10, 12, 15, 17) else o for i, o in enumerate(outs))


def per_device(
    tokens,
    cotangent,
    seq_ids,
    w_query,
    w_keyval,
    w_out,
    w_gateup,
    w_down,
    norm_gains,
    mom_query,
    mom_keyval,
    mom_out,
    mom_gateup,
    mom_down,
    gain_first,
    gain_second,
):
    ctx_count = lax.axis_size("ctx")
    wa_count = lax.axis_size("wa")
    y, x, sums, fresh, updates, gsum = run_whole(
        tokens,
        cotangent,
        seq_ids,
        norm_gains,
        w_keyval,
        (mom_query, mom_keyval, mom_out, mom_gateup, mom_down),
        w_query,
        w_out,
        w_gateup,
        w_down,
        ctx_count,
        wa_count,
    )
    return tuple(
        run_format(
            sums, fresh, updates, gsum, gain_first, gain_second, y, x, ctx_count, wa_count
        )
    )


def solution(mesh):
    in_specs = (
        P("ctx", None),
        P("ctx", None),
        P("ctx"),
        P(None, "wa"),
        P(),
        P("wa", None),
        P(None, None, "wa"),
        P("wa", None),
        P(),
        P("ctx", "wa"),
        P(None, "ctx", "wa"),
        P("wa", "ctx"),
        P(None, "ctx", "wa"),
        P("wa", "ctx"),
        P(None, "ctx"),
        P(None, "ctx"),
    )
    out_specs = (
        P("ctx", None),
        P("ctx", None),
        P("ctx", "wa"),
        P(None, "ctx", "wa"),
        P("wa", "ctx"),
        P(None, "ctx", "wa"),
        P("wa", "ctx"),
        P(None, "ctx"),
        P("ctx", "wa"),
        P(None, "ctx", "wa"),
        P("wa", "ctx"),
        P(None, "ctx", "wa"),
        P("wa", "ctx"),
        P("ctx", "wa"),
        P(None, "ctx", "wa"),
        P("wa", "ctx"),
        P(None, "ctx", "wa"),
        P("wa", "ctx"),
        P(None, "ctx"),
        P(None, "ctx"),
        P(None, "ctx"),
    )
    return jax.shard_map(
        per_device, mesh=mesh, in_specs=in_specs, out_specs=out_specs, check_vma=False
    )
```

time: 265 us -> 361 us (1.36)
  Pallas kernels: 242 us -> 359 us
  local copies, waits for them, and re-layouts: 16.1 us -> 1.29 us
  other arithmetic: 5.48 us -> 0 us
    pallas_call x2, Pallas kernels: 242 us -> 359 us  [the longest x1 196 us: run_whole(): pl.pallas_call(partial(whole_kernel, ctx_count, wa_count, names), out_sha...]
    unnamed x24 -> x0, local copies, waits for them, and re-layouts: 8.32 us -> none
    transpose x4 -> x0, local copies, waits for them, and re-layouts: 4.93 us -> none  [unstack(): return (query, jnp.stack([key, value]), out.T, jnp.stack([gate, up]), dow...]
    another operation x6 -> x0, other arithmetic: 4.1 us -> none  [the longest x3 2.24 us: unstack(): jnp.stack([gate, up])]
where the time goes in v3:
time: 361 us
  Pallas kernels  359 us (99%)
    pallas_call x1, Pallas kernels, run_whole(): pl.pallas_call(partial(whole_kernel, ctx_count, wa_count, names), out_sha...  196 us
    pallas_call x1, Pallas kernels, run_format(): pl.pallas_call(partial(format_kernel, ctx_count, wa_count), out_shape=sha...  163 us

profile of v3, /device:TPU:15, one launch (start us, length us, event | category | flops | bytes accessed | tf_op | source)
XLA Modules:
  0.0 361.1 jit_solution(5461610466096422679)
XLA Ops:
  0.7 1.3 reshape.45.refs_9_
  1.9 195.5 %whole.1 = (bf16[1024,640]{1,0:T(8,128)(2,1)}, f32[1024,640]{1,0:T(8,128)}, f32[40,4352]{1,0:T(8,128)}, f32[40,4352]{1,0:T(8,128)}, bf16[48,4352]{1,0:T(8,128)(2,1)}, /*index=5*/f32[8,128]{1,0:T(8,128)}) custom-call(bf16[1024,640]{1,0:T(8,128)(2,1)} %refs_0_.1, bf16[1024,640]{1,0:T(8,128)(2,1)} %refs_1_.1, f32[512,128]{1,0:T(8,128)} %constant.8.clone.refs_2_, ...), custom_call_target="tpu_custom_call" | custom-call | tf_op jit(solution)/shard_map/whole/pallas_call | solution.py:1067
  197.5 163.5 %format.1 = (bf16[1024,640]{1,0:T(8,128)(2,1)}, f32[1024,640]{1,0:T(8,128)}, f32[40,512]{1,0:T(8,128)}, f32[2,40,128]{2,1,0:T(8,128)}, f32[40,512]{1,0:T(8,128)}...) custom-call(f32[40,4352]{1,0:T(8,128)} %get-tuple-element.48.sum_ref, ...), custom_call_target="tpu_custom_call" | custom-call | tf_op jit(solution)/shard_map/format/pallas_call | solution.py:1167

commit v4 on v3

--- a/solution.py
+++ b/solution.py
@@ -1116,29 +1116,47 @@
     x_ref,
     *rest,
 ):
-    outs, (ubv, gsv, fv, sv, sem) = rest[:21], rest[21:]
-    y_out, x_out = outs[:2]
+    outs, (sumv, nmv, ubv, gsv, fv, sv, yv, xv, sem) = rest[:21], rest[21:]
     rows = D // ctx_count
     halves, offs, _ = layout(wa_count)
-    late = [
-        pltpu.make_async_copy(src, dst, sem.at[i])
-        for i, (src, dst) in enumerate(
-            ((ub_ref, ubv), (gs_ref, gsv), (first_ref, fv), (second_ref, sv))
-        )
-    ]
+
+    def copies(pairs, first):
+        return [pltpu.make_async_copy(a, b, sem.at[first + i]) for i, (a, b) in enumerate(pairs)]
 
     def places(group):
         query, keyval, out, gateup, down = group
         return (down, gateup.at[0], gateup.at[1], out, query, keyval.at[0], keyval.at[1])
 
-    pairs = [(x_ref, x_out), (y_ref, y_out)]
-    for src, group in ((sum_ref, outs[2:7]), (nm_ref, outs[8:13])):
-        for m, dst in enumerate(places(group)):
-            pairs.append((src.at[:, pl.ds(offs[m], halves[m])], dst))
-    copies = [pltpu.make_async_copy(a, b, sem.at[4 + i]) for i, (a, b) in enumerate(pairs)]
-    for cp in late + copies:
+    fetched = copies(
+        (
+            (x_ref, xv),
+            (y_ref, yv),
+            (sum_ref, sumv),
+            (nm_ref, nmv),
+            (ub_ref, ubv),
+            (gs_ref, gsv),
+            (first_ref, fv),
+            (second_ref, sv),
+        ),
+        0,
+    )
+    for cp in fetched:
         cp.start()
-    for cp in late:
+    stored = copies(((xv, outs[1]), (yv, outs[0])), 8)
+    for src, group, first in ((sumv, outs[2:7], 10), (nmv, outs[8:13], 17)):
+        stored += copies(
+            [
+                (src.at[:, pl.ds(offs[m], halves[m])], dst)
+                for m, dst in enumerate(places(group))
+            ],
+            first,
+        )
+    starts = ((0, 1), (1, 2), (2, 9), (9, 16))
+    for cp, (a, b) in zip(fetched[:4], starts):
+        cp.wait()
+        for out in stored[a:b]:
+            out.start()
+    for cp in fetched[4:]:
         cp.wait()
     for m, dst in enumerate(places(outs[13:18])):
         dst[...] = ubv[0:rows, offs[m] : offs[m] + halves[m]].astype(F32)
@@ -1149,7 +1167,7 @@
     outs[18][...] = first
     outs[19][...] = second
     outs[20][...] = -GAIN_RATE * first / (jnp.sqrt(second) + ADAM_EPS)
-    for cp in copies:
+    for cp in stored:
         cp.wait()
 
 
@@ -1170,11 +1188,11 @@
         in_specs=[any_space] * 8,
         out_specs=[any_space] * 7 + [vmem] + [any_space] * 5 + [vmem] * 8,
         scratch_shapes=[
-            pltpu.VMEM(updates.shape, updates.dtype),
-            pltpu.VMEM(gsum.shape, F32),
-            pltpu.VMEM(gain_first.shape, F32),
-            pltpu.VMEM(gain_second.shape, F32),
-            pltpu.SemaphoreType.DMA((20,)),
+            *[
+                pltpu.VMEM(a.shape, a.dtype)
+                for a in (sums, fresh, updates, gsum, gain_first, gain_second, y, x)
+            ],
+            pltpu.SemaphoreType.DMA((24,)),
         ],
         compiler_params=pltpu.CompilerParams(vmem_limit_bytes=VMEM_BYTES),
         name="format",

time: 361 us -> 203 us (0.56)
  Pallas kernels: 359 us -> 201 us
    pallas_call x1, Pallas kernels: 163 us -> 5.15 us  [run_format(): pl.pallas_call(partial(format_kernel, ctx_count, wa_count), out_shape=sha...]
where the time goes in v4:
time: 203 us
  Pallas kernels  201 us (99%)
    pallas_call x1, Pallas kernels, run_whole(): pl.pallas_call(partial(whole_kernel, ctx_count, wa_count, names), out_sha...  196 us
    pallas_call x1, Pallas kernels, run_format(): pl.pallas_call(partial(format_kernel, ctx_count, wa_count), out_shape=sha...  5.15 us

profile of v4, /device:TPU:15, one launch (start us, length us, event | category | flops | bytes accessed | tf_op | source)
XLA Modules:
  0.0 202.8 jit_solution(14423924036361258222)
XLA Ops:
  0.7 1.3 reshape.45.refs_9_
  1.9 195.5 %whole.1 = (bf16[1024,640]{1,0:T(8,128)(2,1)}, f32[1024,640]{1,0:T(8,128)}, f32[40,4352]{1,0:T(8,128)}, f32[40,4352]{1,0:T(8,128)}, bf16[48,4352]{1,0:T(8,128)(2,1)}, /*index=5*/f32[8,128]{1,0:T(8,128)}) custom-call(bf16[1024,640]{1,0:T(8,128)(2,1)} %refs_0_.1, bf16[1024,640]{1,0:T(8,128)(2,1)} %refs_1_.1, f32[512,128]{1,0:T(8,128)} %constant.8.clone.refs_2_, ...), custom_call_target="tpu_custom_call" | custom-call | tf_op jit(solution)/shard_map/whole/pallas_call | solution.py:1067
  197.5 5.2 %format.1 = (bf16[1024,640]{1,0:T(8,128)(2,1)}, f32[1024,640]{1,0:T(8,128)}, f32[40,512]{1,0:T(8,128)}, f32[2,40,128]{2,1,0:T(8,128)}, f32[40,512]{1,0:T(8,128)}...) custom-call(f32[40,4352]{1,0:T(8,128)} %get-tuple-element.48.sum_ref, ...), custom_call_target="tpu_custom_call" | custom-call | tf_op jit(solution)/shard_map/format/pallas_call | solution.py:1185

commit v5 on v4

--- a/solution.py
+++ b/solution.py
@@ -38,7 +38,17 @@
 NAMES = ("down", "gate", "up", "out", "query", "key", "value")
 WIDTHS = (FF, FF, FF, HQ, HQ, HD, HD)
 OWNERS = (7, 4, 8, 5, 11, 9, 10)
-CHUNK_SETS = ((0,), (1,), (2,), (3, 4), (5, 6))
+PARTS = (
+    ((0, 0, 512),),
+    ((0, 512, 512),),
+    ((1, 0, 512),),
+    ((1, 512, 512),),
+    ((2, 0, 512),),
+    ((2, 512, 512),),
+    ((3, 0, 512),),
+    ((4, 0, 512),),
+    ((5, 0, 128), (6, 0, 128)),
+)
 TILE = 256
 
 
@@ -95,26 +105,28 @@
     rows = D // ctx_count
     rp = -(-rows // 16) * 16
     n_dev = ctx_count * wa_count
-    n_ch = len(CHUNK_SETS)
+    n_ch = len(PARTS)
     cols = layout(wa_count)[2]
     return dict(
         mb=v((rp, cols), BF),
+        early=v((6, D // n_in, 512), BF),
         xb=v((ctx_count, rp, FF), BF),
         am=v((D, D), F32),
         dg_ref=v((8, D), F32),
         dgs=v((ctx_count, 8, 128), F32),
         dgr=v((n_dev, 8, 128), F32),
-        psend=dma((n_ch, n_in - 1)),
-        precv=dma((n_ch, n_in - 1)),
+        psend=dma((n_ch, 3)),
+        precv=dma((n_ch, 3)),
         lsend=dma((n_ch, n_out - 1)),
         lrecv=dma((n_ch, n_out - 1)),
-        gsend=dma((MATRIX_COUNT,)),
+        gsend=dma((n_ch, 2)),
         grecv=dma,
         usend=dma((n_dev,)),
         urecv=dma((MATRIX_COUNT,)),
         gnsend=dma((n_dev,)),
         gnrecv=dma,
         msem=dma((MATRIX_COUNT,)),
+        dfree=pltpu.SemaphoreType.REGULAR,
         pfree=pltpu.SemaphoreType.REGULAR,
         lfree=pltpu.SemaphoreType.REGULAR,
     )
@@ -132,32 +144,43 @@
     rp = s.xb.shape[1]
     block = D // n_in
     halves, offs, cols = layout(wa_count)
-    chunks = [(offs[m[0]], sum(halves[i] for i in m)) for m in CHUNK_SETS]
+    chunks = [(offs[m[0][0]] + m[0][1], sum(i[2] for i in m)) for m in PARTS]
     me = c * wa_count + w
     per = ctx_count // 2
 
+    near = (p + 1 - 2 * lax.rem(p, 2), p + 2 - 4 * lax.div(p, 2))
+    across = 3 - p
+
     def plane_slot(ci, k):
-        i = min(ci, 4) * (n_in - 1) + (k - 1 if ci < 4 else 0)
-        buf = (s.wg, s.wu)[i // 8]
-        lanes = pl.ds(0, chunks[ci][1]) if ci < 4 else pl.ds((k - 1) * TILE, TILE)
-        return buf.at[i % 8 // 4, pl.ds(i % 4 * block, block), lanes]
+        lanes = chunks[ci][1]
+        if ci < 2:
+            return s.early.at[ci * 3 + k]
+        if ci < 4:
+            return s.wd.at[pl.ds(((ci - 2) * 3 + k) * block, block), pl.ds(0, lanes)]
+        i = (ci - 4) * 3 + k
+        buf = (s.wg, s.wu)[i // 16]
+        i = i % 16
+        return buf.at[i // 8, pl.ds(i % 8 // 2 * block, block), pl.ds(i % 2 * 512, lanes)]
 
     def line_slot(base, ci, j):
         wid = chunks[ci][1]
-        if ci < 4:
-            start = ci % 2 * 256 + j * rp
-            return s.ffb.at[base * 2 + ci // 2, pl.ds(pl.multiple_of(start, 16), rp), pl.ds(0, wid)]
-        return s.ffb.at[4 + base, pl.ds(pl.multiple_of(j * rp, 16), rp), pl.ds(0, wid)]
+        if ci < 8:
+            start = ci % 4 // 2 * 256 + j * rp
+            page, lane = base * 2 + ci // 4, ci % 2 * 512
+        else:
+            start, page, lane = j * rp, 4 + base, 0
+        return s.ffb.at[page, pl.ds(pl.multiple_of(start, 16), rp), pl.ds(lane, wid)]
 
     def plane_copy(ci, k):
         off, wid = chunks[ci]
-        q = lax.rem(p + k, n_in)
+        first, second = near[ci % 2], near[1 - ci % 2]
+        src, dst = ((first, first), (across, first), (second, second))[k]
         return pltpu.make_async_remote_copy(
-            s.gb.at[q, :, pl.ds(off, wid)],
+            s.gb.at[src, :, pl.ds(off, wid)],
             plane_slot(ci, k),
-            s.psend.at[ci, k - 1],
-            s.precv.at[ci, k - 1],
-            device_id=(z * n_in + q, w),
+            s.psend.at[ci, k],
+            s.precv.at[ci, k],
+            device_id=(z * n_in + dst, w),
             device_id_type=MESH,
         )
 
@@ -172,14 +195,15 @@
             device_id_type=MESH,
         )
 
+    def tell_plane(sem):
+        for q in near:
+            pl.semaphore_signal(sem, inc=1, device_id=(z * n_in + q, w), device_id_type=MESH)
+
+    def down_free():
+        tell_plane(s.dfree)
+
     def buffers_free():
-        for k in range(1, n_in):
-            pl.semaphore_signal(
-                s.pfree,
-                inc=1,
-                device_id=(z * n_in + lax.rem(p + k, n_in), w),
-                device_id_type=MESH,
-            )
+        tell_plane(s.pfree)
         for k in range(1, n_out):
             pl.semaphore_signal(
                 s.lfree,
@@ -189,24 +213,38 @@
             )
 
     def plane_start(ci):
-        for k in range(1, n_in):
-            plane_copy(ci, k).start()
-
-    def first_sends():
-        pl.semaphore_wait(s.pfree, n_in - 1)
-        for ci in range(3):
-            plane_start(ci)
+        if ci == 2:
+            pl.semaphore_wait(s.dfree, 2)
+        if ci == 4:
+            pl.semaphore_wait(s.pfree, 2)
+        plane_copy(ci, 1).start()
+        plane_copy(ci, 0).start()
+
+    def plane_mid(ci):
+        off, wid = chunks[ci]
+        second = near[1 - ci % 2]
+        plane_copy(ci, 1).wait_recv()
+
+        def add(t, carry):
+            cs = aligned(off + t * TILE, TILE)
+            here = aligned(t * TILE, TILE)
+            both = s.gb[second, :, cs].astype(F32) + plane_slot(ci, 1)[:, here].astype(F32)
+            s.gb[second, :, cs] = both.astype(BF)
+            return carry
+
+        lax.fori_loop(0, wid // TILE, add, 0)
+        plane_copy(ci, 2).start()
 
     def plane_finish(ci):
         off, wid = chunks[ci]
-        for k in range(1, n_in):
-            plane_copy(ci, k).wait_recv()
+        plane_copy(ci, 0).wait_recv()
+        plane_copy(ci, 2).wait_recv()
 
         def plane_sum(t, carry):
             cs = aligned(off + t * TILE, TILE)
             here = aligned(t * TILE, TILE)
             total = s.gb[p, :, cs].astype(F32)
-            for k in range(1, n_in):
+            for k in (0, 2):
                 total = total + plane_slot(ci, k)[:, here].astype(F32)
             for j in range(n_out):
                 slab = total[j * rows : (j + 1) * rows]
@@ -224,13 +262,19 @@
         for k in range(1, n_out):
             line_copy(ci, k).start()
 
-    def gather_copy(m, local):
-        src = s.mb.at[:, pl.ds(offs[m], halves[m])]
-        dst = s.xb.at[c, :, pl.ds(pl.multiple_of(w * halves[m], 128), halves[m])]
+    def gather_copy(ci, i, local):
+        m, first, wid = PARTS[ci][i]
+        src = s.mb.at[:, pl.ds(offs[m] + first, wid)]
+        dst = s.xb.at[c, :, pl.ds(pl.multiple_of(w * halves[m] + first, 128), wid)]
         if local:
             return pltpu.make_async_copy(src, dst, s.grecv)
         return pltpu.make_async_remote_copy(
-            src, dst, s.gsend.at[m], s.grecv, device_id=(OWNERS[m], 0), device_id_type=MESH
+            src,
+            dst,
+            s.gsend.at[ci, i],
+            s.grecv,
+            device_id=(OWNERS[m], 0),
+            device_id_type=MESH,
         )
 
     def line_finish(ci):
@@ -251,20 +295,21 @@
             return carry
 
         lax.fori_loop(0, wid // TILE, line_sum, 0)
-        for m in CHUNK_SETS[ci]:
-            mine = me == OWNERS[m] * wa_count
+        for i, piece in enumerate(PARTS[ci]):
+            mine = me == OWNERS[piece[0]] * wa_count
 
             @pl.when(mine)
             def _():
-                gather_copy(m, True).start()
+                gather_copy(ci, i, True).start()
 
             @pl.when(jnp.logical_not(mine))
             def _():
-                gather_copy(m, False).start()
-
+                gather_copy(ci, i, False).start()
+
+    s.down_free = down_free
     s.buffers_free = buffers_free
-    s.first_sends = first_sends
     s.plane_start = plane_start
+    s.plane_mid = plane_mid
     s.plane_finish = plane_finish
 
     sources = (
@@ -308,18 +353,23 @@
 
         for cp in moms:
             cp.wait()
-        plane_finish(2)
+        plane_mid(7)
+        plane_mid(8)
         line_finish(0)
         line_finish(1)
-        plane_finish(3)
-        plane_finish(4)
+        plane_finish(6)
         line_finish(2)
+        line_finish(3)
+        plane_finish(7)
+        plane_finish(8)
+        line_finish(4)
+        line_finish(5)
         pltpu.make_async_copy(s.dgs.at[c], s.dgr.at[me], s.gnrecv).start()
         lax.fori_loop(1, n_dev, gain_send, 0)
-        line_finish(3)
-        line_finish(4)
+        for ci in range(6, 9):
+            line_finish(ci)
         for ci in range(len(chunks)):
-            for k in range(1, n_in):
+            for k in range(3):
                 plane_copy(ci, k).wait_send()
             for k in range(1, n_out):
                 line_copy(ci, k).wait_send()
@@ -489,7 +539,10 @@
 
             @pl.when(me != owner)
             def _(m=m):
-                gather_copy(m, False).wait_send()
+                for ci, part in enumerate(PARTS):
+                    for i, piece in enumerate(part):
+                        if piece[0] == m:
+                            gather_copy(ci, i, False).wait_send()
 
             @pl.when(me == owner)
             def _(m=m, owner=owner):
@@ -577,8 +630,8 @@
         wown=dma((5,)),
         ksend=dma((3,)),
         krecv=dma((3,)),
-        dsend=dma((2,)),
-        drecv=dma((2,)),
+        dsend=dma((2, 2)),
+        drecv=dma((2, 2)),
         csend=dma((MATRIX_COUNT, 4)),
         crecv=dma((MATRIX_COUNT, 4)),
         osend=dma((2,)),
@@ -660,9 +713,7 @@
     def first(rs):
         x = s.tk[rs].astype(F32)
         _, zed, g1 = norm_parts(x, s.gain_ref[0:1])
-        n = zed * g1
-        s.xa[rs] = n.astype(BF)
-        s.xat[:, rs] = permuted(n)
+        s.xa[rs] = (zed * g1).astype(BF)
 
     per_rows(first)
 
@@ -683,19 +734,31 @@
         return jnp.concatenate([a * cosine + b * sine, b * cosine - a * sine], axis=1)
 
     s.ka[WINDOW:, :] = turn(dot32(s.xa[...], s.wkv_ref[0]), s.cs[...], s.sn[...]).astype(BF)
-    s.va[WINDOW:, :] = dot32(s.xa[...], s.wkv_ref[1]).astype(BF)
     s.idown[...] = jnp.broadcast_to(s.ids_ref[pl.ds(w, 1), :], (8, tok))
-
     halo = [
-        remote(s.ka.at[pl.ds(tok, WINDOW)], s.ka.at[pl.ds(0, WINDOW)], s.ksend.at[0], s.krecv.at[0], next_id),
-        remote(s.va.at[pl.ds(tok, WINDOW)], s.va.at[pl.ds(0, WINDOW)], s.ksend.at[1], s.krecv.at[1], next_id),
-        remote(s.idown, s.idprev, s.ksend.at[2], s.krecv.at[2], next_id),
+        remote(src, dst, s.ksend.at[i], s.krecv.at[i], next_id)
+        for i, (src, dst) in enumerate(
+            (
+                (s.ka.at[pl.ds(tok, WINDOW)], s.ka.at[pl.ds(0, WINDOW)]),
+                (s.va.at[pl.ds(tok, WINDOW)], s.va.at[pl.ds(0, WINDOW)]),
+                (s.idown, s.idprev),
+            )
+        )
     ]
 
     @pl.when(flat < n_dev - 1)
     def _():
-        for cp in halo:
-            cp.start()
+        halo[2].start()
+        halo[0].start()
+
+    s.va[WINDOW:, :] = dot32(s.xa[...], s.wkv_ref[1]).astype(BF)
+
+    @pl.when(flat < n_dev - 1)
+    def _():
+        halo[1].start()
+
+    def flip(rs):
+        s.xat[:, rs] = permuted(s.xa[rs])
 
     weights_ready(0)
 
@@ -708,6 +771,7 @@
         return carry
 
     lax.fori_loop(0, heads, project, 0)
+    per_rows(flip)
 
     @pl.when(flat > 0)
     def _():
@@ -832,7 +896,14 @@
         total = value.reshape(IN_COUNT, D // IN_COUNT, width) + s.gb[:, :, ps].astype(F32)
         s.gb[:, :, ps] = total.astype(BF)
 
-    def ffn_back(v, put):
+    def down_back(v, put):
+        def run(u, carry):
+            put(0, u, TILE, dot32(s.ddnt[...], s.ffb[v, :, aligned(u * TILE, TILE)]))
+            return carry
+
+        lax.fori_loop(0, 4, run, 0)
+
+    def gate_back(v, put):
         def run(u, carry):
             us = aligned(u * TILE, TILE)
             dh = dot_nt(s.ddn[...], s.wd[aligned((v * 4 + u) * TILE, TILE), :])
@@ -840,21 +911,25 @@
             dup = (dh * s.ffb[4 + v, :, us].astype(F32)).astype(BF)
             s.ffb[2 + v, :, us] = dgt
             s.ffb[4 + v, :, us] = dup
-            put(0, u, TILE, dot32(s.ddnt[...], s.ffb[v, :, us]))
             put(1, u, TILE, dot32(s.fit[...], dgt))
             put(2, u, TILE, dot32(s.fit[...], dup))
             return carry
 
         lax.fori_loop(0, 4, run, 0)
 
-    ffn_back(other, give)
-    ffn_back(w, keep)
-    s.dn[...] = (
-        dot_nt(s.ffb[2], s.wg[0])
-        + dot_nt(s.ffb[3], s.wg[1])
-        + dot_nt(s.ffb[4], s.wu[0])
-        + dot_nt(s.ffb[5], s.wu[1])
-    )
+    down_back(other, give)
+    down_back(w, keep)
+    s.plane_start(0)
+    s.plane_start(1)
+    gate_back(other, give)
+    gate_back(w, keep)
+    s.down_free()
+    s.dn[...] = dot_nt(s.ffb[2], s.wg[0]) + dot_nt(s.ffb[3], s.wg[1])
+    s.plane_mid(0)
+    s.plane_mid(1)
+    s.plane_start(2)
+    s.plane_start(3)
+    s.dn[...] += dot_nt(s.ffb[4], s.wu[0]) + dot_nt(s.ffb[5], s.wu[1])
 
     s.buffers_free()
 
@@ -869,7 +944,8 @@
         s.ddnt[:, rs] = permuted(dv)
 
     per_rows(fourth)
-    s.first_sends()
+    s.plane_start(4)
+    s.plane_start(5)
     for m in range(3):
         for u in (2, 3):
             exchange(m, u, TILE).wait_send()
@@ -885,6 +961,8 @@
 
     out_back(other, give)
     out_back(w, keep)
+    s.plane_finish(0)
+    s.plane_finish(1)
 
     s.dka[...] = jnp.zeros_like(s.dka)
     s.dva[...] = jnp.zeros_like(s.dva)
@@ -906,21 +984,31 @@
         s.datt[qr, hs] = (turn_back(dq, s.cs[qr], s.sn[qr]) * HD ** (-0.5)).astype(BF)
         return carry
 
+    def d_part(i, half):
+        rs = pl.ds(half * TILE, TILE)
+        return remote(
+            s.dks.at[i, rs], s.dkr.at[i, rs], s.dsend.at[i, half], s.drecv.at[i, half], prev_id
+        )
+
+    d_halo = [d_part(i, half) for half in range(2) for i in range(2)]
+
+    def d_send(half):
+        rs = slice(half * TILE, (half + 1) * TILE)
+        s.dks[0, rs] = s.dka[rs].astype(BF)
+        s.dks[1, rs] = s.dva[rs].astype(BF)
+
+        @pl.when(flat > 0)
+        def _():
+            for cp in d_halo[half * 2 : half * 2 + 2]:
+                cp.start()
+
     lax.fori_loop(0, heads, attend_back, 0)
-    s.plane_finish(0)
+    d_send(0)
+    s.plane_mid(2)
+    s.plane_mid(3)
+    s.plane_start(6)
     lax.fori_loop(heads, tiles * heads, attend_back, 0)
-    s.plane_finish(1)
-
-    s.dks[0] = s.dka[0:WINDOW, :].astype(BF)
-    s.dks[1] = s.dva[0:WINDOW, :].astype(BF)
-    d_halo = [
-        remote(s.dks.at[i], s.dkr.at[i], s.dsend.at[i], s.drecv.at[i], prev_id) for i in range(2)
-    ]
-
-    @pl.when(flat > 0)
-    def _():
-        for cp in d_halo:
-            cp.start()
+    d_send(1)
 
     def query_back(v, put):
         def run(u, carry):
@@ -931,9 +1019,13 @@
         lax.fori_loop(0, 2, run, 0)
 
     query_back(other, give)
+    s.plane_mid(4)
+    s.plane_mid(5)
     s.dn[...] = dot_nt(s.datt[:, : HQ // 2], s.wq[0]) + dot_nt(s.datt[:, HQ // 2 :], s.wq[1])
     query_back(w, keep)
-    s.plane_start(3)
+    s.plane_start(7)
+    s.plane_finish(2)
+    s.plane_finish(3)
 
     @pl.when(flat < n_dev - 1)
     def _():
@@ -952,7 +1044,10 @@
         give(5 + i, 0, kvw, dot32(s.xat[...], s.dkv[i, :, aligned(other * kvw, kvw)]))
     for i in range(2):
         keep(5 + i, 0, kvw, dot32(s.xat[...], s.dkv[i, :, aligned(w * kvw, kvw)]))
-    s.plane_start(4)
+    s.plane_start(8)
+    s.plane_mid(6)
+    s.plane_finish(4)
+    s.plane_finish(5)
     s.dn[...] += dot_nt(s.dkv[0], s.wkv_ref[0]) + dot_nt(s.dkv[1], s.wkv_ref[1])
 
     def fifth(rs):

time: 203 us -> 185 us (0.911)
  Pallas kernels: 201 us -> 183 us
    pallas_call x1, Pallas kernels: 196 us -> 178 us  [run_whole(): pl.pallas_call(partial(whole_kernel, ctx_count, wa_count, names), out_sha...]
where the time goes in v5:
time: 185 us
  Pallas kernels  183 us (99%)
    pallas_call x1, Pallas kernels, run_whole(): pl.pallas_call(partial(whole_kernel, ctx_count, wa_count, names), out_sha...  178 us
    pallas_call x1, Pallas kernels, run_format(): pl.pallas_call(partial(format_kernel, ctx_count, wa_count), out_shape=sha...  5.15 us

profile of v5, /device:TPU:15, one launch (start us, length us, event | category | flops | bytes accessed | tf_op | source)
XLA Modules:
  0.0 184.9 jit_solution(15917565687318335339)
XLA Ops:
  0.7 1.3 reshape.45.refs_9_
  1.9 177.7 %whole.1 = (bf16[1024,640]{1,0:T(8,128)(2,1)}, f32[1024,640]{1,0:T(8,128)}, f32[40,4352]{1,0:T(8,128)}, f32[40,4352]{1,0:T(8,128)}, bf16[48,4352]{1,0:T(8,128)(2,1)}, /*index=5*/f32[8,128]{1,0:T(8,128)}) custom-call(bf16[1024,640]{1,0:T(8,128)(2,1)} %refs_0_.1, bf16[1024,640]{1,0:T(8,128)(2,1)} %refs_1_.1, f32[512,128]{1,0:T(8,128)} %constant.8.clone.refs_2_, ...), custom_call_target="tpu_custom_call" | custom-call | tf_op jit(solution)/shard_map/whole/pallas_call | solution.py:1162
  179.6 5.2 %format.1 = (bf16[1024,640]{1,0:T(8,128)(2,1)}, f32[1024,640]{1,0:T(8,128)}, f32[40,512]{1,0:T(8,128)}, f32[2,40,128]{2,1,0:T(8,128)}, f32[40,512]{1,0:T(8,128)}...) custom-call(f32[40,4352]{1,0:T(8,128)} %get-tuple-element.48.sum_ref, ...), custom_call_target="tpu_custom_call" | custom-call | tf_op jit(solution)/shard_map/format/pallas_call | solution.py:1280

commit v6 on v5

--- a/solution.py
+++ b/solution.py
@@ -74,6 +74,19 @@
     return jnp.concatenate([v, jnp.zeros((rows - v.shape[0], v.shape[1]), v.dtype)], axis=0)
 
 
+def packed_rows(rows):
+    return -(-2 * rows // 16) * 16
+
+
+def pack(left, right, height):
+    return pad_rows(jnp.concatenate([left, right], axis=0), height).astype(BF)
+
+
+def unpack(block, rows):
+    block = block.astype(F32)
+    return block[:rows], block[rows : 2 * rows]
+
+
 def split_into(v, hi, lo):
     top = v.astype(BF)
     hi[...] = top
@@ -106,15 +119,20 @@
     rp = -(-rows // 16) * 16
     n_dev = ctx_count * wa_count
     n_ch = len(PARTS)
+    hp = packed_rows(rows)
     cols = layout(wa_count)[2]
     return dict(
-        mb=v((rp, cols), BF),
+        mb=v((8, hp, 256), BF),
+        mbk=v((2, rp, HD // 2), BF),
         early=v((6, D // n_in, 512), BF),
-        xb=v((ctx_count, rp, FF), BF),
+        xb=v((ctx_count, 4, hp, 256), BF),
         am=v((D, D), F32),
         dg_ref=v((8, D), F32),
-        dgs=v((ctx_count, 8, 128), F32),
-        dgr=v((n_dev, 8, 128), F32),
+        dgs=v((n_in, n_out, 8, 128), F32),
+        dgc=v((n_in, n_out, 8, 128), F32),
+        dgp=v((3, n_out, 8, 128), F32),
+        dgo=v((n_out, 8, 128), F32),
+        dgl=v((n_out - 1, 8, 128), F32),
         psend=dma((n_ch, 3)),
         precv=dma((n_ch, 3)),
         lsend=dma((n_ch, n_out - 1)),
@@ -123,8 +141,12 @@
         grecv=dma,
         usend=dma((n_dev,)),
         urecv=dma((MATRIX_COUNT,)),
-        gnsend=dma((n_dev,)),
-        gnrecv=dma,
+        gcsend=dma,
+        gcrecv=dma,
+        gpsend=dma((3,)),
+        gprecv=dma((3,)),
+        glsend=dma((n_out - 1,)),
+        glrecv=dma((n_out - 1,)),
         msem=dma((MATRIX_COUNT,)),
         dfree=pltpu.SemaphoreType.REGULAR,
         pfree=pltpu.SemaphoreType.REGULAR,
@@ -141,12 +163,13 @@
     p = lax.rem(c, n_in)
     z = lax.div(c, n_in)
     rows = D // ctx_count
-    rp = s.xb.shape[1]
+    rp = s.mbk.shape[1]
+    hp = packed_rows(rows)
     block = D // n_in
     halves, offs, cols = layout(wa_count)
     chunks = [(offs[m[0][0]] + m[0][1], sum(i[2] for i in m)) for m in PARTS]
     me = c * wa_count + w
-    per = ctx_count // 2
+    per = 512 // hp
 
     near = (p + 1 - 2 * lax.rem(p, 2), p + 2 - 4 * lax.div(p, 2))
     across = 3 - p
@@ -163,13 +186,9 @@
         return buf.at[i // 8, pl.ds(i % 8 // 2 * block, block), pl.ds(i % 2 * 512, lanes)]
 
     def line_slot(base, ci, j):
-        wid = chunks[ci][1]
-        if ci < 8:
-            start = ci % 4 // 2 * 256 + j * rp
-            page, lane = base * 2 + ci // 4, ci % 2 * 512
-        else:
-            start, page, lane = j * rp, 4 + base, 0
-        return s.ffb.at[page, pl.ds(pl.multiple_of(start, 16), rp), pl.ds(lane, wid)]
+        half = chunks[ci][1] // 2
+        page, lane = (base * 2 + ci // 4, ci % 4 * 256) if ci < 8 else (4 + base, 0)
+        return s.ffb.at[page, pl.ds(pl.multiple_of(j * hp, 16), hp), pl.ds(lane, half)]
 
     def plane_copy(ci, k):
         off, wid = chunks[ci]
@@ -240,23 +259,18 @@
         plane_copy(ci, 0).wait_recv()
         plane_copy(ci, 2).wait_recv()
 
-        def plane_sum(t, carry):
-            cs = aligned(off + t * TILE, TILE)
-            here = aligned(t * TILE, TILE)
-            total = s.gb[p, :, cs].astype(F32)
-            for k in (0, 2):
-                total = total + plane_slot(ci, k)[:, here].astype(F32)
-            for j in range(n_out):
-                slab = total[j * rows : (j + 1) * rows]
-
-                @pl.when(z == j)
-                def _():
-                    s.sum_ref[:, cs] = slab
-
-                line_slot(0, ci, j)[:, here] = pad_rows(slab, rp).astype(BF)
-            return carry
-
-        lax.fori_loop(0, wid // TILE, plane_sum, 0)
+        half = wid // 2
+        total = s.gb[p, :, off : off + wid].astype(F32)
+        for k in (0, 2):
+            total = total + plane_slot(ci, k)[...].astype(F32)
+        for j in range(n_out):
+            slab = total[j * rows : (j + 1) * rows]
+
+            @pl.when(z == j)
+            def _():
+                s.sum_ref[:, off : off + wid] = slab
+
+            line_slot(0, ci, j)[...] = pack(slab[:, :half], slab[:, half:], hp)
         if ci == 0:
             pl.semaphore_wait(s.lfree, n_out - 1)
         for k in range(1, n_out):
@@ -264,8 +278,12 @@
 
     def gather_copy(ci, i, local):
         m, first, wid = PARTS[ci][i]
-        src = s.mb.at[:, pl.ds(offs[m] + first, wid)]
-        dst = s.xb.at[c, :, pl.ds(pl.multiple_of(w * halves[m] + first, 128), wid)]
+        if ci < 8:
+            src = s.mb.at[ci]
+            dst = s.xb.at[c, w * (halves[m] // 512) + first // 512]
+        else:
+            src = s.mbk.at[i]
+            dst = s.xb.at[c, w, pl.ds(0, rp), pl.ds(0, wid)]
         if local:
             return pltpu.make_async_copy(src, dst, s.grecv)
         return pltpu.make_async_remote_copy(
@@ -279,22 +297,23 @@
 
     def line_finish(ci):
         off, wid = chunks[ci]
+        half = wid // 2
         for k in range(1, n_out):
             line_copy(ci, k).wait_recv()
-
-        def line_sum(t, carry):
-            cs = aligned(off + t * TILE, TILE)
-            here = aligned(t * TILE, TILE)
-            total = s.sum_ref[:, cs]
-            for k in range(n_out - 1):
-                total = total + line_slot(1, ci, k)[:, here][:rows].astype(F32)
-            s.sum_ref[:, cs] = total
-            fresh = MOMENTUM * s.nm_ref[:, cs] + total
-            s.nm_ref[:, cs] = fresh
-            s.mb[:, cs] = pad_rows(fresh, rp).astype(BF)
-            return carry
-
-        lax.fori_loop(0, wid // TILE, line_sum, 0)
+        sides = [s.sum_ref[:, off : off + half], s.sum_ref[:, off + half : off + wid]]
+        for k in range(n_out - 1):
+            for i, extra in enumerate(unpack(line_slot(1, ci, k)[...], rows)):
+                sides[i] = sides[i] + extra
+        for i in range(2):
+            lanes = slice(off + i * half, off + (i + 1) * half)
+            s.sum_ref[:, lanes] = sides[i]
+            sides[i] = MOMENTUM * s.nm_ref[:, lanes] + sides[i]
+            s.nm_ref[:, lanes] = sides[i]
+        if ci < 8:
+            s.mb[ci] = pack(sides[0], sides[1], hp)
+        else:
+            for i in range(2):
+                s.mbk[i] = pad_rows(sides[i], rp).astype(BF)
         for i, piece in enumerate(PARTS[ci]):
             mine = me == OWNERS[piece[0]] * wa_count
 
@@ -328,29 +347,71 @@
     for cp in moms:
         cp.start()
 
+    def gain_core_copy():
+        return pltpu.make_async_remote_copy(
+            s.dgs, s.dgc, s.gcsend, s.gcrecv, device_id=(c, 1 - w), device_id_type=MESH
+        )
+
+    def gain_plane(k):
+        src, dst = ((near[0], near[0]), (across, near[0]), (near[1], near[1]))[k]
+        return pltpu.make_async_remote_copy(
+            s.dgc.at[src],
+            s.dgp.at[k],
+            s.gpsend.at[k],
+            s.gprecv.at[k],
+            device_id=(z * n_in + dst, w),
+            device_id_type=MESH,
+        )
+
+    def gain_line(k):
+        j = lax.rem(z + k, n_out)
+        return pltpu.make_async_remote_copy(
+            s.dgo.at[j],
+            s.dgl.at[k - 1],
+            s.glsend.at[k - 1],
+            s.glrecv.at[k - 1],
+            device_id=(j * n_in + p, w),
+            device_id_type=MESH,
+        )
+
+    def gains_core():
+        for i in range(ctx_count):
+            s.dgs[i % n_in, i // n_in, :, 0:rows] = s.dg_ref[:, i * rows : (i + 1) * rows]
+        gain_core_copy().start()
+
+    def gains_first():
+        gain_core_copy().wait_recv()
+        s.dgc[...] = s.dgc[...] + s.dgs[...]
+        gain_plane(1).start()
+        gain_plane(0).start()
+
+    def gains_mid():
+        gain_plane(1).wait_recv()
+        s.dgc[near[1]] = s.dgc[near[1]] + s.dgp[1]
+        gain_plane(2).start()
+
+    def gains_line():
+        gain_plane(0).wait_recv()
+        gain_plane(2).wait_recv()
+        s.dgo[...] = s.dgc[p] + s.dgp[0] + s.dgp[2]
+        for k in range(1, n_out):
+            gain_line(k).start()
+
+    def gains_end():
+        total = s.dgo[z]
+        for k in range(1, n_out):
+            gain_line(k).wait_recv()
+            total = total + s.dgl[k - 1]
+        s.gs_ref[...] = total
+        gain_core_copy().wait_send()
+        for k in range(3):
+            gain_plane(k).wait_send()
+        for k in range(1, n_out):
+            gain_line(k).wait_send()
+
+    s.gains_core = gains_core
+
     def rest():
-        for i in range(ctx_count):
-            s.dgs[i, :, 0:rows] = s.dg_ref[:, i * rows : (i + 1) * rows]
-
-        def gain_copy(t):
-            i, v = lax.div(t, wa_count), lax.rem(t, wa_count)
-            return pltpu.make_async_remote_copy(
-                s.dgs.at[i],
-                s.dgr.at[me],
-                s.gnsend.at[t],
-                s.gnrecv,
-                device_id=(i, v),
-                device_id_type=MESH,
-            )
-
-        def gain_send(t, carry):
-            gain_copy(lax.rem(me + t, n_dev)).start()
-            return carry
-
-        def gain_sent(t, carry):
-            gain_copy(lax.rem(me + t, n_dev)).wait_send()
-            return carry
-
         for cp in moms:
             cp.wait()
         plane_mid(7)
@@ -362,21 +423,21 @@
         line_finish(3)
         plane_finish(7)
         plane_finish(8)
+        gains_first()
         line_finish(4)
         line_finish(5)
-        pltpu.make_async_copy(s.dgs.at[c], s.dgr.at[me], s.gnrecv).start()
-        lax.fori_loop(1, n_dev, gain_send, 0)
-        for ci in range(6, 9):
-            line_finish(ci)
+        gains_mid()
+        line_finish(6)
+        line_finish(7)
+        gains_line()
+        line_finish(8)
         for ci in range(len(chunks)):
             for k in range(3):
                 plane_copy(ci, k).wait_send()
             for k in range(1, n_out):
                 line_copy(ci, k).wait_send()
         solve()
-        pltpu.make_async_copy(s.dgr, s.dgr, s.gnrecv).wait()
-        s.gs_ref[...] = jnp.sum(s.dgr[...], axis=0)
-        lax.fori_loop(1, n_dev, gain_sent, 0)
+        gains_end()
         updates_back()
 
     def owned_by(*which):
@@ -389,8 +450,9 @@
         is_owner = owned_by(*range(MATRIX_COUNT))
         is_small = owned_by(5, 6)
         is_wide = owned_by(0, 1, 2)
-        tiles = jnp.where(is_small, HD // TILE, jnp.where(is_wide, FF // TILE, HQ // TILE))
-        am, xf = s.am, s.dka.at[pl.ds(0, D)]
+        pairs = jnp.where(is_small, 0, jnp.where(is_wide, FF // 512, HQ // 512))
+        am = s.am
+        xfs = (s.dka.at[pl.ds(0, D)], s.dva.at[pl.ds(0, D)])
         ah = s.wd.at[pl.ds(0, D)]
         al = s.wd.at[pl.ds(D, D)]
         ph = s.wd.at[pl.ds(2 * D, D)]
@@ -404,32 +466,40 @@
 
             @pl.when(me == OWNERS[m] * wa_count)
             def _(m=m):
-                whole = s.xb.at[:, :, pl.ds(0, halves[m] * wa_count)]
+                if m < 5:
+                    whole = s.xb.at[:, pl.ds(0, halves[m] * wa_count // 512)]
+                else:
+                    whole = s.xb.at[:, pl.ds(0, 2), pl.ds(0, rp), pl.ds(0, halves[m])]
                 pltpu.make_async_copy(whole, whole, s.grecv).wait()
 
         @pl.when(is_owner)
         def _():
             am[...] = jnp.zeros_like(am)
 
-            def gram(t, carry):
-                cs = aligned(t * TILE, TILE)
+            def gram(q, carry):
                 for i in range(ctx_count):
-                    xf[i * rows : (i + 1) * rows, :] = s.xb[i, :, cs][:rows].astype(F32)
-                x = xf[...].astype(BF)
-                tile_of(t)[...] = x
-
-                @pl.when(jnp.logical_not(is_small))
-                def _():
+                    for xf, part in zip(xfs, unpack(s.xb[i, q], rows)):
+                        xf[i * rows : (i + 1) * rows, :] = part
+                for side in range(2):
+                    x = xfs[side][...].astype(BF)
+                    tile_of(2 * q + side)[...] = x
                     for a, b in SYM_TILES:
                         am[a:, a:b] += dot_nt(x[a:], x[a:b])
-
-                @pl.when(is_small)
-                def _():
-                    am[0:HD, 0:HD] = dot_tn(x, x)
-
                 return carry
 
-            lax.fori_loop(0, tiles, gram, 0)
+            lax.fori_loop(0, pairs, gram, 0)
+
+            @pl.when(is_small)
+            def _():
+                for i in range(ctx_count):
+                    for v in range(2):
+                        part = s.xb[i, v, 0:rp, 0 : HD // 2][...].astype(F32)[:rows]
+                        lanes = slice(v * (HD // 2), (v + 1) * (HD // 2))
+                        xfs[0][i * rows : (i + 1) * rows, lanes] = part
+                x = xfs[0][...].astype(BF)
+                tile_of(jnp.int32(0))[...] = x
+                am[0:HD, 0:HD] = dot_tn(x, x)
+
             norm2 = jnp.sum(jnp.where(eye_mask(D), am[...], 0.0), keepdims=True)
             inv = 1.0 / (jnp.sqrt(norm2) + 1e-07)
             inv2 = inv * inv
@@ -475,34 +545,27 @@
             rate = jnp.where(is_small, rates[0], jnp.where(is_wide, rates[1], rates[2]))
             scale = rate * inv
 
-            def put(v, lanes, value):
+            def place(i, height, lanes):
+                return i // per, slice(i % per * hp, i % per * hp + height), lanes
+
+            def back(q, carry):
+                for side in range(2):
+                    xfs[side][...] = dot32(qh[...], tile_of(2 * q + side)[...]) * scale
                 for i in range(ctx_count):
-                    s.ffb[v * 2 + i // per, i % per * rp : (i % per + 1) * rp, lanes] = pad_rows(
-                        value[i * rows : (i + 1) * rows], rp
-                    ).astype(BF)
-
-            def back(v, t):
-                @pl.when(jnp.logical_not(is_small))
-                def _():
-                    whole = v * jnp.where(is_wide, 4, 2) + t
-                    xf[...] = dot32(qh[...], tile_of(whole)[...]) * scale
-                    put(v, aligned(t * TILE, TILE), xf)
-
-                @pl.when(is_small)
-                def _():
-                    xf[...] = dot32(tile_of(t)[...], s.wu[0, 0:HD, 0:HD]) * scale
-                    for half in range(2):
-                        lanes = slice(half * (HD // 2), (half + 1) * (HD // 2))
-                        put(half, pl.ds(0, HD // 2), xf[:, lanes])
+                    rs = slice(i * rows, (i + 1) * rows)
+                    s.ffb[place(i, hp, aligned(q * 256, 256))] = pack(xfs[0][rs], xfs[1][rs], hp)
+                return carry
+
+            @pl.when(is_small)
+            def _():
+                xfs[0][...] = dot32(tile_of(jnp.int32(0))[...], s.wu[0, 0:HD, 0:HD]) * scale
+                for i in range(ctx_count):
+                    rs = slice(i * rows, (i + 1) * rows)
+                    both = pad_rows(xfs[0][rs], rp).astype(BF)
+                    s.ffb[place(i, rp, slice(0, HD))] = both
 
             for v in range(2):
-                count = jnp.where(is_small, 1 - v, jnp.where(is_wide, 4, 2))
-
-                def run(t, carry, v=v):
-                    back(v, t)
-                    return carry
-
-                lax.fori_loop(0, count, run, 0)
+                lax.fori_loop(v * lax.div(pairs, 2), (v + 1) * lax.div(pairs, 2), back, 0)
                 for m in range(MATRIX_COUNT):
 
                     @pl.when(me == OWNERS[m] * wa_count)
@@ -518,11 +581,21 @@
                         else:
                             lax.fori_loop(0, ctx_count, send, 0)
 
+    def update_place(m):
+        if m < 5:
+            return s.ub.at[:, pl.ds(offs[m] // 2, halves[m] // 2)]
+        return s.ubk.at[m - 5]
+
     def update_copy(m, t, local):
         i, v = lax.div(t, wa_count), lax.rem(t, wa_count)
-        start = pl.multiple_of(lax.rem(i, per) * rp, 16)
-        src = s.ffb.at[v * 2 + lax.div(i, per), pl.ds(start, rp), pl.ds(0, halves[m])]
-        dst = s.ub.at[:, pl.ds(offs[m], halves[m])]
+        start = pl.multiple_of(lax.rem(i, per) * hp, 16)
+        if m < 5:
+            height, wid = hp, halves[m] // 2
+        else:
+            height, wid = rp, halves[m]
+        lanes = pl.ds(pl.multiple_of(v * wid, 128), wid)
+        src = s.ffb.at[lax.div(i, per), pl.ds(start, height), lanes]
+        dst = update_place(m)
         if local:
             return pltpu.make_async_copy(src, dst, s.urecv.at[m])
         return pltpu.make_async_remote_copy(
@@ -531,7 +604,7 @@
 
     def updates_back():
         for m in range(MATRIX_COUNT):
-            piece = s.ub.at[:, pl.ds(offs[m], halves[m])]
+            piece = update_place(m)
             pltpu.make_async_copy(piece, piece, s.urecv.at[m]).wait()
 
         for m in range(MATRIX_COUNT):
@@ -1006,9 +1079,9 @@
     d_send(0)
     s.plane_mid(2)
     s.plane_mid(3)
-    s.plane_start(6)
     lax.fori_loop(heads, tiles * heads, attend_back, 0)
     d_send(1)
+    s.plane_start(6)
 
     def query_back(v, put):
         def run(u, carry):
@@ -1056,6 +1129,7 @@
         s.h1[rs] = s.h1[rs] + dv
 
     per_rows(fifth)
+    s.gains_core()
     x_far = remote(s.h1, s.x_ref.at[out_rows], s.osend.at[1], s.orecv.at[1], partner)
     x_own = pltpu.make_async_copy(s.h1, s.x_ref.at[out_rows], s.oown.at[1])
     x_far.start()
@@ -1106,7 +1180,7 @@
     "wgu_ref",
     "wd_ref",
 )
-LAYER_OUTPUTS = ("y_ref", "x_ref", "sum_ref", "nm_ref", "ub", "gs_ref")
+LAYER_OUTPUTS = ("y_ref", "x_ref", "sum_ref", "nm_ref", "ub", "ubk", "gs_ref")
 VMEM_BYTES = 63 << 20
 
 
@@ -1157,7 +1231,7 @@
     names = LAYER_INPUTS + LAYER_OUTPUTS + tuple(scratch)
     any_space = pl.BlockSpec(memory_space=pl.ANY)
     vmem = pl.BlockSpec(memory_space=pltpu.VMEM)
-    cols = layout(wa_count)[2]
+    _, offs, cols = layout(wa_count)
     shard = jax.ShapeDtypeStruct((D // ctx_count, cols), F32)
     return pl.pallas_call(
         partial(whole_kernel, ctx_count, wa_count, names),
@@ -1166,11 +1240,12 @@
             jax.ShapeDtypeStruct((block, D), F32),
             shard,
             shard,
-            jax.ShapeDtypeStruct((-(-(D // ctx_count) // 16) * 16, cols), BF),
+            jax.ShapeDtypeStruct((packed_rows(D // ctx_count), offs[5] // 2), BF),
+            jax.ShapeDtypeStruct((2, -(-(D // ctx_count) // 16) * 16, HD // 2), BF),
             jax.ShapeDtypeStruct((8, 128), F32),
         ),
         in_specs=[any_space] * 9 + [vmem] * 5 + [any_space] * 4,
-        out_specs=(any_space, any_space, vmem, vmem, vmem, vmem),
+        out_specs=(any_space, any_space) + (vmem,) * 5,
         scratch_shapes=list(scratch.values()),
         compiler_params=pltpu.CompilerParams(
             collective_id=0, has_side_effects=True, vmem_limit_bytes=VMEM_BYTES
@@ -1204,6 +1279,7 @@
     sum_ref,
     nm_ref,
     ub_ref,
+    ubk_ref,
     gs_ref,
     first_ref,
     second_ref,
@@ -1211,7 +1287,7 @@
     x_ref,
     *rest,
 ):
-    outs, (sumv, nmv, ubv, gsv, fv, sv, yv, xv, sem) = rest[:21], rest[21:]
+    outs, (sumv, nmv, ubv, ubkv, gsv, fv, sv, yv, xv, sem) = rest[:21], rest[21:]
     rows = D // ctx_count
     halves, offs, _ = layout(wa_count)
 
@@ -1229,6 +1305,7 @@
             (sum_ref, sumv),
             (nm_ref, nmv),
             (ub_ref, ubv),
+            (ubk_ref, ubkv),
             (gs_ref, gsv),
             (first_ref, fv),
             (second_ref, sv),
@@ -1237,8 +1314,8 @@
     )
     for cp in fetched:
         cp.start()
-    stored = copies(((xv, outs[1]), (yv, outs[0])), 8)
-    for src, group, first in ((sumv, outs[2:7], 10), (nmv, outs[8:13], 17)):
+    stored = copies(((xv, outs[1]), (yv, outs[0])), 9)
+    for src, group, first in ((sumv, outs[2:7], 11), (nmv, outs[8:13], 18)):
         stored += copies(
             [
                 (src.at[:, pl.ds(offs[m], halves[m])], dst)
@@ -1254,7 +1331,13 @@
     for cp in fetched[4:]:
         cp.wait()
     for m, dst in enumerate(places(outs[13:18])):
-        dst[...] = ubv[0:rows, offs[m] : offs[m] + halves[m]].astype(F32)
+        if m < 5:
+            for q in range(halves[m] // 512):
+                at = offs[m] // 2 + q * 256
+                for side, part in enumerate(unpack(ubv[:, at : at + 256], rows)):
+                    dst[:, q * 512 + side * 256 : q * 512 + (side + 1) * 256] = part
+        else:
+            dst[...] = ubkv[m - 5].astype(F32)[:rows]
     g = gsv[0:4, 0:rows]
     first = ADAM_ONE * fv[...] + (1.0 - ADAM_ONE) * g
     second = ADAM_TWO * sv[...] + (1.0 - ADAM_TWO) * g * g
@@ -1266,7 +1349,7 @@
         cp.wait()
 
 
-def run_format(sums, fresh, updates, gsum, gain_first, gain_second, y, x, ctx_count, wa_count):
+def run_format(sums, fresh, updates, small, gsum, gain_first, gain_second, y, x, ctx_count, wa_count):
     rows = D // ctx_count
     halves = layout(wa_count)[0]
     down, gate, _, out, query, key, _ = halves
@@ -1280,18 +1363,18 @@
     outs = pl.pallas_call(
         partial(format_kernel, ctx_count, wa_count),
         out_shape=shapes,
-        in_specs=[any_space] * 8,
+        in_specs=[any_space] * 9,
         out_specs=[any_space] * 7 + [vmem] + [any_space] * 5 + [vmem] * 8,
         scratch_shapes=[
             *[
                 pltpu.VMEM(a.shape, a.dtype)
-                for a in (sums, fresh, updates, gsum, gain_first, gain_second, y, x)
+                for a in (sums, fresh, updates, small, gsum, gain_first, gain_second, y, x)
             ],
-            pltpu.SemaphoreType.DMA((24,)),
+            pltpu.SemaphoreType.DMA((25,)),
         ],
         compiler_params=pltpu.CompilerParams(vmem_limit_bytes=VMEM_BYTES),
         name="format",
-    )(sums, fresh, updates, gsum, gain_first, gain_second, y, x)
+    )(sums, fresh, updates, small, gsum, gain_first, gain_second, y, x)
     return tuple(o.T if i in (4, 6, 10, 12, 15, 17) else o for i, o in enumerate(outs))
 
 
@@ -1315,7 +1398,7 @@
 ):
     ctx_count = lax.axis_size("ctx")
     wa_count = lax.axis_size("wa")
-    y, x, sums, fresh, updates, gsum = run_whole(
+    y, x, sums, fresh, updates, small, gsum = run_whole(
         tokens,
         cotangent,
         seq_ids,
@@ -1331,7 +1414,7 @@
     )
     return tuple(
         run_format(
-            sums, fresh, updates, gsum, gain_first, gain_second, y, x, ctx_count, wa_count
+            sums, fresh, updates, small, gsum, gain_first, gain_second, y, x, ctx_count, wa_count
         )
     )
 

time: 185 us -> 172 us (0.930)
  Pallas kernels: 183 us -> 170 us
    pallas_call x1, Pallas kernels: 178 us -> 164 us  [run_whole(): pl.pallas_call(partial(whole_kernel, ctx_count, wa_count, names), out_sha...]
where the time goes in v6:
time: 172 us
  Pallas kernels  170 us (99%)
    pallas_call x1, Pallas kernels, run_whole(): pl.pallas_call(partial(whole_kernel, ctx_count, wa_count, names), out_sha...  164 us
    pallas_call x1, Pallas kernels, run_format(): pl.pallas_call(partial(format_kernel, ctx_count, wa_count), out_shape=sha...  5.19 us

profile of v6, /device:TPU:15, one launch (start us, length us, event | category | flops | bytes accessed | tf_op | source)
XLA Modules:
  0.0 171.8 jit_solution(8250215104506577034)
XLA Ops:
  0.7 1.3 reshape.45.refs_9_
  1.9 164.4 %whole.1 = (bf16[1024,640]{1,0:T(8,128)(2,1)}, f32[1024,640]{1,0:T(8,128)}, f32[40,4352]{1,0:T(8,128)}, f32[40,4352]{1,0:T(8,128)}, bf16[80,2048]{1,0:T(8,128)(2...) custom-call(bf16[1024,640]{1,0:T(8,128)(2,1)} %refs_0_.1, bf16[1024,640]{1,0:T(8,128)(2,1)} %refs_1_.1, ...), custom_call_target="tpu_custom_call" | custom-call | tf_op jit(solution)/shard_map/whole/pallas_call | solution.py:1236
  166.4 5.2 %format.1 = (bf16[1024,640]{1,0:T(8,128)(2,1)}, f32[1024,640]{1,0:T(8,128)}, f32[40,512]{1,0:T(8,128)}, f32[2,40,128]{2,1,0:T(8,128)}, f32[40,512]{1,0:T(8,128)}...) custom-call(f32[40,4352]{1,0:T(8,128)} %get-tuple-element.49.sum_ref, ...), custom_call_target="tpu_custom_call" | custom-call | tf_op jit(solution)/shard_map/format/pallas_call | solution.py:1363

commit v7 on v6

--- a/solution.py
+++ b/solution.py
@@ -773,9 +773,13 @@
     )
     w_far = [remote(a, b, s.wsend.at[i], s.wrecv.at[i], partner) for i, (a, b) in enumerate(wk_refs)]
     w_own = [pltpu.make_async_copy(a, b, s.wown.at[i]) for i, (a, b) in enumerate(wk_refs)]
-    for far, own in zip(w_far, w_own):
-        far.start()
-        own.start()
+
+    def weights_start(first, last):
+        for i in range(first, last):
+            w_far[i].start()
+            w_own[i].start()
+
+    weights_start(0, 1)
 
     def weights_ready(i):
         w_own[i].wait()
@@ -807,7 +811,7 @@
         return jnp.concatenate([a * cosine + b * sine, b * cosine - a * sine], axis=1)
 
     s.ka[WINDOW:, :] = turn(dot32(s.xa[...], s.wkv_ref[0]), s.cs[...], s.sn[...]).astype(BF)
-    s.idown[...] = jnp.broadcast_to(s.ids_ref[pl.ds(w, 1), :], (8, tok))
+    s.idown[...] = jnp.broadcast_to(s.ids_ref[:, aligned(w * tok, tok)], (8, tok))
     halo = [
         remote(src, dst, s.ksend.at[i], s.krecv.at[i], next_id)
         for i, (src, dst) in enumerate(
@@ -829,6 +833,8 @@
     @pl.when(flat < n_dev - 1)
     def _():
         halo[1].start()
+
+    weights_start(1, 5)
 
     def flip(rs):
         s.xat[:, rs] = permuted(s.xa[rs])
@@ -985,7 +991,13 @@
             s.ffb[2 + v, :, us] = dgt
             s.ffb[4 + v, :, us] = dup
             put(1, u, TILE, dot32(s.fit[...], dgt))
-            put(2, u, TILE, dot32(s.fit[...], dup))
+            return carry
+
+        lax.fori_loop(0, 4, run, 0)
+
+    def up_back(v, put):
+        def run(u, carry):
+            put(2, u, TILE, dot32(s.fit[...], s.ffb[4 + v, :, aligned(u * TILE, TILE)]))
             return carry
 
         lax.fori_loop(0, 4, run, 0)
@@ -997,11 +1009,13 @@
     gate_back(other, give)
     gate_back(w, keep)
     s.down_free()
-    s.dn[...] = dot_nt(s.ffb[2], s.wg[0]) + dot_nt(s.ffb[3], s.wg[1])
+    up_back(other, give)
+    s.plane_start(2)
+    s.plane_start(3)
+    up_back(w, keep)
     s.plane_mid(0)
     s.plane_mid(1)
-    s.plane_start(2)
-    s.plane_start(3)
+    s.dn[...] = dot_nt(s.ffb[2], s.wg[0]) + dot_nt(s.ffb[3], s.wg[1])
     s.dn[...] += dot_nt(s.ffb[4], s.wu[0]) + dot_nt(s.ffb[5], s.wu[1])
 
     s.buffers_free()
@@ -1261,7 +1275,7 @@
         mom_gateup,
         mom_out.T,
         mom_down.T,
-        seq_ids.reshape(wa_count, tok),
+        seq_ids[None],
         gains,
         wkv,
         cosb,

time: 172 us -> 166 us (0.965)
  Pallas kernels: 170 us -> 165 us
    pallas_call x1, Pallas kernels: 164 us -> 160 us  [run_whole(): pl.pallas_call(partial(whole_kernel, ctx_count, wa_count, names), out_sha...]
where the time goes in v7:
time: 166 us
  Pallas kernels  165 us (99%)
    pallas_call x1, Pallas kernels, run_whole(): pl.pallas_call(partial(whole_kernel, ctx_count, wa_count, names), out_sha...  160 us
    pallas_call x1, Pallas kernels, run_format(): pl.pallas_call(partial(format_kernel, ctx_count, wa_count), out_shape=sha...  5.19 us

profile of v7, /device:TPU:15, one launch (start us, length us, event | category | flops | bytes accessed | tf_op | source)
XLA Modules:
  0.0 166.2 jit_solution(4640381719507764207)
XLA Ops:
  0.7 160.2 %whole.1 = (bf16[1024,640]{1,0:T(8,128)(2,1)}, f32[1024,640]{1,0:T(8,128)}, f32[40,4352]{1,0:T(8,128)}, f32[40,4352]{1,0:T(8,128)}, bf16[80,2048]{1,0:T(8,128)(2...) custom-call(bf16[1024,640]{1,0:T(8,128)(2,1)} %refs_0_.1, bf16[1024,640]{1,0:T(8,128)(2,1)} %refs_1_.1, ...), custom_call_target="tpu_custom_call" | custom-call | tf_op jit(solution)/shard_map/whole/pallas_call | solution.py:1250
  160.8 5.2 %format.1 = (bf16[1024,640]{1,0:T(8,128)(2,1)}, f32[1024,640]{1,0:T(8,128)}, f32[40,512]{1,0:T(8,128)}, f32[2,40,128]{2,1,0:T(8,128)}, f32[40,512]{1,0:T(8,128)}...) custom-call(f32[40,4352]{1,0:T(8,128)} %get-tuple-element.49.sum_ref, ...), custom_call_target="tpu_custom_call" | custom-call | tf_op jit(solution)/shard_map/format/pallas_call | solution.py:1377

commit v8 on v7

--- a/solution.py
+++ b/solution.py
@@ -37,7 +37,7 @@
 IN_COUNT = 4
 NAMES = ("down", "gate", "up", "out", "query", "key", "value")
 WIDTHS = (FF, FF, FF, HQ, HQ, HD, HD)
-OWNERS = (7, 4, 8, 5, 11, 9, 10)
+OWNERS = (7, 4, 9, 6, 10, 8, 11)
 PARTS = (
     ((0, 0, 512),),
     ((0, 512, 512),),
@@ -416,9 +416,9 @@
             cp.wait()
         plane_mid(7)
         plane_mid(8)
+        plane_finish(6)
         line_finish(0)
         line_finish(1)
-        plane_finish(6)
         line_finish(2)
         line_finish(3)
         plane_finish(7)
@@ -854,13 +854,10 @@
 
     @pl.when(flat > 0)
     def _():
-        for cp in halo:
-            cp.wait_recv()
+        halo[2].wait_recv()
 
     @pl.when(flat == 0)
     def _():
-        s.ka[0:WINDOW, :] = jnp.zeros((WINDOW, HD), BF)
-        s.va[0:WINDOW, :] = jnp.zeros((WINDOW, HD), BF)
         s.idprev[...] = jnp.full((8, tok), -1, jnp.int32)
 
     row_ids = jnp.concatenate([s.idprev[0:1, :], s.idown[0:1, :]], axis=1)
@@ -872,6 +869,16 @@
         same = own_col[a * TILE : (a + 1) * TILE] == row_ids[:, a * TILE : a * TILE + win]
         ok = jnp.logical_and(same, jnp.logical_and(gap > 0, gap <= WINDOW))
         s.ffb[a, 0:TILE, 0:win] = jnp.where(ok, 1.0, 0.0).astype(BF)
+
+    @pl.when(flat > 0)
+    def _():
+        halo[0].wait_recv()
+        halo[1].wait_recv()
+
+    @pl.when(flat == 0)
+    def _():
+        s.ka[0:WINDOW, :] = jnp.zeros((WINDOW, HD), BF)
+        s.va[0:WINDOW, :] = jnp.zeros((WINDOW, HD), BF)
 
     def attend(i, carry):
         a, h = lax.div(i, heads), lax.rem(i, heads)

time: 166 us -> 165 us (level)
  no operation moved by 1% of the time
where the time goes in v8:
time: 165 us
  Pallas kernels  164 us (99%)
    pallas_call x1, Pallas kernels, run_whole(): pl.pallas_call(partial(whole_kernel, ctx_count, wa_count, names), out_sha...  159 us
    pallas_call x1, Pallas kernels, run_format(): pl.pallas_call(partial(format_kernel, ctx_count, wa_count), out_shape=sha...  5.19 us

profile of v8, /device:TPU:15, one launch (start us, length us, event | category | flops | bytes accessed | tf_op | source)
XLA Modules:
  0.0 164.9 jit_solution(1784408498619206625)
XLA Ops:
  0.7 158.9 %whole.1 = (bf16[1024,640]{1,0:T(8,128)(2,1)}, f32[1024,640]{1,0:T(8,128)}, f32[40,4352]{1,0:T(8,128)}, f32[40,4352]{1,0:T(8,128)}, bf16[80,2048]{1,0:T(8,128)(2...) custom-call(bf16[1024,640]{1,0:T(8,128)(2,1)} %refs_0_.1, bf16[1024,640]{1,0:T(8,128)(2,1)} %refs_1_.1, ...), custom_call_target="tpu_custom_call" | custom-call | tf_op jit(solution)/shard_map/whole/pallas_call | solution.py:1257
  159.6 5.2 %format.1 = (bf16[1024,640]{1,0:T(8,128)(2,1)}, f32[1024,640]{1,0:T(8,128)}, f32[40,512]{1,0:T(8,128)}, f32[2,40,128]{2,1,0:T(8,128)}, f32[40,512]{1,0:T(8,128)}...) custom-call(f32[40,4352]{1,0:T(8,128)} %get-tuple-element.49.sum_ref, ...), custom_call_target="tpu_custom_call" | custom-call | tf_op jit(solution)/shard_map/format/pallas_call | solution.py:1384

commit v9 on v8

--- a/solution.py
+++ b/solution.py
@@ -1019,9 +1019,9 @@
     up_back(other, give)
     s.plane_start(2)
     s.plane_start(3)
-    up_back(w, keep)
     s.plane_mid(0)
     s.plane_mid(1)
+    up_back(w, keep)
     s.dn[...] = dot_nt(s.ffb[2], s.wg[0]) + dot_nt(s.ffb[3], s.wg[1])
     s.dn[...] += dot_nt(s.ffb[4], s.wu[0]) + dot_nt(s.ffb[5], s.wu[1])
 

time: 165 us -> 165 us (level)
  no operation moved by 1% of the time
where the time goes in v9:
time: 165 us
  Pallas kernels  164 us (99%)
    pallas_call x1, Pallas kernels, run_whole(): pl.pallas_call(partial(whole_kernel, ctx_count, wa_count, names), out_sha...  159 us
    pallas_call x1, Pallas kernels, run_format(): pl.pallas_call(partial(format_kernel, ctx_count, wa_count), out_shape=sha...  5.19 us

profile of v9, /device:TPU:15, one launch (start us, length us, event | category | flops | bytes accessed | tf_op | source)
XLA Modules:
  0.0 164.9 jit_solution(18060977913288329885)
XLA Ops:
  0.7 158.9 %whole.1 = (bf16[1024,640]{1,0:T(8,128)(2,1)}, f32[1024,640]{1,0:T(8,128)}, f32[40,4352]{1,0:T(8,128)}, f32[40,4352]{1,0:T(8,128)}, bf16[80,2048]{1,0:T(8,128)(2...) custom-call(bf16[1024,640]{1,0:T(8,128)(2,1)} %refs_0_.1, bf16[1024,640]{1,0:T(8,128)(2,1)} %refs_1_.1, ...), custom_call_target="tpu_custom_call" | custom-call | tf_op jit(solution)/shard_map/whole/pallas_call | solution.py:1257
  159.6 5.2 %format.1 = (bf16[1024,640]{1,0:T(8,128)(2,1)}, f32[1024,640]{1,0:T(8,128)}, f32[40,512]{1,0:T(8,128)}, f32[2,40,128]{2,1,0:T(8,128)}, f32[40,512]{1,0:T(8,128)}...) custom-call(f32[40,4352]{1,0:T(8,128)} %get-tuple-element.49.sum_ref, ...), custom_call_target="tpu_custom_call" | custom-call | tf_op jit(solution)/shard_map/format/pallas_call | solution.py:1384
